TPU v7x, 32 devices: a whole 2x2x4 slice. The times are simulated.
32 devices in a mesh: dp: 8 (over z, y), seq: 4 (over x, core).
Axes of the slice: x: 2, y: 2, z: 4, core: 2. Of those that a mesh axis runs over, the one named last changes fastest.
Arguments:
- tokens: bfloat16 [8, 1024, 2048], P('dp', 'seq'), may hold values from -6 to 6
- cotangent: bfloat16 [8, 1024, 2048], P('dp', 'seq'), may hold values from -6 to 6
- lengths: int32 [8], P('dp'), may hold values from 256 to 1024, as said below
- norm_gain: float32 [2048], replicated, may hold values from 0.5 to 1.5
- w_in: float32 [2048, 8512], P(('dp', 'seq')), may hold values from -0.125 to 0.125
- conv_w: float32 [4352, 4], replicated, may hold values from -3 to 3
- conv_b: float32 [4352], replicated, may hold values from -3 to 3
- dt_bias: float32 [64], replicated, may hold values from -5 to -3
- a_log: float32 [64], replicated
- skip_scale: float32 [64], replicated, may hold values from 0.5 to 1.5
- gate_gain: float32 [4096], replicated, may hold values from 0.5 to 1.5
- w_out: float32 [4096, 2048], P(('dp', 'seq')), may hold values from -0.09375 to 0.09375
Outputs:
- output: bfloat16 [8, 1024, 2048], P('dp', 'seq')
- input_grad: float32 [8, 1024, 2048], P('dp', 'seq')
- grad_norm_gain: float32 [2048], replicated
- grad_w_in: float32 [2048, 8512], P(('dp', 'seq'))
- grad_conv_w: float32 [4352, 4], replicated
- grad_conv_b: float32 [4352], replicated
- grad_dt_bias: float32 [64], replicated
- grad_a_log: float32 [64], replicated
- grad_skip_scale: float32 [64], replicated
- grad_gate_gain: float32 [4096], replicated
- grad_w_out: float32 [4096, 2048], P(('dp', 'seq'))
Inputs may be any that keep to these rules, and one draw needn't show every extreme that they name: Slot s holds 1024 positions; the first lengths[s] are tokens, the rest padding. Some slot is full in every draw.
All inputs are finite; a program needn't handle non-finite values.
Results may differ from a plain program's by a relative error of at most 0.018.
Values may be sent and summed in bfloat16 or wider, within the bound.
A program may use at most 256 MiB of HBM per device.

v0:
```python
import jax
import jax.numpy as jnp
from jax import lax
from jax.sharding import PartitionSpec as P

D = 2048
HEADS = 64
HEADDIM = 64
STATE = 128
KERNEL = 4
STRETCH = 256
INNER = 4096
CHANNELS = 4352


EPSILON = 1e-05
HIGH = lax.Precision.HIGHEST


def passed_along(block, axis, distance):
    devices = range(lax.axis_size(axis))
    route = [(i - distance, i) for i in devices if i - distance in devices]
    return lax.ppermute(block, axis, route)


def stretch_step(carry_state, block_x, block_step, block_decay, block_b, block_c):
    running = jnp.cumsum(block_decay, 0).T
    width = block_x.shape[0]
    causal = jnp.arange(width)[:, None] >= jnp.arange(width)[None, :]
    differ = running[:, :, None] - running[:, None, :]
    decay = jnp.where(causal[None], jnp.exp(jnp.where(causal[None], differ, 0.0)), 0.0)
    products = jnp.dot(block_c, block_b.T, precision=HIGH)
    mixing = products[None] * decay * block_step.T[:, None, :]
    within = jnp.einsum("hts,shp->thp", mixing, block_x, precision=HIGH)
    entering = jnp.exp(running.T)[:, :, None] * jnp.einsum(
        "tn,hpn->thp", block_c, carry_state, precision=HIGH
    )
    to_end = jnp.exp(running[:, -1:] - running) * block_step.T
    new_state = jnp.exp(running[:, -1])[:, None, None] * carry_state + jnp.einsum(
        "hs,shp,sn->hpn", to_end, block_x, block_b, precision=HIGH
    )
    return (new_state, within + entering)


def state_space(heads_x, time_step, log_decay, b_in, c_out):
    span_rows = heads_x.shape[0]
    blocks_count = span_rows // STRETCH
    blocks = (
        heads_x.reshape(blocks_count, STRETCH, HEADS, HEADDIM),
        time_step.reshape(blocks_count, STRETCH, HEADS),
        log_decay.reshape(blocks_count, STRETCH, HEADS),
        b_in.reshape(blocks_count, STRETCH, STATE),
        c_out.reshape(blocks_count, STRETCH, STATE),
    )

    def advance(carry_state, pieces):
        return stretch_step(carry_state, *pieces)

    final, outputs = lax.scan(
        jax.checkpoint(advance), jnp.zeros((HEADS, HEADDIM, STATE), jnp.float32), blocks
    )
    return (outputs.reshape(span_rows, HEADS, HEADDIM), final)


def convolve(padded, conv_w, conv_b):
    span_rows = padded.shape[0] - KERNEL + 1
    summed = conv_b[None, :]
    for offset in range(KERNEL):
        summed = summed + conv_w[:, offset][None, :] * padded[offset : offset + span_rows]
    return jax.nn.silu(summed)


def mixer_in(padded, dt_raw, conv_w, conv_b, dt_bias, a_log):
    active = convolve(padded, conv_w, conv_b)
    span_rows = active.shape[0]
    heads_x = active[:, :INNER].reshape(span_rows, HEADS, HEADDIM)
    b_in = active[:, INNER : INNER + STATE]
    c_out = active[:, INNER + STATE :]
    time_step = jax.nn.softplus(dt_raw + dt_bias)
    log_decay = time_step * -jnp.exp(a_log)
    return (heads_x, time_step, log_decay, b_in, c_out)


def gated(scanned, gate_in, gate_gain):
    product = scanned * jax.nn.silu(gate_in)
    return product * lax.rsqrt(jnp.mean(product * product, -1, keepdims=True) + EPSILON) * gate_gain


def norm_in(inputs, norm_gain):
    return inputs * lax.rsqrt(jnp.mean(inputs * inputs, -1, keepdims=True) + EPSILON) * norm_gain


def finish(heads_x, log_decay, c_out, local_out, skip_scale, state_in):
    running = jnp.cumsum(log_decay, 0)
    inward = jnp.exp(running)[:, :, None] * jnp.einsum(
        "tn,hpn->thp", c_out, state_in, precision=HIGH
    )
    scanned = local_out + inward + skip_scale[None, :, None] * heads_x
    return (scanned.reshape(scanned.shape[0], INNER), running)


def mixer_local(padded, dt_raw, conv_w, conv_b, dt_bias, a_log, skip_scale, state_in):
    heads_x, time_step, log_decay, b_in, c_out = mixer_in(
        padded, dt_raw, conv_w, conv_b, dt_bias, a_log
    )
    local_out, carried = state_space(heads_x, time_step, log_decay, b_in, c_out)
    scanned, running = finish(heads_x, log_decay, c_out, local_out, skip_scale, state_in)
    return (scanned, jnp.exp(running[-1]), carried)


def pass_states(factor, carried):

    def advance(index, incoming):
        return passed_along(
            (factor[:, None, None] * incoming + carried).astype(jnp.bfloat16), "seq", 1
        ).astype(jnp.float32)

    entering = lax.fori_loop(0, lax.axis_size("seq") - 1, advance, jnp.zeros_like(carried))
    return entering


def pass_grads(factor, local_grad):

    def advance(index, incoming):
        return passed_along(
            (factor[:, None, None] * incoming + local_grad).astype(jnp.bfloat16), "seq", -1
        ).astype(jnp.float32)

    leaving = lax.fori_loop(0, lax.axis_size("seq") - 1, advance, jnp.zeros_like(local_grad))
    return leaving


def column_weights(in_low, out_low):
    turned = (
        lax.all_to_all(in_low, "seq", split_axis=1, concat_axis=0, tiled=True),
        lax.all_to_all(out_low, "seq", split_axis=1, concat_axis=0, tiled=True),
    )
    return (
        lax.all_gather(turned[0], "dp", axis=0, tiled=True),
        lax.all_gather(turned[1], "dp", axis=0, tiled=True),
    )


def whole_rows(values):
    return lax.all_gather(values, "seq", axis=0, tiled=True)


def into_positions(values):
    return lax.all_to_all(values, "seq", split_axis=0, concat_axis=1, tiled=True)


def into_columns(values):
    return lax.all_to_all(values, "seq", split_axis=1, concat_axis=0, tiled=True)


def position_sum(term, rows):
    return lax.psum_scatter(
        term(jnp.int32(0), rows * lax.axis_size("seq")).astype(jnp.bfloat16),
        "seq",
        scatter_dimension=0,
        tiled=True,
    ).astype(jnp.float32)


def owner_total(term, rows):
    return lax.psum_scatter(
        term(jnp.int32(0), rows * lax.axis_size("dp")).astype(jnp.bfloat16),
        "dp",
        scatter_dimension=0,
        tiled=True,
    ).astype(jnp.float32)


def body(
    tokens,
    cotangent,
    lengths,
    norm_gain,
    w_in,
    conv_w,
    conv_b,
    dt_bias,
    a_log,
    skip_scale,
    gate_gain,
    w_out,
):
    row_count = tokens.shape[1]
    inputs = tokens.reshape(row_count, D).astype(jnp.float32)
    position = lax.axis_index("seq") * row_count + jnp.arange(row_count, dtype=jnp.int32)
    valid_mask = (position < lengths[0]).astype(jnp.float32)[:, None]
    normed = norm_in(inputs, norm_gain).astype(jnp.bfloat16)
    in_low = w_in.astype(jnp.bfloat16)
    out_low = w_out.astype(jnp.bfloat16)
    contract_cols = (((1,), (1,)), ((), ()))
    contract_rows = (((0,), (0,)), ((), ()))
    in_slice, out_slice = column_weights(in_low, out_low)
    normed_all = whole_rows(normed)
    piece_proj = jnp.dot(normed_all, in_slice, preferred_element_type=jnp.float32).astype(
        jnp.bfloat16
    )
    projected = into_positions(piece_proj)
    gate_in = projected[:, :INNER].astype(jnp.float32)
    conv_in = projected[:, INNER : INNER + CHANNELS]
    dt_raw = projected[:, INNER + CHANNELS :].astype(jnp.float32)
    before = passed_along(conv_in[row_count - KERNEL + 1 :], "seq", 1)
    padded = jnp.concatenate([before, conv_in], 0).astype(jnp.float32)
    heads_x, time_step, log_decay, b_in, c_out = mixer_in(
        padded, dt_raw, conv_w, conv_b, dt_bias, a_log
    )
    local_out, carried = state_space(heads_x, time_step, log_decay, b_in, c_out)
    factor = jnp.exp(jnp.sum(log_decay, 0))
    state_in = pass_states(factor, carried)
    scanned, running = finish(heads_x, log_decay, c_out, local_out, skip_scale, state_in)
    mixed = gated(scanned, gate_in, gate_gain).astype(jnp.bfloat16)
    mixed_all = whole_rows(mixed)
    piece_branch = jnp.dot(mixed_all, out_slice, preferred_element_type=jnp.float32)
    branch = lax.all_to_all(
        piece_branch.astype(jnp.bfloat16), "seq", split_axis=0, concat_axis=1, tiled=True
    ).astype(piece_branch.dtype)
    output = (valid_mask * (inputs + branch)).astype(jnp.bfloat16)
    masked_cot = cotangent.reshape(row_count, D).astype(jnp.float32) * valid_mask
    branch_grad = masked_cot.astype(jnp.bfloat16)
    in_slice, out_slice = column_weights(in_low, out_low)
    grad_columns = into_columns(branch_grad)

    def mixed_term(start, count):
        return lax.dot_general(
            grad_columns, out_slice, contract_cols, preferred_element_type=jnp.float32
        )

    mixed_grad = position_sum(mixed_term, row_count)

    def out_piece_term(start, count):
        return lax.dot_general(
            mixed_all, grad_columns, contract_rows, preferred_element_type=jnp.float32
        )

    w_out_part = owner_total(out_piece_term, INNER // lax.axis_size("dp"))
    _, pull_gate = jax.vjp(gated, scanned, gate_in, gate_gain)
    scanned_grad, gate_in_grad, gate_gain_grad = pull_gate(mixed_grad)
    local_grad = jnp.einsum(
        "th,thp,tn->hpn",
        jnp.exp(running),
        scanned_grad.reshape(row_count, HEADS, HEADDIM),
        c_out,
        precision=HIGH,
    )
    state_grad = pass_grads(factor, local_grad)
    factor_grad = jnp.sum(state_grad * state_in, axis=(1, 2))
    _, pull_mix = jax.vjp(
        mixer_local, padded, dt_raw, conv_w, conv_b, dt_bias, a_log, skip_scale, state_in
    )
    padded_grad, dt_grad, conv_w_grad, conv_b_grad, dt_bias_grad, a_log_grad, skip_grad, _ = (
        pull_mix((scanned_grad, factor_grad, state_grad))
    )
    rim_grad = passed_along(padded_grad[: KERNEL - 1].astype(jnp.bfloat16), "seq", -1).astype(
        jnp.float32
    )
    conv_in_grad = padded_grad[KERNEL - 1 :] + jnp.concatenate(
        [jnp.zeros((row_count - KERNEL + 1, CHANNELS), jnp.float32), rim_grad], 0
    )
    projected_grad = jnp.concatenate([gate_in_grad, conv_in_grad, dt_grad], 1).astype(jnp.bfloat16)
    projected_columns = into_columns(projected_grad)

    def normed_term(start, count):
        return lax.dot_general(
            projected_columns, in_slice, contract_cols, preferred_element_type=jnp.float32
        )

    normed_grad = position_sum(normed_term, row_count)

    def in_piece_term(start, count):
        return lax.dot_general(
            normed_all, projected_columns, contract_rows, preferred_element_type=jnp.float32
        )

    w_in_part = owner_total(in_piece_term, D // lax.axis_size("dp"))
    grad_w_in, grad_w_out = (
        lax.all_to_all(
            w_in_part.astype(jnp.bfloat16), "seq", split_axis=0, concat_axis=1, tiled=True
        ).astype(w_in_part.dtype),
        lax.all_to_all(
            w_out_part.astype(jnp.bfloat16), "seq", split_axis=0, concat_axis=1, tiled=True
        ).astype(w_out_part.dtype),
    )
    _, pull_norm = jax.vjp(norm_in, inputs, norm_gain)
    inputs_grad, norm_gain_grad = pull_norm(normed_grad)
    input_grad = masked_cot + inputs_grad
    sums = lax.psum(
        (
            norm_gain_grad,
            conv_w_grad,
            conv_b_grad,
            dt_bias_grad,
            a_log_grad,
            skip_grad,
            gate_gain_grad,
        ),
        ("dp", "seq"),
    )
    return (
        output.reshape(tokens.shape),
        input_grad.reshape(1, row_count, D),
        sums[0],
        grad_w_in,
        sums[1],
        sums[2],
        sums[3],
        sums[4],
        sums[5],
        sums[6],
        grad_w_out,
    )


def solution(mesh):
    in_specs = (
        P("dp", "seq", None),
        P("dp", "seq", None),
        P("dp"),
        P(),
        P(("dp", "seq"), None),
        P(),
        P(),
        P(),
        P(),
        P(),
        P(),
        P(("dp", "seq"), None),
    )
    out_specs = (
        P("dp", "seq", None),
        P("dp", "seq", None),
        P(),
        P(("dp", "seq"), None),
        P(),
        P(),
        P(),
        P(),
        P(),
        P(),
        P(("dp", "seq"), None),
    )
    return jax.shard_map(body, mesh=mesh, in_specs=in_specs, out_specs=out_specs, check_vma=False)
```

profile of v0, /device:TPU:1, one launch (start us, length us, event | category | flops | bytes accessed | tf_op | source)
XLA Modules:
  0.0 1284.9 jit_solution(9389904667880306491)
XLA Ops:
  8.8 11.9 all_to_all.138
  26.3 18.8 %all_to_all.139 = bf16[64,4,2128]{2,0,1:T(8,128)(2,1)} all-to-all(bf16[64,4,2128]{2,0,1:T(8,128)(2,1)S(1)} %copy.162), channel_id=1, replica_groups=mesh['dp'=8,'seq'=4] {'seq'}, dimensions={1} | all-to-all | bytes 2179072 | tf_op jit(solution)/shard_map/all_to_all | solution.py:135
  48.3 16.8 %all_to_all.140 = bf16[256,4,512]{2,0,1:T(8,128)(2,1)S(1)} all-to-all(bf16[256,4,512]{2,0,1:T(8,128)(2,1)S(1)} %fusion.75), channel_id=1, replica_groups=mesh['dp'=8,'seq'=4] {'seq'}, dimensions={1} | all-to-all | bytes 2097152 | tf_op jit(solution)/shard_map/all_to_all | solution.py:153
  65.1 29.7 %all-gather.11.cloned.1.call-done = bf16[4096,512]{1,0:T(8,128)(2,1)} async-done(((bf16[512,512]{1,0:T(8,128)(2,1)}), bf16[4096,512]{1,0:T(8,128)(2,1)}) %all-gather.11.cloned.1.call-update) | async-done | bytes 4194320 | tf_op jit(solution)/shard_map/all_gather | solution.py:140
  103.7 27.6 %all-gather.5.cloned.1.call-done = bf16[1024,2048]{1,0:T(8,128)(2,1)} async-done(((bf16[256,2048]{1,0:T(8,128)(2,1)}), bf16[1024,2048]{1,0:T(8,128)(2,1)}) %all-gather.5.cloned.1.call-update) | async-done | bytes 4194320 | tf_op jit(solution)/shard_map/all_gather | solution.py:145
  131.3 133.1 %all-gather.7.cloned.1.call-done = bf16[2048,2128]{1,0:T(8,128)(2,1)} async-done(((bf16[256,2128]{1,0:T(8,128)(2,1)}), bf16[2048,2128]{1,0:T(8,128)(2,1)}) %all-gather.7.cloned.1.call-update) | async-done | bytes 8716304 | tf_op jit(solution)/shard_map/all_gather | solution.py:139
  264.4 13.6 %convolution_convert_fusion.3 = bf16[1024,2128]{0,1:T(8,128)(2,1)S(1)} fusion(bf16[1024,2048]{1,0:T(8,128)(2,1)} %all-gather.5.cloned.1.call-done, bf16[2048,2128]{1,0:T(8,128)(2,1)} %all-gather.7.cloned.1.call-done), kind=kOutput, calls=%fused_computation.44 | convolution fusion | flops 8927657984 | bytes 17268736 | tf_op jit(solution)/shard_map/dot_general | solution.py:199
  288.8 91.0 %all-to-all-done.1 = bf16[4,256,2128]{1,2,0:T(8,128)(2,1)} async-done(((bf16[4,256,2128]{1,2,0:T(8,128)(2,1)}), bf16[4,256,2128]{1,2,0:T(8,128)(2,1)}, u32[]{:S(2)}, u32[]{:S(2)}) %all-to-all-start.1) | async-done | bytes 4358176 | tf_op jit(solution)/shard_map/all_to_all | solution.py:149
  440.0 61.4 %while.6 = (s32[]{:T(128)}, f32[64,64,128]{2,1,0:T(8,128)}, f32[64]{0:T(128)S(1)}, f32[64,64,128]{2,1,0:T(8,128)}, s32[]{:T(128)}, /*index=5*/s32[]{:T(128)}) while((s32[]{:T(128)}, f32[64,64,128]{2,1,0:T(8,128)}, f32[64]{0:T(128)S(1)}, f32[64,64,128]{2,1,0:T(8,128)}, s32[]{:T(128)}, /*index=5*/s32[]{:T(128)}) %tuple.92), condition=%wide.region_5.6_spmd.clone, body=%wide.region_4.5_spmd.clone.sunk | while | flops 2621443 | bytes 12583287 | solution.py:118
  444.8 12.0 collective-permute-done
  466.2 12.0 collective-permute-done
  487.6 12.0 collective-permute-done
  506.8 23.1 %fusion.48 = f32[256,64,64]{0,2,1:T(8,128)} fusion(f32[256,64,64]{0,2,1:T(8,128)S(1)} %bitcast.224, f32[256,64,64]{0,2,1:T(8,128)S(1)} %fusion.115, f32[256,64,64]{0,2,1:T(8,128)} %fusion.100, f32[64,256]{1,0:T(8,128)S(1)} %copy.172, f32[64,256]{1,0:T(8,128)S(1)} %copy.170, f32[256,256]{1,0:T(8,128)S(1)} %copy-done.31, pred[256,256]{1,0:T(8,128)(4,1)S(1)} %copy-done.50, ...), kind=kOutput, calls=%fused_computation.77 | convolution fusion | flops 3248488448 | bytes 17301760 | tf_op jit(solution)/shard_map/while/body/eval_jaxpr/checkpoint/hts,shp->thp/dot_general | solution.py:34
  549.0 9.1 multiply_reduce_fusion.7
  578.4 59.0 %while.7 = (s32[]{:T(128)}, f32[64,64,128]{2,1,0:T(8,128)S(1)}, f32[64]{0:T(128)S(1)}, f32[64,64,128]{2,1,0:T(8,128)}, s32[]{:T(128)}, /*index=5*/s32[]{:T(128)}) while((s32[]{:T(128)}, f32[64,64,128]{2,1,0:T(8,128)S(1)}, f32[64]{0:T(128)S(1)}, f32[64,64,128]{2,1,0:T(8,128)}, s32[]{:T(128)}, /*index=5*/s32[]{:T(128)}) %tuple.117), condition=%wide.region_10.11_spmd.clone, body=%wide.region_9.10_spmd.clone.sunk | while | flops 2621443 | bytes 12583287 | solution.py:129
  583.2 15.0 %collective-permute-done.1 = bf16[64,64,128]{2,1,0:T(8,128)(2,1)S(1)} collective-permute-done((bf16[64,64,128]{2,1,0:T(8,128)(2,1)}, bf16[64,64,128]{2,1,0:T(8,128)(2,1)S(1)}, u32[]{:S(2)}, u32[]{:S(2)}) %collective-permute-start.1) | collective-permute-done | bytes 1048608 | tf_op jit(solution)/shard_map/while/body/eval_jaxpr/ppermute | solution.py:23
  603.4 14.4 %collective-permute-done.1 = bf16[64,64,128]{2,1,0:T(8,128)(2,1)S(1)} collective-permute-done((bf16[64,64,128]{2,1,0:T(8,128)(2,1)}, bf16[64,64,128]{2,1,0:T(8,128)(2,1)S(1)}, u32[]{:S(2)}, u32[]{:S(2)}) %collective-permute-start.1) | collective-permute-done | bytes 1048608 | tf_op jit(solution)/shard_map/while/body/eval_jaxpr/ppermute | solution.py:23
  622.8 14.4 %collective-permute-done.1 = bf16[64,64,128]{2,1,0:T(8,128)(2,1)S(1)} collective-permute-done((bf16[64,64,128]{2,1,0:T(8,128)(2,1)}, bf16[64,64,128]{2,1,0:T(8,128)(2,1)S(1)}, u32[]{:S(2)}, u32[]{:S(2)}) %collective-permute-start.1) | collective-permute-done | bytes 1048608 | tf_op jit(solution)/shard_map/while/body/eval_jaxpr/ppermute | solution.py:23
  666.7 27.5 %fusion.17 = (f32[64,256]{1,0:T(8,128)}, f32[64,256]{1,0:T(8,128)}, f32[64,256]{1,0:T(8,128)}, f32[256,256]{1,0:T(8,128)S(1)}) fusion(f32[256,256]{1,0:T(8,128)S(1)} %copy-done.32, f32[64,256]{1,0:T(8,128)S(1)} %copy.187, f32[64,256]{1,0:T(8,128)S(1)} %copy.186, pred[256,256]{1,0:T(8,128)(4,1)S(1)} %copy-done.50, f32[256,64,64]{0,2,1:T(8,128)S(1)} %bitcast.225, ...), kind=kOutput, calls=%fused_computation.23 | convolution fusion | flops 3284025344 | bytes 9306112 | tf_op jit(solution)/shard_map/transpose(jvp())/while/body/eval_jaxpr/checkpoint/hts,shp->thp/dot_general | solution.py:34
  694.1 16.3 %bitcast_add_fusion = f32[256,64,64]{0,2,1:T(8,128)} fusion(f32[256,64,64]{0,2,1:T(8,128)S(1)} %copy-done.19, f32[256,64]{0,1:T(8,128)S(1)} %copy.189, f32[256,256]{1,0:T(8,128)S(1)} %copy-done.32, f32[64,256]{1,0:T(8,128)S(1)} %copy.187, f32[64,256]{1,0:T(8,128)S(1)} %copy.186, pred[256,256]{1,0:T(8,128)(4,1)S(1)} %copy-done.50, ...), kind=kOutput, calls=%fused_computation.71 | convolution fusion | flops 3244294144 | bytes 13107200 | tf_op jit(solution)/shard_map/transpose(jvp())/while/body/eval_jaxpr/checkpoint/hts,shp->thp/dot_general | solution.py:34
  736.9 9.8 pad_add_fusion
  782.7 54.2 %all_to_all.141 = bf16[256,4,2128]{0,2,1:T(8,128)(2,1)} all-to-all(bf16[256,4,2128]{0,2,1:T(8,128)(2,1)} %bitcast.227), channel_id=1, replica_groups=mesh['dp'=8,'seq'=4] {'seq'}, dimensions={1} | all-to-all | bytes 8716288 | tf_op jit(solution)/shard_map/all_to_all | solution.py:153
  843.3 15.2 %convolution_convert_fusion.4 = bf16[1024,2048]{1,0:T(8,128)(2,1)} fusion(bf16[1024,2128]{1,0:T(8,128)(2,1)} %bitcast.229, bf16[2048,2128]{1,0:T(8,128)(2,1)} %all-gather.7.cloned.1.call-done), kind=kOutput, calls=%fused_computation.95 | convolution fusion | flops 8927576064 | bytes 17268736 | tf_op jit(solution)/shard_map/dot_general | solution.py:267
  859.7 10.9 convolution_convert_fusion.2
  870.7 14.7 %convolution_convert_fusion = bf16[2048,2128]{0,1:T(8,128)(2,1)} fusion(bf16[1024,2048]{1,0:T(8,128)(2,1)} %all-gather.5.cloned.1.call-done, bf16[1024,2128]{1,0:T(8,128)(2,1)} %bitcast.230), kind=kOutput, calls=%fused_computation.21 | convolution fusion | flops 8929837056 | bytes 17268736 | tf_op jit(solution)/shard_map/dot_general | solution.py:274
  885.6 10.2 convolution_convert_fusion.5
  903.5 10.3 all-to-all-done.3
  913.8 79.4 %reduce-scatter.11.cloned.1.call-done = bf16[512,512]{1,0:T(8,128)(2,1)} async-done(((bf16[4096,512]{1,0:T(8,128)(2,1)}), bf16[512,512]{1,0:T(8,128)(2,1)}) %reduce-scatter.11.cloned.1.call-update) | async-done | bytes 524304 | tf_op jit(solution)/shard_map/reduce_scatter | solution.py:166
  1001.2 48.3 %all-reduce.15 = (f32[2048]{0:T(1024)}, f32[4352]{0:T(1024)}, f32[64]{0:T(128)}, f32[64]{0:T(128)}, f32[64]{0:T(128)}, /*index=5*/f32[4096]{0:T(1024)}) all-reduce(f32[2048]{0:T(1024)S(1)} %get-tuple-element.201, f32[4352]{0:T(1024)S(1)} %get-tuple-element.200, ...), channel_id=1, replica_groups=mesh['dp'=8,'seq'=4] {'dp','seq'}, use_global_device_ids=true, to_apply=%region_29.30 | all-reduce | flops 10688 | bytes 85504 | tf_op jit(solution)/shard_map/psum | solution.py:290
  1055.1 95.8 %reduce-scatter.9.cloned.1.call-done = bf16[256,2128]{0,1:T(8,128)(2,1)} async-done(((bf16[2048,2128]{0,1:T(8,128)(2,1)}), bf16[256,2128]{0,1:T(8,128)(2,1)}) %reduce-scatter.9.cloned.1.call-update) | async-done | bytes 1089552 | tf_op jit(solution)/shard_map/reduce_scatter | solution.py:166
  1161.6 11.1 all-to-all-done.6
  1177.7 98.8 %all-reduce.18.cloned.1.call-done = f32[4352,4]{0,1:T(4,128)} async-done(((f32[4352,4]{0,1:T(4,128)}), f32[4352,4]{0,1:T(4,128)}) %all-reduce.18.cloned.1.call-update) | async-done | bytes 69648 | tf_op jit(solution)/shard_map/psum | solution.py:290
  (326 shorter events, 311.4 us)
Async XLA Ops:
  7.2 87.6 %all-gather.11.cloned.1.call-start = ((), (), s32[]{:S(2)}) async-start(), calls=%async_computation.15 | async-start | bytes 4718592 | tf_op jit(solution)/shard_map/all_gather | solution.py:140
  21.7 109.6 %all-gather.5.cloned.1.call-start = ((), (), s32[]{:S(2)}) async-start(), calls=%async_computation.12 | async-start | bytes 5242880 | tf_op jit(solution)/shard_map/all_gather | solution.py:145
  23.4 241.0 %all-gather.7.cloned.1.call-start = ((), (), s32[]{:S(2)}) async-start(), calls=%async_computation.13 | async-start | bytes 10027008 | tf_op jit(solution)/shard_map/all_gather | solution.py:139
  25.2 20.6 %copy-start.17 = (bf16[1,256,2048]{2,1,0:T(8,128)(2,1)S(1)}, bf16[1,256,2048]{2,1,0:T(8,128)(2,1)}, u32[]{:S(2)}) copy-start(bf16[1,256,2048]{2,1,0:T(8,128)(2,1)} %param.17) | copy-start | bytes 3145732
  45.1 498.3 %reduce-scatter.5.cloned.1.call-start = ((), (), s32[]{:S(2)}) async-start(), calls=%async_computation.16 | async-start | bytes 10485760 | tf_op jit(solution)/shard_map/reduce_scatter | solution.py:157
  65.1 38.6 %copy-start.27 = (bf16[256,4,512]{2,0,1:T(8,128)(2,1)}, bf16[256,4,512]{2,0,1:T(8,128)(2,1)S(1)}, u32[]{:S(2)}) copy-start(bf16[256,4,512]{2,0,1:T(8,128)(2,1)S(1)} %all_to_all.140) | copy-start | bytes 3145732
  280.5 101.9 %copy-start.58 = (f32[64]{0:T(128)S(1)}, f32[64]{0:T(128)}, u32[]{:S(2)}) copy-start(f32[64]{0:T(128)} %param.23) | copy-start | bytes 772
  280.5 99.3 %all-to-all-start.1 = ((bf16[4,256,2128]{1,2,0:T(8,128)(2,1)}), bf16[4,256,2128]{1,2,0:T(8,128)(2,1)}, u32[]{:S(2)}, u32[]{:S(2)}) async-start(bf16[4,256,2128]{1,2,0:T(8,128)(2,1)} %bitcast.226), calls=%async_computation.1 | async-start | bytes 8716288 | tf_op jit(solution)/shard_map/all_to_all | solution.py:149
  286.4 572.2 %all-gather.9.cloned.1.call-start = ((), (), s32[]{:S(2)}) async-start(), calls=%async_computation.14 | async-start | bytes 10485760 | tf_op jit(solution)/shard_map/all_gather | solution.py:145
  288.8 97.5 %copy-start.62 = (f32[64]{0:T(128)}, f32[64]{0:T(128)S(1)}, u32[]{:S(2)}) copy-start(f32[64]{0:T(128)S(1)} %exponential_negate_fusion) | copy-start | bytes 772
  382.4 18.5 %copy-start.25 = (bf16[256,64]{1,0:T(8,128)(2,1)}, bf16[256,64]{1,0:T(8,128)(2,1)S(1)}, u32[]{:S(2)}) copy-start(bf16[256,64]{1,0:T(8,128)(2,1)S(1)} %copy.213) | copy-start | bytes 98308
  390.9 18.5 %collective-permute-start.2 = (bf16[3,4352]{1,0:T(4,128)(2,1)}, bf16[3,4352]{1,0:T(4,128)(2,1)S(1)}, u32[]{:S(2)}, u32[]{:S(2)}) collective-permute-start(bf16[3,4352]{1,0:T(4,128)(2,1)} %copy.211), channel_id=1, source_target_pairs={{0,1},{1,2},{2,3},{4,5},{5,6},{6,7},{8,9},{9,10},{10,11},{12,13},{... | collective-permute-start | bytes 78344 | tf_op jit(solution)/shard_map/ppermute | solution.py:23
  442.8 14.0 %collective-permute-start = (bf16[64,64,128]{2,1,0:T(8,128)(2,1)}, bf16[64,64,128]{2,1,0:T(8,128)(2,1)S(1)}, u32[]{:S(2)}, u32[]{:S(2)}) collective-permute-start(bf16[64,64,128]{2,1,0:T(8,128)(2,1)} %fusion.169), channel_id=1, source_target_pairs={{0,1},{1,2},{2,3},{4,5},{5,6},{6,7},{8,9},{9,10},{10,11},{12,13},{... | collective-permute-start | bytes 3145736 | tf_op jit(solution)/shard_map/while/body/eval_jaxpr/ppermute | solution.py:23
  461.9 16.3 %collective-permute-start = (bf16[64,64,128]{2,1,0:T(8,128)(2,1)}, bf16[64,64,128]{2,1,0:T(8,128)(2,1)S(1)}, u32[]{:S(2)}, u32[]{:S(2)}) collective-permute-start(bf16[64,64,128]{2,1,0:T(8,128)(2,1)} %fusion.169), channel_id=1, source_target_pairs={{0,1},{1,2},{2,3},{4,5},{5,6},{6,7},{8,9},{9,10},{10,11},{12,13},{... | collective-permute-start | bytes 3145736 | tf_op jit(solution)/shard_map/while/body/eval_jaxpr/ppermute | solution.py:23
  483.3 16.3 %collective-permute-start = (bf16[64,64,128]{2,1,0:T(8,128)(2,1)}, bf16[64,64,128]{2,1,0:T(8,128)(2,1)S(1)}, u32[]{:S(2)}, u32[]{:S(2)}) collective-permute-start(bf16[64,64,128]{2,1,0:T(8,128)(2,1)} %fusion.169), channel_id=1, source_target_pairs={{0,1},{1,2},{2,3},{4,5},{5,6},{6,7},{8,9},{9,10},{10,11},{12,13},{... | collective-permute-start | bytes 3145736 | tf_op jit(solution)/shard_map/while/body/eval_jaxpr/ppermute | solution.py:23
  506.8 23.1 %copy-start.15 = (f32[256,64,64]{0,2,1:T(8,128)}, f32[256,64,64]{0,2,1:T(8,128)S(1)}, u32[]{:S(2)}) copy-start(f32[256,64,64]{0,2,1:T(8,128)S(1)} %fusion.115) | copy-start | bytes 12582916
  581.3 17.0 %collective-permute-start.1 = (bf16[64,64,128]{2,1,0:T(8,128)(2,1)}, bf16[64,64,128]{2,1,0:T(8,128)(2,1)S(1)}, u32[]{:S(2)}, u32[]{:S(2)}) collective-permute-start(bf16[64,64,128]{2,1,0:T(8,128)(2,1)} %fusion.170), channel_id=1, source_target_pairs={{1,0},{2,1},{3,2},{5,4},{6,5},{7,6},{9,8},{10,9},{11,10},{13,12},{... | collective-permute-start | bytes 3145736 | tf_op jit(solution)/shard_map/while/body/eval_jaxpr/ppermute | solution.py:23
  601.4 16.3 %collective-permute-start.1 = (bf16[64,64,128]{2,1,0:T(8,128)(2,1)}, bf16[64,64,128]{2,1,0:T(8,128)(2,1)S(1)}, u32[]{:S(2)}, u32[]{:S(2)}) collective-permute-start(bf16[64,64,128]{2,1,0:T(8,128)(2,1)} %fusion.170), channel_id=1, source_target_pairs={{1,0},{2,1},{3,2},{5,4},{6,5},{7,6},{9,8},{10,9},{11,10},{13,12},{... | collective-permute-start | bytes 3145736 | tf_op jit(solution)/shard_map/while/body/eval_jaxpr/ppermute | solution.py:23
  620.9 16.3 %collective-permute-start.1 = (bf16[64,64,128]{2,1,0:T(8,128)(2,1)}, bf16[64,64,128]{2,1,0:T(8,128)(2,1)S(1)}, u32[]{:S(2)}, u32[]{:S(2)}) collective-permute-start(bf16[64,64,128]{2,1,0:T(8,128)(2,1)} %fusion.170), channel_id=1, source_target_pairs={{1,0},{2,1},{3,2},{5,4},{6,5},{7,6},{9,8},{10,9},{11,10},{13,12},{... | collective-permute-start | bytes 3145736 | tf_op jit(solution)/shard_map/while/body/eval_jaxpr/ppermute | solution.py:23
  666.7 27.5 %copy-start.19 = (f32[256,64,64]{0,2,1:T(8,128)S(1)}, f32[256,64,64]{0,2,1:T(8,128)}, u32[]{:S(2)}) copy-start(f32[256,64,64]{0,2,1:T(8,128)} %get-tuple-element.257) | copy-start | bytes 12582916
  716.2 184.9 %reduce-scatter.7.cloned.1.call-start = ((), (), s32[]{:S(2)}) async-start(), calls=%async_computation.17 | async-start | bytes 5242880 | tf_op jit(solution)/shard_map/reduce_scatter | solution.py:157
  747.6 23.6 %collective-permute-start.3 = (bf16[3,4352]{1,0:T(4,128)(2,1)S(1)}, bf16[3,4352]{1,0:T(4,128)(2,1)}, u32[]{:S(2)}, u32[]{:S(2)}) collective-permute-start(bf16[3,4352]{1,0:T(4,128)(2,1)S(1)} %slice.203), channel_id=1, source_target_pairs={{1,0},{2,1},{3,2},{5,4},{6,5},{7,6},{9,8},{10,9},{11,10},{13,12},{... | collective-permute-start | bytes 78344 | tf_op jit(solution)/shard_map/ppermute | solution.py:23
  858.5 134.7 %reduce-scatter.11.cloned.1.call-start = ((), (), s32[]{:S(2)}) async-start(), calls=%async_computation.20 | async-start | bytes 4718592 | tf_op jit(solution)/shard_map/reduce_scatter | solution.py:166
  870.7 280.3 %reduce-scatter.9.cloned.1.call-start = ((), (), s32[]{:S(2)}) async-start(), calls=%async_computation.18 | async-start | bytes 9805824 | tf_op jit(solution)/shard_map/reduce_scatter | solution.py:166
  885.6 15.6 %copy-start.13 = (bf16[1,256,2048]{2,1,0:T(8,128)(2,1)S(1)}, bf16[1,256,2048]{2,1,0:T(8,128)(2,1)}, u32[]{:S(2)}) copy-start(bf16[1,256,2048]{2,1,0:T(8,128)(2,1)} %param.16) | copy-start | bytes 3145732
  895.8 102.1 %copy-start.18 = (bf16[1,256,2048]{2,1,0:T(8,128)(2,1)S(1)}, bf16[1,256,2048]{2,1,0:T(8,128)(2,1)}, u32[]{:S(2)}) copy-start(bf16[1,256,2048]{2,1,0:T(8,128)(2,1)} %param.17) | copy-start | bytes 3145732
  895.8 102.1 %copy-start.55 = (f32[256]{0:T(256)S(1)}, f32[256]{0:T(256)}, u32[]{:S(2)}) copy-start(f32[256]{0:T(256)} %copy-done.54) | copy-start | bytes 3076
  895.8 17.9 %all-to-all-start.3 = ((bf16[4,256,512]{2,1,0:T(8,128)(2,1)}), bf16[4,256,512]{2,1,0:T(8,128)(2,1)S(1)}, u32[]{:S(2)}, u32[]{:S(2)}) async-start(bf16[4,256,512]{2,1,0:T(8,128)(2,1)} %bitcast.250), calls=%async_computation.3 | async-start | bytes 2097152 | tf_op jit(solution)/shard_map/all_to_all | solution.py:218
  900.2 376.4 %all-reduce.18.cloned.1.call-start = ((), (), s32[]{:S(2)}) async-start(), calls=%async_computation.19 | async-start | bytes 139264 | tf_op jit(solution)/shard_map/psum | solution.py:290
  901.1 100.1 %copy-start.45 = (f32[4096]{0:T(1024)S(1)}, f32[4096]{0:T(1024)}, u32[]{:S(2)}) copy-start(f32[4096]{0:T(1024)} %get-tuple-element.198) | copy-start | bytes 49156
  993.2 160.1 %all-to-all-start.7 = ((bf16[4,128,512]{2,1,0:T(8,128)(2,1)}), bf16[4,128,512]{2,1,0:T(8,128)(2,1)}, u32[]{:S(2)}, u32[]{:S(2)}) async-start(bf16[4,128,512]{2,1,0:T(8,128)(2,1)} %bitcast.252), calls=%async_computation.11 | async-start | bytes 1048576 | tf_op jit(solution)/shard_map/all_to_all | solution.py:283
  1153.3 19.4 %all-to-all-start.6 = ((bf16[4,64,2128]{2,1,0:T(8,128)(2,1)}), bf16[4,64,2128]{2,1,0:T(8,128)(2,1)}, u32[]{:S(2)}, u32[]{:S(2)}) async-start(bf16[4,64,2128]{2,1,0:T(8,128)(2,1)} %bitcast.232), calls=%async_computation.9 | async-start | bytes 2228224 | tf_op jit(solution)/shard_map/all_to_all | solution.py:280
  (58 other events, 408.7 us)
Sparse Core Ops, SparseCore 0:
  21.9 72.8 all-gather.10
  96.9 34.3 all-gather.4
  133.5 130.8 all-gather.6
  266.8 115.2 reduce-scatter.4
  716.3 55.2 all-gather.8
  858.7 40.9 reduce-scatter.6
  903.3 89.8 reduce-scatter.10
  997.1 153.7 reduce-scatter.8
  1158.1 118.4 all-reduce.17
where the time goes:
time: 1300 us; the launch traced here: 1280 us
  waiting for transfers between devices  657 us (51%)
  matrix products  207 us (16%)
  blocking collectives  150 us (12%)
  other arithmetic  120 us (9%)
  local copies, waits for them, and re-layouts  93.7 us (7%)
  starting transfers between devices  41.8 us (3%)
  between operations  16 us (1%)
    reduce_scatter x2, waiting for transfers between devices, owner_total(): lax.psum_scatter(term(jnp.int32(0), rows * lax.axis_size('dp')).astype(jn...  175 us
    all_gather x1, waiting for transfers between devices, column_weights(): lax.all_gather(turned[0], 'dp', axis=0, tiled=True)  133 us
    psum x1, waiting for transfers between devices, body(): lax.psum((norm_gain_grad, conv_w_grad, conv_b_grad, dt_bias_grad, a_log_g...  98.8 us
    all_to_all x1, waiting for transfers between devices, into_positions(): lax.all_to_all(values, 'seq', split_axis=0, concat_axis=1, tiled=True)  91 us
    ppermute x8, waiting for transfers between devices, passed_along(): return lax.ppermute(block, axis, route)  80 us
    all_to_all x2, blocking collectives, into_columns(): lax.all_to_all(values, 'seq', split_axis=1, concat_axis=0, tiled=True)  71 us
    dot_general x3, matrix products, stretch_step(): within = jnp.einsum('hts,shp->thp', mixing, block_x, precision=HIGH)  66.9 us
    psum x1, blocking collectives, body(): lax.psum((norm_gain_grad, conv_w_grad, conv_b_grad, dt_bias_grad, a_log_g...  48.3 us
  transfers between devices with their start and end apart: 21, of which 15 were waited for; matrix products, arithmetic and copies ran while one was open for 22% of the time, Pallas kernels for 0%

commit v1 on v0

v1 whole, which is shorter than its diff:
```python
import functools

import jax
import jax.numpy as jnp
from jax import lax
from jax.experimental import pallas as pl
from jax.experimental.pallas import tpu as pltpu
from jax.sharding import Mesh
from jax.sharding import PartitionSpec as P

D = 2048
HEADS = 64
HEADDIM = 64
STATE = 128
KERNEL = 4
STRETCH = 256
INNER = 4096
CHANNELS = 4352
EPSILON = 1e-05
HIGH = lax.Precision.HIGHEST
BF16 = jnp.bfloat16
F32 = jnp.float32
GROUP = ("y", "seq")


def mm(a, b):
    return jnp.dot(a.astype(BF16), b.astype(BF16), preferred_element_type=F32)


def mm_last(a, b):
    return lax.dot_general(
        a.astype(BF16), b.astype(BF16), (((1,), (1,)), ((), ())), preferred_element_type=F32
    )


def iota(shape, axis):
    return lax.broadcasted_iota(jnp.int32, shape, axis)


def head_times(raw, bias, a_log):
    pre = raw + bias
    step = jnp.maximum(pre, 0.0) + jnp.log1p(jnp.exp(-jnp.abs(pre)))
    log_decay = step * -jnp.exp(a_log)
    width = raw.shape[1]
    upper = (iota((width, width), 0) <= iota((width, width), 1)).astype(F32)
    running = jnp.dot(log_decay, upper, precision=HIGH, preferred_element_type=F32)
    return pre, step, log_decay, running


def over_channels(values, pair):
    left = values[:, 2 * pair : 2 * pair + 1]
    right = values[:, 2 * pair + 1 : 2 * pair + 2]
    lane = iota((values.shape[0], 2 * HEADDIM), 1)
    return jnp.where(lane < HEADDIM, left, right)


def spread(values):
    pairs = values.shape[1] // 2
    return jnp.concatenate([over_channels(values, i) for i in range(pairs)], axis=1)


def convolved(block, halo, conv_w, conv_b):
    rows = block.shape[0]
    joined = jnp.concatenate([halo, block], axis=0)
    base = halo.shape[0] - KERNEL + 1
    shifted = [joined[base + k : base + k + rows] for k in range(KERNEL)]
    total = conv_b
    for k in range(KERNEL):
        total = total + conv_w[k : k + 1] * shifted[k]
    return total, shifted


def forward_kernel(
    x_ref, gate_ref, bc_ref, bct_ref, dt_ref, wx_ref, bx_ref, bias_ref, alog_ref, skip_ref,
    scanned_ref, state_ref, state, halo,
):
    @pl.when(pl.program_id(1) == 0)
    def _():
        state[...] = jnp.zeros_like(state)
        halo[...] = jnp.zeros_like(halo)

    rows, channels = x_ref.shape
    raw = x_ref[...].astype(F32)
    conv, _ = convolved(raw, halo[...], wx_ref[...], bx_ref[...])
    halo[...] = raw[rows - 8 :]
    xs = conv / (1.0 + jnp.exp(-conv))
    _, step_t, _, run_t = head_times(dt_ref[...], bias_ref[...], alog_ref[...])
    run = run_t.T
    xdt = xs * spread(step_t.T)
    b_t = bct_ref[:STATE]
    c = bc_ref[:, STATE:]
    causal = iota((rows, rows), 0) >= iota((rows, rows), 1)
    products = jnp.where(causal, mm(c, b_t), 0.0)
    entering = state[...]
    state_ref[0] = entering
    inward = mm(c, entering) * spread(jnp.exp(run))
    skipped = skip_ref[...] * xs
    lane = iota((rows, 2 * HEADDIM), 1)
    for pair in range(channels // 128):
        cols = slice(pair * 128, pair * 128 + 128)
        part = xdt[:, cols]
        total = inward[:, cols] + skipped[:, cols]
        for side in range(2):
            h = 2 * pair + side
            decay = jnp.exp(jnp.minimum(run[:, h : h + 1] - run_t[h : h + 1], 0.0))
            own = (lane < HEADDIM) if side == 0 else (lane >= HEADDIM)
            total = total + mm(products * decay, jnp.where(own, part, 0.0))
        scanned_ref[:, cols] = total
    last = run[rows - 1 :]
    to_end = spread(jnp.exp(last - run))
    state[...] = entering * spread(jnp.exp(last)) + mm(b_t, xdt * to_end)


def backward_kernel(
    x_ref, halo_ref, gate_ref, bc_ref, bct_ref, dt_ref, wx_ref, bx_ref, bias_ref, alog_ref, skip_ref,
    gain_ref, scanned_ref, state_ref, mixed_grad_ref, norms_ref,
    grad_ref, dbc_ref, ddt_ref, sums_ref, heads_ref,
    lam, rim,
):
    step_id = pl.program_id(1)
    first = (pl.program_id(0) == 0) & (step_id == 0)

    @pl.when(first)
    def _():
        sums_ref[...] = jnp.zeros_like(sums_ref)
        heads_ref[...] = jnp.zeros_like(heads_ref)

    @pl.when(step_id == 0)
    def _():
        lam[...] = jnp.zeros_like(lam)
        rim[...] = jnp.zeros_like(rim)

    rows, channels = x_ref.shape
    heads = channels // HEADDIM
    gate = gate_ref[...].astype(F32)
    scanned = scanned_ref[...]
    mixed_grad = mixed_grad_ref[...].astype(F32)
    norms = norms_ref[...].T
    r = norms[:, 0:1]
    inner = norms[:, 1:2]
    sig = 1.0 / (1.0 + jnp.exp(-gate))
    silu = gate * sig
    product = scanned * silu
    product_grad = r * (mixed_grad * gain_ref[...]) - product * (r * r * r * inner)
    sums_ref[5:6] += jnp.sum(mixed_grad * product * r, 0, keepdims=True)
    dy = product_grad * silu
    grad_ref[:, :channels] = (product_grad * scanned * (sig * (1.0 + gate * (1.0 - sig)))).astype(BF16)

    raw = x_ref[...].astype(F32)
    before = jnp.where(step_id == pl.num_programs(1) - 1, 0.0, halo_ref[...].astype(F32))
    conv, shifted = convolved(raw, before, wx_ref[...], bx_ref[...])
    sig_c = 1.0 / (1.0 + jnp.exp(-conv))
    xs = conv * sig_c
    sums_ref[6:7] += jnp.sum(dy * xs, 0, keepdims=True)
    pre, step_t, decay_t, run_t = head_times(dt_ref[...], bias_ref[...], alog_ref[...])
    run = run_t.T
    step = spread(step_t.T)
    xdt = xs * step
    b = bc_ref[:, :STATE]
    c = bc_ref[:, STATE:]
    b_t = bct_ref[:STATE]
    c_t = bct_ref[STATE:]
    causal = iota((rows, rows), 0) >= iota((rows, rows), 1)
    products = jnp.where(causal, mm(c, b_t), 0.0)
    entering = state_ref[0]
    leaving = lam[...]
    last = run[rows - 1 :]
    to_end = spread(jnp.exp(last - run))
    whole = spread(jnp.exp(last))
    dye = dy * spread(jnp.exp(run))
    xend = xdt * to_end
    inward = dye * mm(c, entering)
    outward_grad = mm(b, leaving) * to_end
    outward = outward_grad * xdt
    dc_t = mm_last(entering, dye)
    db_t = mm_last(leaving, xend)
    kept = leaving * whole
    lam[...] = kept + mm(c_t, dye)

    dy_t = dy.T.astype(BF16)
    lane = iota((rows, 2 * HEADDIM), 1)
    wide = iota((rows, heads), 1)
    dproducts = jnp.zeros((rows, rows), F32)
    row_sums = jnp.zeros((rows, heads), F32)
    col_sums = []
    dxdt_t = []
    for h in range(heads):
        cols = slice((h // 2) * 128, (h // 2) * 128 + 128)
        own = (lane < HEADDIM) if h % 2 == 0 else (lane >= HEADDIM)
        decay = jnp.exp(jnp.minimum(run[:, h : h + 1] - run_t[h : h + 1], 0.0))
        weights = products * decay
        dweights = mm_last(dy[:, cols], jnp.where(own, xdt[:, cols], 0.0))
        dproducts = dproducts + dweights * decay
        shares = dweights * weights
        row_sums = jnp.where(wide == h, jnp.sum(shares, 1, keepdims=True), row_sums)
        col_sums.append(jnp.sum(shares, 0, keepdims=True))
        dxdt_t.append(mm(dy_t[h * HEADDIM : (h + 1) * HEADDIM], weights))
    dproducts = jnp.where(causal, dproducts, 0.0)
    dc_t = dc_t + mm_last(b_t, dproducts)
    db_t = db_t + mm(c_t, dproducts)
    dbc_ref[:STATE] = db_t
    dbc_ref[STATE:] = dc_t
    dxdt = jnp.concatenate(dxdt_t, 0).T + outward_grad

    member = (iota((heads, channels), 1) // HEADDIM == iota((heads, channels), 0)).astype(F32)

    def per_head(values):
        return lax.dot_general(
            member, values, (((1,), (1,)), ((), ())), precision=HIGH, preferred_element_type=F32
        )

    out_t = per_head(outward)
    run_grad = per_head(inward) - out_t + row_sums.T - jnp.concatenate(col_sums, 0)
    at_end = jnp.sum(out_t, 1, keepdims=True) + jnp.sum(per_head(kept * entering), 1, keepdims=True)
    lower = (iota((rows, rows), 0) >= iota((rows, rows), 1)).astype(F32)
    decay_grad = at_end + jnp.dot(run_grad, lower, precision=HIGH, preferred_element_type=F32)
    step_grad = per_head(dxdt * xs) - jnp.exp(alog_ref[...]) * decay_grad
    dt_grad = step_grad / (1.0 + jnp.exp(-pre))
    ddt_ref[...] = dt_grad.astype(BF16)
    heads_ref[:, 0:1] += jnp.sum(dt_grad, 1, keepdims=True)
    heads_ref[:, 1:2] += jnp.sum(decay_grad * decay_t, 1, keepdims=True)

    dx = dxdt * step + skip_ref[...] * dy
    dconv = dx * (sig_c * (1.0 + conv * (1.0 - sig_c)))
    sums_ref[4:5] += jnp.sum(dconv, 0, keepdims=True)
    for k in range(KERNEL):
        sums_ref[k : k + 1] += jnp.sum(dconv * shifted[k], 0, keepdims=True)
    joined = jnp.concatenate([dconv, rim[...]], 0)
    rim[...] = dconv[:8]
    dx_in = wx_ref[KERNEL - 1 : KERNEL] * dconv
    for k in range(KERNEL - 1):
        ahead = KERNEL - 1 - k
        dx_in = dx_in + wx_ref[k : k + 1] * joined[ahead : ahead + rows]
    grad_ref[:, channels:] = dx_in.astype(BF16)


def whole_spec(array):
    return pl.BlockSpec(array.shape, lambda q, i: (0,) * array.ndim)


def scan_forward(projected, bc, bc_t, dt_t, params, seqs):
    total, channels = projected.shape[0], projected.shape[1] // 2
    heads = channels // HEADDIM
    steps = total // seqs // STRETCH
    row = lambda q, i: q * steps + i
    return pl.pallas_call(
        forward_kernel,
        grid=(seqs, steps),
        in_specs=[
            pl.BlockSpec((STRETCH, channels), lambda q, i: (row(q, i), 1)),
            pl.BlockSpec((STRETCH, channels), lambda q, i: (row(q, i), 0)),
            pl.BlockSpec((STRETCH, 2 * STATE), lambda q, i: (row(q, i), 0)),
            pl.BlockSpec((2 * STATE, STRETCH), lambda q, i: (0, row(q, i))),
            pl.BlockSpec((heads, STRETCH), lambda q, i: (0, row(q, i))),
        ]
        + [whole_spec(p) for p in params],
        out_specs=[
            pl.BlockSpec((STRETCH, channels), lambda q, i: (row(q, i), 0)),
            pl.BlockSpec((1, STATE, channels), lambda q, i: (row(q, i), 0, 0)),
        ],
        out_shape=[
            jax.ShapeDtypeStruct((total, channels), F32),
            jax.ShapeDtypeStruct((seqs * steps, STATE, channels), F32),
        ],
        scratch_shapes=[pltpu.VMEM((STATE, channels), F32), pltpu.VMEM((8, channels), F32)],
        compiler_params=pltpu.CompilerParams(vmem_limit_bytes=48 << 20),
        name="scan_forward",
    )(projected, projected, bc, bc_t, dt_t, *params)


def scan_backward(projected, bc, bc_t, dt_t, params, gain, scanned, states, mixed_grad, norms, seqs):
    total, channels = projected.shape[0], projected.shape[1] // 2
    heads = channels // HEADDIM
    steps = total // seqs // STRETCH
    row = lambda q, i: q * steps + steps - 1 - i
    halo_row = lambda q, i: jnp.maximum(row(q, i) * (STRETCH // 16) - 1, 0)
    return pl.pallas_call(
        backward_kernel,
        grid=(seqs, steps),
        in_specs=[
            pl.BlockSpec((STRETCH, channels), lambda q, i: (row(q, i), 1)),
            pl.BlockSpec((16, channels), lambda q, i: (halo_row(q, i), 1)),
            pl.BlockSpec((STRETCH, channels), lambda q, i: (row(q, i), 0)),
            pl.BlockSpec((STRETCH, 2 * STATE), lambda q, i: (row(q, i), 0)),
            pl.BlockSpec((2 * STATE, STRETCH), lambda q, i: (0, row(q, i))),
            pl.BlockSpec((heads, STRETCH), lambda q, i: (0, row(q, i))),
        ]
        + [whole_spec(p) for p in params]
        + [
            whole_spec(gain),
            pl.BlockSpec((STRETCH, channels), lambda q, i: (row(q, i), 0)),
            pl.BlockSpec((1, STATE, channels), lambda q, i: (row(q, i), 0, 0)),
            pl.BlockSpec((STRETCH, channels), lambda q, i: (row(q, i), 0)),
            pl.BlockSpec((8, STRETCH), lambda q, i: (0, row(q, i))),
        ],
        out_specs=[
            pl.BlockSpec((STRETCH, 2 * channels), lambda q, i: (row(q, i), 0)),
            pl.BlockSpec((2 * STATE, STRETCH), lambda q, i: (0, row(q, i))),
            pl.BlockSpec((heads, STRETCH), lambda q, i: (0, row(q, i))),
            pl.BlockSpec((8, channels), lambda q, i: (0, 0)),
            pl.BlockSpec((heads, 128), lambda q, i: (0, 0)),
        ],
        out_shape=[
            jax.ShapeDtypeStruct((total, 2 * channels), BF16),
            jax.ShapeDtypeStruct((2 * STATE, total), F32),
            jax.ShapeDtypeStruct((heads, total), BF16),
            jax.ShapeDtypeStruct((8, channels), F32),
            jax.ShapeDtypeStruct((heads, 128), F32),
        ],
        scratch_shapes=[pltpu.VMEM((STATE, channels), F32), pltpu.VMEM((8, channels), F32)],
        compiler_params=pltpu.CompilerParams(vmem_limit_bytes=56 << 20),
        name="scan_backward",
    )(projected, projected, projected, bc, bc_t, dt_t, *params, gain, scanned, states, mixed_grad, norms)


def shift_later(values, by, seqs):
    if by == 0:
        return values
    split = values.reshape(values.shape[0], seqs, -1)
    moved = jnp.pad(split, ((0, 0), (0, 0), (by, 0)))[:, :, : split.shape[2]]
    return moved.reshape(values.shape)


def shift_earlier(values, by, seqs):
    if by == 0:
        return values
    split = values.reshape(values.shape[0], seqs, -1)
    moved = jnp.pad(split, ((0, 0), (0, 0), (0, by)))[:, :, by:]
    return moved.reshape(values.shape)


class Layout:
    def __init__(self, planes, group, rows_out):
        self.planes, self.group = planes, group
        self.aligned = rows_out % HEADDIM == 0
        self.blocks = planes if self.aligned else 1
        self.block = INNER // group // self.blocks
        self.heads = HEADS // group
        self.channels = INNER // group
        self.small = 2 * STATE // group

    def pieces(self, values, unit):
        rows = values.shape[0]
        parts = values.reshape(rows, self.blocks, self.group, self.block // HEADDIM * unit)
        return parts.transpose(0, 2, 1, 3).reshape(rows, self.group, -1)

    def joined(self, values, unit):
        rows = values.shape[0]
        parts = values.reshape(rows, self.group, self.blocks, self.block // HEADDIM * unit)
        return parts.transpose(0, 2, 1, 3).reshape(rows, -1)

    def columns(self, w):
        gate = self.pieces(w[:, :INNER], HEADDIM)
        x = self.pieces(w[:, INNER : 2 * INNER], HEADDIM)
        bc = w[:, 2 * INNER : INNER + CHANNELS].reshape(w.shape[0], self.group, self.small)
        dt = self.pieces(w[:, INNER + CHANNELS :], 1)
        return jnp.concatenate([gate, x, bc, dt], 2)

    def uncolumns(self, g):
        c, s = self.channels, self.small
        gate = self.joined(g[:, :, :c], HEADDIM)
        x = self.joined(g[:, :, c : 2 * c], HEADDIM)
        bc = g[:, :, 2 * c : 2 * c + s].reshape(g.shape[0], -1)
        dt = self.joined(g[:, :, 2 * c + s :], 1)
        return jnp.concatenate([gate, x, bc, dt], 1)


def body(
    tokens, cotangent, lengths, norm_gain, w_in, conv_w, conv_b, dt_bias, a_log, skip_scale, gate_gain, w_out,
):
    row_count = tokens.shape[1]
    planes, group = lax.axis_size("z"), lax.axis_size("y") * lax.axis_size("seq")
    seqs = lax.axis_size("y")
    rank = lax.axis_index("y") * lax.axis_size("seq") + lax.axis_index("seq")
    lay = Layout(planes, group, w_out.shape[0])
    channels, small = lay.channels, lay.small
    inputs = tokens.reshape(row_count, D).astype(F32)
    position = lax.axis_index("seq") * row_count + jnp.arange(row_count, dtype=jnp.int32)
    valid_mask = (position < lengths[0]).astype(F32)[:, None]
    rms = lax.rsqrt(jnp.mean(inputs * inputs, -1, keepdims=True) + EPSILON)
    normed = (inputs * rms * norm_gain).astype(BF16)
    masked_cot = cotangent.reshape(row_count, D).astype(F32) * valid_mask
    branch_grad = masked_cot.astype(BF16)

    pieces = lay.columns(w_in.astype(BF16)).reshape(w_in.shape[0], -1)
    plane_rows = lax.all_to_all(pieces, GROUP, split_axis=1, concat_axis=0, tiled=True)
    w_own = lax.all_gather(plane_rows, "z", axis=0, tiled=True)
    w_main, w_small = w_own[:, : 2 * channels], w_own[:, 2 * channels :]
    if lay.aligned:
        out_own = lax.all_gather(w_out.astype(BF16), "z", axis=0, tiled=True)
    else:
        out_all = lax.all_gather(w_out.astype(BF16), ("z",) + GROUP, axis=0, tiled=True)
        out_own = lax.dynamic_slice_in_dim(out_all, rank * channels, channels, 0)

    def own(values, unit):
        return lax.dynamic_index_in_dim(lay.pieces(values, unit), rank, 1, keepdims=False)

    conv_wx = own(conv_w[:INNER].T, HEADDIM)
    conv_bx = own(conv_b[None, :INNER], HEADDIM)
    bias_own = own(dt_bias[None], 1).T
    a_own = own(a_log[None], 1).T
    skip_own = jnp.repeat(own(skip_scale[None], 1), HEADDIM, 1)
    gain_own = own(gate_gain[None], HEADDIM)
    params = (conv_wx, conv_bx, bias_own, a_own, skip_own)

    normed_all = lax.all_gather(normed, GROUP, axis=0, tiled=True)
    projected = jnp.dot(normed_all, w_main, preferred_element_type=F32).astype(BF16)
    small_t = lax.dot_general(
        w_small, normed_all, (((0,), (1,)), ((), ())), preferred_element_type=F32
    ).astype(BF16)
    dt_t = small_t[small:].astype(F32)
    bc_in = lax.all_gather(small_t[:small], GROUP, axis=0, tiled=True).astype(F32)
    conv_bc = conv_b[INNER:, None]
    for k in range(KERNEL):
        conv_bc = conv_bc + conv_w[INNER:, k : k + 1] * shift_later(bc_in, KERNEL - 1 - k, seqs)
    bc_t = jax.nn.silu(conv_bc).astype(BF16)
    bc = bc_t.T

    scanned, states = scan_forward(projected, bc, bc_t, dt_t, params, seqs)

    grad_all = lax.all_gather(branch_grad, GROUP, axis=0, tiled=True)
    mixed_grad = lax.dot_general(
        grad_all, out_own, (((1,), (1,)), ((), ())), preferred_element_type=F32
    )
    product = scanned * jax.nn.silu(projected[:, :channels].astype(F32))
    sums = lax.psum(
        jnp.stack([jnp.sum(product * product, 1), jnp.sum(mixed_grad * gain_own * product, 1)]), GROUP
    )
    r = lax.rsqrt(sums[0] / INNER + EPSILON)
    norms = jnp.concatenate([r[None], sums[1:] / INNER, jnp.zeros((6, r.shape[0]), F32)], 0)
    mixed = (product * r[:, None] * gain_own).astype(BF16)

    branch = lax.psum_scatter(
        jnp.dot(mixed, out_own, preferred_element_type=F32).astype(BF16),
        GROUP, scatter_dimension=0, tiled=True,
    ).astype(F32)
    output = (valid_mask * (inputs + branch)).astype(BF16)
    out_part = lax.dot_general(
        mixed, grad_all, (((0,), (0,)), ((), ())), preferred_element_type=F32
    ).astype(BF16)
    if lay.aligned:
        grad_w_out = lax.psum_scatter(out_part, "z", scatter_dimension=0, tiled=True).astype(F32)
    else:
        placed = lax.dynamic_update_slice_in_dim(jnp.zeros((INNER, D), BF16), out_part, rank * channels, 0)
        grad_w_out = lax.psum_scatter(placed, ("z",) + GROUP, scatter_dimension=0, tiled=True).astype(F32)

    proj_grad, dbc_t, ddt_t, sums_x, sums_h = scan_backward(
        projected, bc, bc_t, dt_t, params, gain_own, scanned, states, mixed_grad, norms, seqs
    )
    dbc = lax.psum_scatter(dbc_t, GROUP, scatter_dimension=0, tiled=True)
    own_rows = lambda v: lax.dynamic_slice_in_dim(v, rank * small, small, 0)
    conv_own, in_own, w_bc = own_rows(conv_bc), own_rows(bc_in), own_rows(conv_w[INNER:])
    sig = jax.nn.sigmoid(conv_own)
    dconv = dbc * sig * (1.0 + conv_own * (1.0 - sig))
    din = 0.0
    grad_w_bc = []
    for k in range(KERNEL):
        grad_w_bc.append(jnp.sum(dconv * shift_later(in_own, KERNEL - 1 - k, seqs), 1))
        din = din + w_bc[:, k : k + 1] * shift_earlier(dconv, KERNEL - 1 - k, seqs)
    small_grad_t = jnp.concatenate([din.astype(BF16), ddt_t], 0)

    contract_rows = (((0,), (0,)), ((), ()))
    in_main = lax.dot_general(normed_all, proj_grad, contract_rows, preferred_element_type=F32)
    in_small = lax.dot_general(
        normed_all, small_grad_t, (((0,), (1,)), ((), ())), preferred_element_type=F32
    )
    in_part = jnp.concatenate([in_main.astype(BF16), in_small.astype(BF16)], 1)
    in_rows = lax.psum_scatter(in_part, "z", scatter_dimension=0, tiled=True)
    in_pieces = lax.all_to_all(in_rows, GROUP, split_axis=0, concat_axis=1, tiled=True)
    grad_w_in = lay.uncolumns(in_pieces.reshape(w_in.shape[0], group, -1).astype(F32))

    normed_part = lax.dot_general(
        proj_grad, w_main, (((1,), (1,)), ((), ())), preferred_element_type=F32
    ) + lax.dot_general(small_grad_t, w_small, (((0,), (1,)), ((), ())), preferred_element_type=F32)
    normed_grad = lax.psum_scatter(
        normed_part.astype(BF16), GROUP, scatter_dimension=0, tiled=True
    ).astype(F32)
    g = normed_grad * norm_gain
    input_grad = masked_cot + rms * g - inputs * (rms ** 3 * jnp.mean(g * inputs, -1, keepdims=True))
    norm_gain_grad = jnp.sum(normed_grad * inputs * rms, 0)

    own_sums = jnp.concatenate(
        [
            sums_x[: KERNEL + 2].reshape(-1),
            jnp.sum(sums_x[KERNEL + 2].reshape(-1, HEADDIM), 1),
            sums_h[:, 0],
            sums_h[:, 1],
            jnp.stack(grad_w_bc).reshape(-1),
            jnp.sum(dconv, 1),
        ]
    )
    count = own_sums.shape[0]
    everyone = lax.all_gather(jnp.concatenate([own_sums, norm_gain_grad]), ("z",) + GROUP)
    grad_norm_gain = jnp.sum(everyone[:, count:], 0)
    by_rank = jnp.sum(everyone[:, :count].reshape(planes, group, count), 0)
    at = 0

    def take(size):
        nonlocal at
        at += size
        return by_rank[:, at - size : at]

    taken_x = take((KERNEL + 2) * channels).reshape(group, KERNEL + 2, channels).transpose(1, 0, 2)
    full_x = lay.joined(taken_x, HEADDIM)
    grad_skip, grad_bias, grad_a = (
        lay.joined(take(lay.heads)[None], 1)[0] for _ in range(3)
    )
    conv_w_bc = take(KERNEL * small).reshape(group, KERNEL, small).transpose(1, 0, 2).reshape(KERNEL, -1)
    conv_b_bc = take(small).reshape(-1)
    grad_conv_w = jnp.concatenate([full_x[:KERNEL], conv_w_bc], 1).T
    grad_conv_b = jnp.concatenate([full_x[KERNEL], conv_b_bc])
    return (
        output.reshape(tokens.shape),
        input_grad.reshape(1, row_count, D),
        grad_norm_gain,
        grad_w_in,
        grad_conv_w,
        grad_conv_b,
        grad_bias,
        grad_a,
        grad_skip,
        full_x[KERNEL + 1],
        grad_w_out,
    )


def solution(mesh):
    dp, seq = mesh.shape["dp"], mesh.shape["seq"]
    inner_mesh = Mesh(mesh.devices.reshape(dp // 2, 2, seq), ("z", "y", "seq"))
    placed = P(("z", "y"), "seq", None)
    rows = P(("z", "y", "seq"), None)
    in_specs = (placed, placed, P(("z", "y")), P(), rows, P(), P(), P(), P(), P(), P(), rows)
    out_specs = (placed, placed, P(), rows, P(), P(), P(), P(), P(), P(), rows)
    return jax.shard_map(body, mesh=inner_mesh, in_specs=in_specs, out_specs=out_specs, check_vma=False)
```

time: 1300 us -> 884 us (0.68)
  blocking collectives: 150 us -> 41.7 us
  matrix products: 207 us -> 103 us
  other arithmetic: 120 us -> 25 us
  waiting for transfers between devices: 657 us -> 562 us
  Pallas kernels: 0 us -> 70.2 us
  local copies, waits for them, and re-layouts: 93.7 us -> 55.5 us
  starting transfers between devices: 41.8 us -> 5.6 us
    unnamed x9 -> x12, waiting for transfers between devices: 0.16 us -> 131 us
    all_to_all x4 -> x1, waiting for transfers between devices: 112 us -> 0.01 us  [body(): lax.all_to_all(in_rows, GROUP, split_axis=0, concat_axis=1, tiled=True)]
    dot_general x22 -> x9, matrix products: 207 us -> 103 us  [the longest x1 15.5 us: body(): lax.dot_general(proj_grad, w_main, (((1,), (1,)), ((), ())), preferred_el...]
    psum x1 -> x0, waiting for transfers between devices: 98.8 us -> none  [body(): lax.psum((norm_gain_grad, conv_w_grad, conv_b_grad, dt_bias_grad, a_log_g...]
    all_to_all x4 -> x1, blocking collectives: 102 us -> 21.2 us  [body(): lax.all_to_all(pieces, GROUP, split_axis=1, concat_axis=0, tiled=True)]
    ppermute x8 -> x0, waiting for transfers between devices: 80 us -> none  [passed_along(): return lax.ppermute(block, axis, route)]
    pallas_call x0 -> x2, Pallas kernels: none -> 70.2 us  [the longest x1 48.9 us: scan_backward(): pl.pallas_call(backward_kernel, grid=(seqs, steps), in_specs=[pl.BlockSpe...]
    reduce_scatter x4 -> x5, waiting for transfers between devices: 175 us -> 221 us  [the longest x1 70.1 us: body(): lax.psum_scatter(jnp.dot(mixed, out_own, preferred_element_type=F32).asty...]
  transfers between devices with their start and end apart: 21 -> 12, of which waited for: 15 -> 11; matrix products, arithmetic and copies ran while one was open for 22% -> 15% of each run, Pallas kernels for 0% -> 2%
where the time goes in v1:
time: 884 us; the launch traced here: 878 us
  waiting for transfers between devices  562 us (64%)
  matrix products  103 us (12%)
  Pallas kernels  70.2 us (8%)
  local copies, waits for them, and re-layouts  55.5 us (6%)
  blocking collectives  41.7 us (5%)
  other arithmetic  25 us (3%)
  between operations  15.7 us (2%)
    unnamed x12, waiting for transfers between devices  131 us
    all_gather x1, waiting for transfers between devices, body(): w_own = lax.all_gather(plane_rows, 'z', axis=0, tiled=True)  86.3 us
    reduce_scatter x1, waiting for transfers between devices, body(): lax.psum_scatter(jnp.dot(mixed, out_own, preferred_element_type=F32).asty...  70.1 us
    reduce_scatter x1, waiting for transfers between devices, body(): lax.psum_scatter(normed_part.astype(BF16), GROUP, scatter_dimension=0, ti...  57.5 us
    all_gather x1, waiting for transfers between devices, body(): normed_all = lax.all_gather(normed, GROUP, axis=0, tiled=True)  55.7 us
    all_gather x1, waiting for transfers between devices, body(): grad_all = lax.all_gather(branch_grad, GROUP, axis=0, tiled=True)  55.3 us
    pallas_call x1, Pallas kernels, scan_backward(): pl.pallas_call(backward_kernel, grid=(seqs, steps), in_specs=[pl.BlockSpe...  48.9 us
    reduce_scatter x1, waiting for transfers between devices, body(): lax.psum_scatter(out_part, 'z', scatter_dimension=0, tiled=True).astype(F32)  37.6 us
  transfers between devices with their start and end apart: 12, of which 11 were waited for; matrix products, arithmetic and copies ran while one was open for 15% of the time, Pallas kernels for 2%

profile of v1, /device:TPU:1, one launch (start us, length us, event | category | flops | bytes accessed | tf_op | source)
XLA Modules:
  0.0 878.5 jit_solution(2817350856492601788)
XLA Ops:
  7.2 3.4 copy.110
  16.0 21.2 %all_to_all.29 = bf16[64,8,1064]{2,0,1:T(8,128)(2,1)} all-to-all(bf16[64,8,1064]{2,0,1:T(8,128)(2,1)S(1)} %concatenate.24), channel_id=1, replica_groups=mesh['z'=4,'y'=2,'seq'=4] {'y','seq'}, dimensions={1} | all-to-all | bytes 2179072 | tf_op jit(solution)/shard_map/all_to_all | solution.py:386
  40.1 86.3 %all-gather.9.cloned.1.call-done = bf16[2048,1064]{1,0:T(8,128)(2,1)} async-done(((bf16[512,1064]{1,0:T(8,128)(2,1)}), bf16[2048,1064]{1,0:T(8,128)(2,1)}) %all-gather.9.cloned.1.call-update) | async-done | bytes 4358160 | tf_op jit(solution)/shard_map/all_gather | solution.py:387
  126.4 55.7 %all-gather.7.cloned.1.call-done = bf16[2048,2048]{1,0:T(8,128)(2,1)} async-done(((bf16[256,2048]{1,0:T(8,128)(2,1)}), bf16[2048,2048]{1,0:T(8,128)(2,1)}) %all-gather.7.cloned.1.call-update) | async-done | bytes 8388624 | tf_op jit(solution)/shard_map/all_gather | solution.py:406
  182.1 6.2 convolution_convert_fusion.5
  194.2 14.0 %convolution_convert_fusion.1.x_ref.gate_ref.halo_ref = bf16[2048,1024]{1,0:T(8,128)(2,1)} fusion(bf16[2048,2048]{1,0:T(8,128)(2,1)} %all-gather.7.cloned.1.call-done, bf16[2048,1064]{1,0:T(8,128)(2,1)} %all-gather.9.cloned.1.call-done), kind=kOutput, calls=%fused_computation.18 | convolution fusion | flops 8592031744 | bytes 16777216 | tf_op jit(solution)/shard_map/dot_general | solution.py:407
  208.2 4.5 all-gather.11.cloned.1.call-done
  212.7 3.1 reshape.235
  215.9 6.6 pad_slice_fusion.2
  225.5 2.5 multiply_convert_fusion.1
  228.6 21.3 %scan_forward.1 = (f32[2048,512]{1,0:T(8,128)}, f32[8,128,512]{2,1,0:T(8,128)S(1)}) custom-call(bf16[2048,1024]{1,0:T(8,128)(2,1)} %convolution_convert_fusion.1.x_ref.gate_ref.halo_ref, bf16[2048,1024]{1,0:T(8,128)(2,1)} %convolution_convert_fusion.1.x_ref.gate_ref.halo_ref, bf16[2048,256]{1,0:T(8,128)(2,1)S(1)} %copy.121.bc_ref, ...), custom_call_target="tpu_custom_call" | custom-call | tf_op jit(solution)/shard_map/scan_forward/pallas_call | solution.py:246
  251.2 8.5 all-gather.15.cloned.1.call-done
  259.7 55.3 %all-gather.13.cloned.1.call-done = bf16[2048,2048]{1,0:T(8,128)(2,1)} async-done(((bf16[256,2048]{1,0:T(8,128)(2,1)}), bf16[2048,2048]{1,0:T(8,128)(2,1)}) %all-gather.13.cloned.1.call-update) | async-done | bytes 8388624 | tf_op jit(solution)/shard_map/all_gather | solution.py:421
  315.0 14.3 %multiply_reduce_fusion.1 = (f32[2048]{0:T(1024)S(1)}, f32[2048]{0:T(1024)S(1)}, f32[2048,512]{1,0:T(8,128)}, f32[2048,512]{1,0:T(8,128)}) fusion(f32[512]{0:T(512)S(1)} %bitcast.249, f32[2048,512]{1,0:T(8,128)} %get-tuple-element.18.scanned_ref, bf16[2048,1024]{1,0:T(8,128)(2,1)} %convolution_convert_fusion.1.x_ref.gate_ref.halo_ref, ...), kind=kOutput, calls=%fused_computation.17 | convolution fusion | flops 4306497536 | bytes 25184256 | tf_op jit(solution)/shard_map/dot_general | solution.py:422
  329.3 20.5 %psum.7 = f32[2,2048]{1,0:T(2,128)S(1)} all-reduce(f32[2,2048]{1,0:T(2,128)S(1)} %pad_maximum_fusion.6), channel_id=1, replica_groups=mesh['z'=4,'y'=2,'seq'=4] {'y','seq'}, use_global_device_ids=true, to_apply=%region_3.4 | all-reduce | flops 4096 | bytes 32768 | tf_op jit(solution)/shard_map/psum | solution.py:426
  350.6 48.9 %scan_backward.1 = (bf16[2048,1024]{1,0:T(8,128)(2,1)}, f32[256,2048]{1,0:T(8,128)}, bf16[8,2048]{1,0:T(8,128)(2,1)}, f32[8,512]{1,0:T(8,128)}, f32[8,128]{1,0:T(8,128)}) custom-call(bf16[2048,1024]{1,0:T(8,128)(2,1)} %convolution_convert_fusion.1.x_ref.gate_ref.halo_ref, bf16[2048,1024]{1,0:T(8,128)(2,1)} %convolution_convert_fusion.1.x_ref.gate_ref.halo_ref, ...), custom_call_target="tpu_custom_call" | custom-call | tf_op jit(solution)/shard_map/scan_backward/pallas_call | solution.py:277
  403.7 14.2 %convolution_convert_fusion.2 = bf16[2048,1024]{0,1:T(8,128)(2,1)} fusion(bf16[2048,2048]{1,0:T(8,128)(2,1)} %all-gather.7.cloned.1.call-done, bf16[2048,1024]{1,0:T(8,128)(2,1)} %get-tuple-element.20), kind=kOutput, calls=%fused_computation.19 | convolution fusion | flops 8592031744 | bytes 16777216 | tf_op jit(solution)/shard_map/dot_general | solution.py:463
  417.9 25.6 %reduce-scatter.8.cloned.1.call-done = f32[32,2048]{1,0:T(8,128)} async-done(((f32[256,2048]{1,0:T(8,128)}), f32[32,2048]{1,0:T(8,128)}) %reduce-scatter.8.cloned.1.call-update) | async-done | bytes 262160 | tf_op jit(solution)/shard_map/reduce_scatter | solution.py:450
  446.9 5.0 convolution_convert_fusion.4
  452.0 2.3 pad_maximum_fusion
  454.4 10.8 %convolution_convert_fusion.3 = bf16[512,2048]{1,0:T(8,128)(2,1)} fusion(bf16[2048,2048]{1,0:T(8,128)(2,1)} %all-gather.13.cloned.1.call-done, f32[2048,512]{1,0:T(8,128)} %get-tuple-element.37, f32[2048]{0:T(1024)S(1)} %bitcast.234, f32[512]{0:T(512)S(1)} %bitcast.250), kind=kOutput, calls=%fused_computation.23 | convolution fusion | flops 4299161600 | bytes 14690304 | tf_op jit(solution)/shard_map/dot_general | solution.py:438
  465.2 15.5 %fusion.4 = f32[2048,2048]{1,0:T(8,128)} fusion(bf16[2048,1024]{1,0:T(8,128)(2,1)} %get-tuple-element.20, bf16[2048,1064]{1,0:T(8,128)(2,1)} %all-gather.9.cloned.1.call-done), kind=kOutput, calls=%fused_computation.20 | convolution fusion | flops 8589934592 | bytes 25165824 | tf_op jit(solution)/shard_map/dot_general | solution.py:472
  480.7 11.7 %add_convert_fusion = bf16[2048,2048]{1,0:T(8,128)(2,1)} fusion(f32[2048,2048]{1,0:T(8,128)} %fusion.4, bf16[2048,1064]{1,0:T(8,128)(2,1)} %all-gather.9.cloned.1.call-done, bf16[8,2048]{1,0:T(8,128)(2,1)S(1)} %copy-done.23, bf16[32,2048]{1,0:T(8,128)(2,1)S(1)} %add_convert_fusion.1), kind=kOutput, calls=%fused_computation | convolution fusion | flops 344260608 | bytes 25853952 | tf_op jit(solution)/shard_map/dot_general | solution.py:474
  492.5 10.7 %convolution_convert_fusion = bf16[2048,2048]{1,0:T(8,128)(2,1)} fusion(bf16[512,2048]{1,0:T(8,128)(2,1)} %all-gather.15.cloned.1.call-done, f32[2048,512]{1,0:T(8,128)} %get-tuple-element.37, f32[2048]{0:T(1024)S(1)} %bitcast.235, f32[512]{0:T(512)S(1)} %bitcast.251), kind=kOutput, calls=%fused_computation.1 | convolution fusion | flops 4302307328 | bytes 14690304 | tf_op jit(solution)/shard_map/dot_general | solution.py:434
  503.3 30.7 %reduce-scatter.12.cloned.1.call-done = bf16[512,1064]{0,1:T(8,128)(2,1)} async-done(((bf16[2048,1064]{0,1:T(8,128)(2,1)}), bf16[512,1064]{0,1:T(8,128)(2,1)}) %reduce-scatter.12.cloned.1.call-update) | async-done | bytes 1089552 | tf_op jit(solution)/shard_map/reduce_scatter | solution.py:468
  533.9 2.4 copy.129
  536.3 4.8 all-to-all-start.1
  543.4 37.6 %reduce-scatter.14.cloned.1.call-done = bf16[128,2048]{1,0:T(8,128)(2,1)} async-done(((bf16[512,2048]{1,0:T(8,128)(2,1)}), bf16[128,2048]{1,0:T(8,128)(2,1)}) %reduce-scatter.14.cloned.1.call-update) | async-done | bytes 524304 | tf_op jit(solution)/shard_map/reduce_scatter | solution.py:442
  598.1 57.5 %reduce-scatter.10.cloned.1.call-done = bf16[256,2048]{1,0:T(8,128)(2,1)} async-done(((bf16[2048,2048]{1,0:T(8,128)(2,1)}), bf16[256,2048]{1,0:T(8,128)(2,1)}) %reduce-scatter.10.cloned.1.call-update) | async-done | bytes 1048592 | tf_op jit(solution)/shard_map/reduce_scatter | solution.py:475
  660.2 70.1 %reduce-scatter.6.cloned.1.call-done = bf16[256,2048]{1,0:T(8,128)(2,1)} async-done(((bf16[2048,2048]{1,0:T(8,128)(2,1)}), bf16[256,2048]{1,0:T(8,128)(2,1)}) %reduce-scatter.6.cloned.1.call-update) | async-done | bytes 1048592 | tf_op jit(solution)/shard_map/reduce_scatter | solution.py:433
  730.3 3.8 fusion.10
  734.1 130.5 %all-reduce.12.cloned.1.call-done = f32[169728]{0:T(1024)} async-done(((f32[169728]{0:T(1024)}), f32[169728]{0:T(1024)}) %all-reduce.12.cloned.1.call-update) | async-done | bytes 678928
  (234 shorter events, 57.3 us)
Async XLA Ops:
  7.2 186.2 %copy-start = (f32[4096]{0:T(1024)S(1)}, f32[4096]{0:T(1024)}, u32[]{:S(2)}) copy-start(f32[4096]{0:T(1024)} %param.22) | copy-start | bytes 49156
  7.2 119.2 %all-gather.9.cloned.1.call-start = ((), (), s32[]{:S(2)}) async-start(), calls=%async_computation.8 | async-start | bytes 5898240 | tf_op jit(solution)/shard_map/all_gather | solution.py:387
  37.2 144.9 %all-gather.7.cloned.1.call-start = ((), (), s32[]{:S(2)}) async-start(), calls=%async_computation.7 | async-start | bytes 9437184 | tf_op jit(solution)/shard_map/all_gather | solution.py:406
  40.1 149.1 %copy-start.21 = (f32[128,2048]{1,0:T(8,128)S(1)}, f32[128,2048]{1,0:T(8,128)}, u32[]{:S(2)}) copy-start(f32[128,2048]{1,0:T(8,128)} %param.23) | copy-start | bytes 3145732
  40.1 172.7 %all-gather.11.cloned.1.call-start = ((), (), s32[]{:S(2)}) async-start(), calls=%async_computation.9 | async-start | bytes 1179648 | tf_op jit(solution)/shard_map/all_gather | solution.py:412
  189.1 70.6 %all-gather.15.cloned.1.call-start = ((), (), s32[]{:S(2)}) async-start(), calls=%async_computation.11 | async-start | bytes 2621440 | tf_op jit(solution)/shard_map/all_gather | solution.py:390
  190.0 124.9 %all-gather.13.cloned.1.call-start = ((), (), s32[]{:S(2)}) async-start(), calls=%async_computation.10 | async-start | bytes 9437184 | tf_op jit(solution)/shard_map/all_gather | solution.py:421
  192.0 251.5 %reduce-scatter.8.cloned.1.call-start = ((), (), s32[]{:S(2)}) async-start(), calls=%async_computation.13 | async-start | bytes 2359296 | tf_op jit(solution)/shard_map/reduce_scatter | solution.py:450
  193.2 35.3 %copy-start.9 = (f32[1,512]{1,0:T(1,128)}, f32[1,512]{1,0:T(1,128)S(1)}, u32[]{:S(2)}) copy-start(f32[1,512]{1,0:T(1,128)S(1)} %broadcast_in_dim.7.skip_ref) | copy-start | bytes 6148
  194.1 34.5 %copy-start.10 = (f32[1,512]{1,0:T(1,128)}, f32[1,512]{1,0:T(1,128)S(1)}, u32[]{:S(2)}) copy-start(f32[1,512]{1,0:T(1,128)S(1)} %fusion.26.bx_ref) | copy-start | bytes 6148
  194.1 34.5 %copy-start.6 = (f32[4,512]{1,0:T(4,128)}, f32[4,512]{1,0:T(4,128)S(1)}, u32[]{:S(2)}) copy-start(f32[4,512]{1,0:T(4,128)S(1)} %dynamic-slice_bitcast_fusion.wx_ref) | copy-start | bytes 24580
  350.6 49.0 %slice-start.1 = ((f32[4352,4]{0,1:T(4,128)}), f32[256,4]{0,1:T(4,128)S(1)}, s32[]{:S(2)}) async-start(f32[4352,4]{0,1:T(4,128)} %param.17), calls=%async_computation.19 | async-start | bytes 8192 | tf_op jit(solution)/shard_map/slice | solution.py:452
  399.5 134.4 %reduce-scatter.12.cloned.1.call-start = ((), (), s32[]{:S(2)}) async-start(), calls=%async_computation.15 | async-start | bytes 5447680 | tf_op jit(solution)/shard_map/reduce_scatter | solution.py:468
  454.3 126.7 %reduce-scatter.14.cloned.1.call-start = ((), (), s32[]{:S(2)}) async-start(), calls=%async_computation.16 | async-start | bytes 2621440 | tf_op jit(solution)/shard_map/reduce_scatter | solution.py:442
  465.1 190.5 %reduce-scatter.10.cloned.1.call-start = ((), (), s32[]{:S(2)}) async-start(), calls=%async_computation.14 | async-start | bytes 9437184 | tf_op jit(solution)/shard_map/reduce_scatter | solution.py:475
  492.5 237.8 %reduce-scatter.6.cloned.1.call-start = ((), (), s32[]{:S(2)}) async-start(), calls=%async_computation.12 | async-start | bytes 9437184 | tf_op jit(solution)/shard_map/reduce_scatter | solution.py:433
  503.3 38.1 %copy-start.27 = (f32[8,512]{1,0:T(8,128)S(1)}, f32[8,512]{1,0:T(8,128)}, u32[]{:S(2)}) copy-start(f32[8,512]{1,0:T(8,128)} %get-tuple-element.23) | copy-start | bytes 49156
  503.3 38.8 %copy-start.30 = (f32[8,128]{1,0:T(8,128)S(1)}, f32[8,128]{1,0:T(8,128)}, u32[]{:S(2)}) copy-start(f32[8,128]{1,0:T(8,128)} %get-tuple-element.24) | copy-start | bytes 12292
  536.3 46.8 %all-to-all-start.1 = ((bf16[8,64,1064]{2,1,0:T(8,128)(2,1)}), bf16[8,64,1064]{2,1,0:T(8,128)(2,1)}, u32[]{:S(2)}, u32[]{:S(2)}) async-start(bf16[8,64,1064]{2,1,0:T(8,128)(2,1)} %bitcast.54), calls=%async_computation.5 | async-start | bytes 2359296 | tf_op jit(solution)/shard_map/all_to_all | solution.py:469
  541.0 323.5 %all-reduce.12.cloned.1.call-start = ((), (), s32[]{:S(2)}) async-start(), calls=%async_computation.17 | async-start | bytes 1359872
  596.6 59.1 %copy-start.26 = (f32[2048]{0:T(1024)S(1)}, f32[2048]{0:T(1024)}, u32[]{:S(2)}) copy-start(f32[2048]{0:T(1024)} %param.15) | copy-start | bytes 24580
  596.6 59.1 %copy-start.29 = (f32[256]{0:T(256)S(1)}, f32[256]{0:T(256)}, u32[]{:S(2)}) copy-start(f32[256]{0:T(256)} %copy-done.28) | copy-start | bytes 3076
  596.6 61.0 %copy-start.36 = (f32[8]{0:T(128)S(1)}, f32[8]{0:T(128)}, u32[]{:S(2)}) copy-start(f32[8]{0:T(128)} %reduce_sum.121) | copy-start | bytes 100
  596.6 61.0 %copy-start.37 = (f32[8]{0:T(128)S(1)}, f32[8]{0:T(128)}, u32[]{:S(2)}) copy-start(f32[8]{0:T(128)} %get-tuple-element.34) | copy-start | bytes 100
  596.6 61.0 %copy-start.38 = (f32[8]{0:T(128)S(1)}, f32[8]{0:T(128)}, u32[]{:S(2)}) copy-start(f32[8]{0:T(128)} %get-tuple-element.35) | copy-start | bytes 100
  596.6 61.0 %copy-start.39 = (f32[128]{0:T(128)S(1)}, f32[128]{0:T(128)}, u32[]{:S(2)}) copy-start(f32[128]{0:T(128)} %reshape.257) | copy-start | bytes 1540
  596.6 61.0 %copy-start.40 = (f32[32]{0:T(128)S(1)}, f32[32]{0:T(128)}, u32[]{:S(2)}) copy-start(f32[32]{0:T(128)} %get-tuple-element.29) | copy-start | bytes 388
  598.1 62.0 %copy-start.35 = (f32[256]{0:T(256)S(1)}, f32[256]{0:T(256)}, u32[]{:S(2)}) copy-start(f32[256]{0:T(256)} %copy-done.34) | copy-start | bytes 3076
  598.1 132.1 %copy-start.17 = (bf16[1,256,2048]{2,1,0:T(8,128)(2,1)S(1)}, bf16[1,256,2048]{2,1,0:T(8,128)(2,1)}, u32[]{:S(2)}) copy-start(bf16[1,256,2048]{2,1,0:T(8,128)(2,1)} %param.13) | copy-start | bytes 3145732
  598.1 132.1 %copy-start.33 = (f32[256]{0:T(256)S(1)}, f32[256]{0:T(256)}, u32[]{:S(2)}) copy-start(f32[256]{0:T(256)} %copy-done.32) | copy-start | bytes 3076
  655.7 74.6 %copy-start.15 = (bf16[256,2048]{1,0:T(8,128)(2,1)S(1)}, bf16[256,2048]{1,0:T(8,128)(2,1)}, u32[]{:S(2)}) copy-start(bf16[256,2048]{1,0:T(8,128)(2,1)} %reduce-scatter.10.cloned.1.call-done) | copy-start | bytes 3145732
  730.2 141.4 %copy-start.1 = (f32[4096]{0:T(1024)S(1)}, f32[4096]{0:T(1024)}, u32[]{:S(2)}) copy-start(f32[4096]{0:T(1024)} %param.22) | copy-start | bytes 49156
  (27 other events, 244.5 us)
Sparse Core Ops, SparseCore 0:
  37.3 89.0 all-gather.8
  128.9 53.1 all-gather.6
  189.2 23.4 all-gather.10
  214.1 45.4 all-gather.14
  261.4 53.5 all-gather.12
  399.7 43.7 reduce-scatter.7
  454.4 79.4 reduce-scatter.11
  536.8 44.1 reduce-scatter.13
  584.9 70.7 reduce-scatter.9
  659.0 71.2 reduce-scatter.5
  736.3 128.1 all-reduce.11

commit v2 on v1

--- a/solution.py
+++ b/solution.py
@@ -68,6 +68,382 @@
     for k in range(KERNEL):
         total = total + conv_w[k : k + 1] * shifted[k]
     return total, shifted
+
+
+MESH = pl.DeviceIdType.MESH
+
+
+def remote(src, dst, send_sem, recv_sem, device):
+    return pltpu.make_async_remote_copy(
+        src_ref=src, dst_ref=dst, send_sem=send_sem, recv_sem=recv_sem,
+        device_id=device, device_id_type=MESH,
+    )
+
+
+class Place:
+    def __init__(self, planes, ny, ns):
+        self.planes, self.ny, self.ns, self.group = planes, ny, ns, ny * ns
+        self.z, self.y, self.s = lax.axis_index("z"), lax.axis_index("y"), lax.axis_index("seq")
+        self.rank = self.y * ns + self.s
+        self.up, self.down = (self.z + 1, self.y, self.s), (self.z - 1, self.y, self.s)
+        self.has_up, self.has_down = self.z < planes - 1, self.z > 0
+
+    def member(self, rank):
+        return (self.z, rank // self.ns, lax.rem(rank, self.ns))
+
+    def peer(self, i):
+        return lax.rem(self.rank + i, self.group)
+
+    def far(self):
+        chips = self.ns // 2
+        x, core = self.s // 2, lax.rem(self.s, 2)
+        for dy in range(self.ny):
+            for dx in range(chips):
+                if dy or dx:
+                    yield lax.rem(self.y + dy, self.ny) * self.ns + lax.rem(x + dx, chips) * 2 + core
+
+    def sibling(self, rank):
+        return rank + 1 - 2 * lax.rem(rank, 2)
+
+    def greet(self):
+        barrier = pltpu.get_barrier_semaphore()
+        for i in range(1, self.group):
+            pl.semaphore_signal(barrier, inc=1, device_id=self.member(self.peer(i)), device_id_type=MESH)
+
+        @pl.when(self.has_up)
+        def _():
+            pl.semaphore_signal(barrier, inc=1, device_id=self.up, device_id_type=MESH)
+
+        @pl.when(self.has_down)
+        def _():
+            pl.semaphore_signal(barrier, inc=1, device_id=self.down, device_id_type=MESH)
+
+        count = self.group - 1 + self.has_up.astype(jnp.int32) + self.has_down.astype(jnp.int32)
+        pl.semaphore_wait(barrier, count)
+
+
+def project_kernel(
+    planes, ny, ns, cut, heads,
+    pm_ref, ps_ref, nm_ref,
+    proj_ref, bct_ref, dt_ref, nall_ref, wm_ref, ws_ref,
+    wmain, wsmall, normed, acc, outb, bcb,
+    am_send, am_recv, as_send, as_recv, n_send, n_recv, f_send, b_send, b_recv,
+    up_send, up_recv, down_send, down_recv, sup_send, sup_recv, sdown_send, sdown_recv, local_sem,
+):
+    at = Place(planes, ny, ns)
+    group, rank, z = at.group, at.rank, at.z
+    piece = pm_ref.shape[1]
+    plane_rows = piece * group
+    total, slab = normed.shape[0], 256
+    own_rows = nm_ref.shape[0]
+    small = bcb.shape[0] // group
+    part = plane_rows // cut
+
+    def rows_of(r):
+        return pl.ds(pl.multiple_of(z * plane_rows + r * piece, piece), piece)
+
+    def block_rows(p, q):
+        return pl.ds(pl.multiple_of(p * plane_rows + q * part, part), part)
+
+    def plane_block(p):
+        return pl.ds(pl.multiple_of(p * plane_rows, plane_rows), plane_rows)
+
+    def norm_rows(r):
+        return pl.ds(pl.multiple_of(r * own_rows, own_rows), own_rows)
+
+    own_copies = [
+        pltpu.make_async_copy(pm_ref.at[rank], wmain.at[rows_of(rank)], local_sem.at[0]),
+        pltpu.make_async_copy(ps_ref.at[rank], wsmall.at[rows_of(rank)], local_sem.at[1]),
+        pltpu.make_async_copy(nm_ref, normed.at[norm_rows(rank)], local_sem.at[2]),
+    ]
+    for copy in own_copies:
+        copy.start()
+    at.greet()
+
+    def main_piece(r, i):
+        return remote(pm_ref.at[r], wmain.at[rows_of(rank)], am_send.at[i], am_recv.at[rank], at.member(r))
+
+    def small_piece(r, i):
+        return remote(ps_ref.at[r], wsmall.at[rows_of(rank)], as_send.at[i], as_recv.at[rank], at.member(r))
+
+    def norm_piece(r, i):
+        return remote(nm_ref, normed.at[norm_rows(rank)], n_send.at[i], n_recv.at[rank], at.member(r))
+
+    for i in range(1, group):
+        small_piece(at.peer(i), i).start()
+    for i in range(1, group):
+        main_piece(at.peer(i), i).start()
+    far = list(at.far())
+    sibling = at.sibling(rank)
+    norm_piece(sibling, 0).start()
+    for i, r in enumerate(far):
+        norm_piece(r, i + 1).start()
+    acc[...] = jnp.zeros_like(acc)
+    for copy in own_copies:
+        copy.wait()
+
+    for i in range(1, group):
+        r = at.peer(i)
+        remote(ps_ref.at[r], wsmall.at[rows_of(r)], as_send.at[i], as_recv.at[r], at.member(r)).wait_recv()
+
+    def small_up(p, j):
+        return remote(wsmall.at[plane_block(p)], wsmall.at[plane_block(p)], sup_send.at[j], sup_recv.at[j], at.up)
+
+    def small_down(p, j):
+        return remote(wsmall.at[plane_block(p)], wsmall.at[plane_block(p)], sdown_send.at[j], sdown_recv.at[j], at.down)
+
+    def wide_up(p, q, k):
+        return remote(wmain.at[block_rows(p, q)], wmain.at[block_rows(p, q)], up_send.at[k], up_recv.at[k], at.up)
+
+    def wide_down(p, q, k):
+        return remote(wmain.at[block_rows(p, q)], wmain.at[block_rows(p, q)], down_send.at[k], down_recv.at[k], at.down)
+
+    def each_way(p, above, fn_up, fn_down):
+        @pl.when(at.has_up & jnp.logical_not(above))
+        def _():
+            fn_up()
+
+        @pl.when(at.has_down & above)
+        def _():
+            fn_down()
+
+    @pl.when(at.has_up)
+    def _():
+        small_up(z, 0).start()
+
+    @pl.when(at.has_down)
+    def _():
+        small_down(z, 0).start()
+
+    ranks_in = group // cut
+    for q in range(cut):
+        for r in range(q * ranks_in, (q + 1) * ranks_in):
+            @pl.when(rank != r)
+            def _():
+                remote(pm_ref.at[r], wmain.at[rows_of(r)], am_send.at[0], am_recv.at[r], at.member(r)).wait_recv()
+
+        @pl.when(at.has_up)
+        def _():
+            wide_up(z, q, q).start()
+
+        @pl.when(at.has_down)
+        def _():
+            wide_down(z, q, q).start()
+
+    def small_step(j, _):
+        @pl.when(z + j < planes)
+        def _():
+            small_down(z + j, j - 1).wait_recv()
+
+            @pl.when(at.has_down)
+            def _():
+                small_down(z + j, j).start()
+
+        @pl.when(z - j >= 0)
+        def _():
+            small_up(z - j, j - 1).wait_recv()
+
+            @pl.when(at.has_up)
+            def _():
+                small_up(z - j, j).start()
+
+        return 0
+
+    lax.fori_loop(1, planes, small_step, 0)
+
+    def relay(i, r):
+        norm_piece_in = remote(nm_ref, normed.at[norm_rows(r)], n_send.at[i + 1], n_recv.at[r], at.member(r))
+        norm_piece_in.wait_recv()
+        remote(normed.at[norm_rows(r)], normed.at[norm_rows(r)], f_send.at[i], n_recv.at[r], at.member(sibling)).start()
+
+    def norm_done():
+        for r in [sibling] + [at.sibling(r) for r in far]:
+            remote(nm_ref, normed.at[norm_rows(r)], n_send.at[0], n_recv.at[r], at.member(sibling)).wait_recv()
+
+    def plane_in_turn(j):
+        return lax.rem(jnp.where(2 * z < planes, z + j, z - j + planes), planes)
+
+    slabs = total // slab
+
+    def product(index):
+        j, m = index // slabs, lax.rem(index, slabs)
+        p = plane_in_turn(j)
+        rows = pl.ds(pl.multiple_of(m * slab, slab), slab)
+        lanes = pl.ds(pl.multiple_of(p * plane_rows, 128), plane_rows)
+        return rows, acc[rows, :] + jnp.dot(
+            normed[rows, lanes], wmain[plane_block(p), :], preferred_element_type=F32
+        )
+
+    def narrow(m, _):
+        rows = pl.ds(pl.multiple_of(m * slab, slab), slab)
+        value = jnp.dot(normed[rows, :], wsmall[...], preferred_element_type=F32).T
+        bcb[pl.ds(pl.multiple_of(rank * small, small), small), rows] = value[:small].astype(BF16)
+        dt_ref[:, rows] = value[small : small + heads].astype(BF16).astype(F32)
+        return 0
+
+    def bc_piece(r, i, owner):
+        rows = pl.ds(pl.multiple_of(owner * small, small), small)
+        return remote(bcb.at[rows], bcb.at[rows], b_send.at[i], b_recv.at[owner], at.member(r))
+
+    steps = (planes - 1) * cut
+    busy = (planes - 2) * cut
+    per_step = -(-(planes - 1) * slabs // cut)
+
+    def wide_step(k, _):
+        j, q = k // cut + 1, lax.rem(k, cut)
+
+        @pl.when(z + j < planes)
+        def _():
+            wide_down(z + j, q, k).wait_recv()
+
+            @pl.when(at.has_down)
+            def _():
+                wide_down(z + j, q, k + cut).start()
+
+        @pl.when(z - j >= 0)
+        def _():
+            wide_up(z - j, q, k).wait_recv()
+
+            @pl.when(at.has_up)
+            def _():
+                wide_up(z - j, q, k + cut).start()
+
+        return 0
+
+    marks = [cut + i * max(busy - cut, 0) // len(far) for i in range(len(far))]
+    last = 0
+    for i, r in enumerate(far):
+        lax.fori_loop(last, marks[i], wide_step, 0)
+        last = marks[i]
+        relay(i, r)
+    lax.fori_loop(last, busy, wide_step, 0)
+    norm_done()
+    lax.fori_loop(0, slabs, narrow, 0)
+    for i in range(1, group):
+        bc_piece(at.peer(i), i, rank).start()
+    nall_copy = pltpu.make_async_copy(normed, nall_ref, local_sem.at[0])
+    nall_copy.start()
+    ws_copy = pltpu.make_async_copy(wsmall, ws_ref, local_sem.at[1])
+    ws_copy.start()
+
+    def busy_step(k, _):
+        wide_step(k, 0)
+
+        def one(i, _):
+            rows, value = product(jnp.minimum((k - busy) * per_step + i, (planes - 1) * slabs))
+
+            @pl.when((k - busy) * per_step + i < (planes - 1) * slabs)
+            def _():
+                acc[rows, :] = value
+
+            return 0
+
+        lax.fori_loop(0, per_step, one, 0)
+        return 0
+
+    lax.fori_loop(busy, steps, busy_step, 0)
+    wm_copy = pltpu.make_async_copy(wmain, wm_ref, local_sem.at[2])
+    wm_copy.start()
+
+    def out_copy(m):
+        rows = pl.ds(pl.multiple_of(m * slab, slab), slab)
+        return pltpu.make_async_copy(outb.at[rows], proj_ref.at[rows], local_sem.at[4 + m])
+
+    def final(m, _):
+        rows, value = product((planes - 1) * slabs + m)
+        outb[rows, :] = value.astype(BF16)
+        out_copy(m).start()
+        return 0
+
+    lax.fori_loop(0, slabs, final, 0)
+
+    for i in range(1, group):
+        r = at.peer(i)
+        bc_piece(r, i, r).wait_recv()
+    bct_copy = pltpu.make_async_copy(bcb, bct_ref, local_sem.at[3])
+    bct_copy.start()
+    for i in range(1, group):
+        r = at.peer(i)
+        main_piece(r, i).wait_send()
+        small_piece(r, i).wait_send()
+        bc_piece(r, i, rank).wait_send()
+    norm_piece(sibling, 0).wait_send()
+    for i, r in enumerate(far):
+        norm_piece(r, i + 1).wait_send()
+        remote(normed.at[norm_rows(r)], normed.at[norm_rows(r)], f_send.at[i], n_recv.at[r], at.member(sibling)).wait_send()
+
+    def small_sent(j, _):
+        @pl.when((z + j < planes) & at.has_down)
+        def _():
+            small_down(z + j, j).wait_send()
+
+        @pl.when((z - j >= 0) & at.has_up)
+        def _():
+            small_up(z - j, j).wait_send()
+
+        return 0
+
+    lax.fori_loop(0, planes, small_sent, 0)
+
+    def wide_sent(k, _):
+        j, q = k // cut, lax.rem(k, cut)
+
+        @pl.when((z + j < planes) & at.has_down)
+        def _():
+            wide_down(z + j, q, k).wait_send()
+
+        @pl.when((z - j >= 0) & at.has_up)
+        def _():
+            wide_up(z - j, q, k).wait_send()
+
+        return 0
+
+    lax.fori_loop(0, planes * cut, wide_sent, 0)
+    nall_copy.wait()
+    ws_copy.wait()
+    wm_copy.wait()
+    bct_copy.wait()
+    lax.fori_loop(0, slabs, lambda m, _: (out_copy(m).wait(), 0)[1], 0)
+
+
+def gather_project(pieces, pieces_small, normed, planes, ny, ns, heads):
+    group, rows, width = pieces.shape
+    total = normed.shape[0] * group
+    cut = 1
+    while cut * 2 <= min(group, 32 // planes):
+        cut *= 2
+    dma = pltpu.SemaphoreType.DMA
+    anywhere = pl.BlockSpec(memory_space=pl.ANY)
+    return pl.pallas_call(
+        functools.partial(project_kernel, planes, ny, ns, cut, heads),
+        in_specs=[anywhere] * 3,
+        out_specs=[anywhere, anywhere, pl.BlockSpec(memory_space=pltpu.VMEM), anywhere, anywhere, anywhere],
+        out_shape=[
+            jax.ShapeDtypeStruct((total, width), BF16),
+            jax.ShapeDtypeStruct((2 * STATE, total), BF16),
+            jax.ShapeDtypeStruct((heads, total), F32),
+            jax.ShapeDtypeStruct((total, D), BF16),
+            jax.ShapeDtypeStruct((D, width), BF16),
+            jax.ShapeDtypeStruct((D, 128), BF16),
+        ],
+        scratch_shapes=[
+            pltpu.VMEM((D, width), BF16),
+            pltpu.VMEM((D, 128), BF16),
+            pltpu.VMEM((total, D), BF16),
+            pltpu.VMEM((total, width), F32),
+            pltpu.VMEM((total, width), BF16),
+            pltpu.VMEM((2 * STATE, total), BF16),
+            dma((group,)), dma((group,)), dma((group,)), dma((group,)),
+            dma((group,)), dma((group,)), dma((group,)), dma((group,)), dma((group,)),
+            dma((planes * cut,)), dma((planes * cut,)), dma((planes * cut,)), dma((planes * cut,)),
+            dma((planes,)), dma((planes,)), dma((planes,)), dma((planes,)),
+            dma((4 + total // 256,)),
+        ],
+        compiler_params=pltpu.CompilerParams(
+            collective_id=1, has_side_effects=True, vmem_limit_bytes=58 << 20
+        ),
+        name="gather_project",
+    )(pieces, pieces_small, normed)
 
 
 def forward_kernel(
@@ -382,10 +758,9 @@
     masked_cot = cotangent.reshape(row_count, D).astype(F32) * valid_mask
     branch_grad = masked_cot.astype(BF16)
 
-    pieces = lay.columns(w_in.astype(BF16)).reshape(w_in.shape[0], -1)
-    plane_rows = lax.all_to_all(pieces, GROUP, split_axis=1, concat_axis=0, tiled=True)
-    w_own = lax.all_gather(plane_rows, "z", axis=0, tiled=True)
-    w_main, w_small = w_own[:, : 2 * channels], w_own[:, 2 * channels :]
+    columns = lay.columns(w_in.astype(BF16)).transpose(1, 0, 2)
+    pieces = columns[:, :, : 2 * channels]
+    pieces_small = jnp.pad(columns[:, :, 2 * channels :], ((0, 0), (0, 0), (0, 128 - small - lay.heads)))
     if lay.aligned:
         out_own = lax.all_gather(w_out.astype(BF16), "z", axis=0, tiled=True)
     else:
@@ -403,13 +778,11 @@
     gain_own = own(gate_gain[None], HEADDIM)
     params = (conv_wx, conv_bx, bias_own, a_own, skip_own)
 
-    normed_all = lax.all_gather(normed, GROUP, axis=0, tiled=True)
-    projected = jnp.dot(normed_all, w_main, preferred_element_type=F32).astype(BF16)
-    small_t = lax.dot_general(
-        w_small, normed_all, (((0,), (1,)), ((), ())), preferred_element_type=F32
-    ).astype(BF16)
-    dt_t = small_t[small:].astype(F32)
-    bc_in = lax.all_gather(small_t[:small], GROUP, axis=0, tiled=True).astype(F32)
+    projected, bc_raw, dt_t, normed_all, w_main, w_small = gather_project(
+        pieces, pieces_small, normed, planes, lax.axis_size("y"), lax.axis_size("seq"), lay.heads
+    )
+    w_small = w_small[:, : small + lay.heads]
+    bc_in = bc_raw.astype(F32)
     conv_bc = conv_b[INNER:, None]
     for k in range(KERNEL):
         conv_bc = conv_bc + conv_w[INNER:, k : k + 1] * shift_later(bc_in, KERNEL - 1 - k, seqs)

time: 884 us -> 750 us (0.85)
  waiting for transfers between devices: 562 us -> 348 us
  Pallas kernels: 70.2 us -> 190 us
  blocking collectives: 41.7 us -> 20.1 us
  matrix products: 103 us -> 82.2 us
    all_gather x3 -> x0, waiting for transfers between devices: 146 us -> none  [the longest x1 86.3 us: body(): w_own = lax.all_gather(plane_rows, 'z', axis=0, tiled=True)]
    pallas_call x0 -> x1, Pallas kernels: none -> 120 us  [gather_project(): pl.pallas_call(functools.partial(project_kernel, planes, ny, ns, cut, hea...]
    all_gather x1, waiting for transfers between devices: 55.3 us -> 0.01 us  [body(): grad_all = lax.all_gather(branch_grad, GROUP, axis=0, tiled=True)]
    all_to_all x1 -> x0, blocking collectives: 21.2 us -> none  [body(): lax.all_to_all(pieces, GROUP, split_axis=1, concat_axis=0, tiled=True)]
    dot_general x2 -> x0, matrix products: 20.3 us -> none  [the longest x1 14 us: body(): jnp.dot(normed_all, w_main, preferred_element_type=F32).astype(BF16)]
    unnamed x12 -> x9, waiting for transfers between devices: 131 us -> 131 us
  transfers between devices with their start and end apart: 12 -> 9, of which waited for: 11 -> 6; matrix products, arithmetic and copies ran while one was open for 15% -> 17% of each run, Pallas kernels for 2% -> 19%
where the time goes in v2:
time: 750 us; the launch traced here: 746 us
  waiting for transfers between devices  348 us (46%)
  Pallas kernels  190 us (25%)
  matrix products  82.2 us (11%)
  local copies, waits for them, and re-layouts  55.8 us (7%)
  other arithmetic  27.6 us (4%)
  blocking collectives  20.1 us (3%)
  between operations  15.9 us (2%)
    unnamed x9, waiting for transfers between devices  131 us
    pallas_call x1, Pallas kernels, gather_project(): pl.pallas_call(functools.partial(project_kernel, planes, ny, ns, cut, hea...  120 us
    reduce_scatter x1, waiting for transfers between devices, body(): lax.psum_scatter(jnp.dot(mixed, out_own, preferred_element_type=F32).asty...  70.3 us
    reduce_scatter x1, waiting for transfers between devices, body(): lax.psum_scatter(normed_part.astype(BF16), GROUP, scatter_dimension=0, ti...  57.4 us
    pallas_call x1, Pallas kernels, scan_backward(): pl.pallas_call(backward_kernel, grid=(seqs, steps), in_specs=[pl.BlockSpe...  48.9 us
    reduce_scatter x1, waiting for transfers between devices, body(): lax.psum_scatter(out_part, 'z', scatter_dimension=0, tiled=True).astype(F32)  37.5 us
    reduce_scatter x1, waiting for transfers between devices, body(): in_rows = lax.psum_scatter(in_part, 'z', scatter_dimension=0, tiled=True)  31 us
    reduce_scatter x1, waiting for transfers between devices, body(): dbc = lax.psum_scatter(dbc_t, GROUP, scatter_dimension=0, tiled=True)  21.7 us
  transfers between devices with their start and end apart: 9, of which 6 were waited for; matrix products, arithmetic and copies ran while one was open for 17% of the time, Pallas kernels for 19%

profile of v2, /device:TPU:1, one launch (start us, length us, event | category | flops | bytes accessed | tf_op | source)
XLA Modules:
  0.0 745.5 jit_solution(1167253132069019435)
XLA Ops:
  7.3 2.1 convert_element_type.110
  11.9 3.4 copy.110
  25.3 120.0 %gather_project.1 = (bf16[2048,1024]{1,0:T(8,128)(2,1)}, bf16[256,2048]{1,0:T(8,128)(2,1)}, f32[8,2048]{1,0:T(8,128)}, bf16[2048,2048]{1,0:T(8,128)(2,1)}, bf16[...) custom-call(bf16[8,64,1024]{2,1,0:T(8,128)(2,1)} %slice.210.pm_ref, bf16[8,64,128]{2,1,0:T(8,128)(2,1)} %pad.40.ps_ref, ...), custom_call_target="tpu_custom_call" | custom-call | tf_op jit(solution)/shard_map/gather_project/pallas_call | solution.py:417
  145.4 3.1 reshape.230
  148.5 6.6 pad_slice_fusion.2
  158.2 2.5 multiply_convert_fusion.1
  161.5 21.2 %scan_forward.1 = (f32[2048,512]{1,0:T(8,128)}, f32[8,128,512]{2,1,0:T(8,128)S(1)}) custom-call(bf16[2048,1024]{1,0:T(8,128)(2,1)} %get-tuple-element.24.x_ref.gate_ref.halo_ref, bf16[2048,1024]{1,0:T(8,128)(2,1)} %get-tuple-element.24.x_ref.gate_ref.halo_ref, bf16[2048,256]{1,0:T(8,128)(2,1)S(1)} %copy.120.bc_ref, ...), custom_call_target="tpu_custom_call" | custom-call | tf_op jit(solution)/shard_map/scan_forward/pallas_call | solution.py:622
  184.7 14.3 %multiply_reduce_fusion.1 = (f32[2048]{0:T(1024)S(1)}, f32[2048]{0:T(1024)S(1)}, f32[2048,512]{1,0:T(8,128)}, f32[2048,512]{1,0:T(8,128)}) fusion(f32[512]{0:T(512)S(1)} %bitcast.247, f32[2048,512]{1,0:T(8,128)} %get-tuple-element.27.scanned_ref, bf16[2048,1024]{1,0:T(8,128)(2,1)} %get-tuple-element.24.x_ref.gate_ref.halo_ref, ...), kind=kOutput, calls=%fused_computation.17 | convolution fusion | flops 4306497536 | bytes 25184256 | tf_op jit(solution)/shard_map/dot_general | solution.py:795
  199.1 20.1 %psum.7 = f32[2,2048]{1,0:T(2,128)S(1)} all-reduce(f32[2,2048]{1,0:T(2,128)S(1)} %pad_maximum_fusion.6), channel_id=1, replica_groups=mesh['z'=4,'y'=2,'seq'=4] {'y','seq'}, use_global_device_ids=true, to_apply=%region_3.4 | all-reduce | flops 4096 | bytes 32768 | tf_op jit(solution)/shard_map/psum | solution.py:799
  219.9 48.9 %scan_backward.1 = (bf16[2048,1024]{1,0:T(8,128)(2,1)}, f32[256,2048]{1,0:T(8,128)}, bf16[8,2048]{1,0:T(8,128)(2,1)}, f32[8,512]{1,0:T(8,128)}, f32[8,128]{1,0:T(8,128)}) custom-call(bf16[2048,1024]{1,0:T(8,128)(2,1)} %get-tuple-element.24.x_ref.gate_ref.halo_ref, bf16[2048,1024]{1,0:T(8,128)(2,1)} %get-tuple-element.24.x_ref.gate_ref.halo_ref, ...), custom_call_target="tpu_custom_call" | custom-call | tf_op jit(solution)/shard_map/scan_backward/pallas_call | solution.py:653
  274.1 14.5 %convolution_convert_fusion.1 = bf16[2048,1024]{0,1:T(8,128)(2,1)} fusion(bf16[2048,2048]{1,0:T(8,128)(2,1)} %get-tuple-element.36, bf16[2048,1024]{1,0:T(8,128)(2,1)} %get-tuple-element.29), kind=kOutput, calls=%fused_computation.18 | convolution fusion | flops 8592031744 | bytes 16777216 | tf_op jit(solution)/shard_map/dot_general | solution.py:836
  288.6 21.7 %reduce-scatter.8.cloned.1.call-done = f32[32,2048]{1,0:T(8,128)} async-done(((f32[256,2048]{1,0:T(8,128)}), f32[32,2048]{1,0:T(8,128)}) %reduce-scatter.8.cloned.1.call-update) | async-done | bytes 262160 | tf_op jit(solution)/shard_map/reduce_scatter | solution.py:823
  310.3 1.9 fusion.26
  313.7 5.0 convolution_convert_fusion.3
  318.8 2.4 pad_maximum_fusion
  321.2 10.7 %convolution_convert_fusion.2 = bf16[512,2048]{1,0:T(8,128)(2,1)} fusion(bf16[2048,2048]{1,0:T(8,128)(2,1)} %all-gather.4.cloned.1.call-done, f32[2048,512]{1,0:T(8,128)} %get-tuple-element.49, f32[2048]{0:T(1024)S(1)} %bitcast.232, f32[512]{0:T(512)S(1)} %bitcast.248), kind=kOutput, calls=%fused_computation.19 | convolution fusion | flops 4299161600 | bytes 14690304 | tf_op jit(solution)/shard_map/dot_general | solution.py:811
  332.1 15.4 %fusion.32 = f32[2048,2048]{1,0:T(8,128)} fusion(bf16[2048,1024]{1,0:T(8,128)(2,1)} %get-tuple-element.29, bf16[2048,1024]{1,0:T(8,128)(2,1)} %get-tuple-element.30), kind=kOutput, calls=%fused_computation.106 | convolution fusion | flops 8589934592 | bytes 25165824 | tf_op jit(solution)/shard_map/dot_general | solution.py:845
  347.5 11.5 %add_convert_fusion = bf16[2048,2048]{1,0:T(8,128)(2,1)} fusion(f32[2048,2048]{1,0:T(8,128)} %fusion.32, bf16[2048,128]{1,0:T(8,128)(2,1)S(1)} %copy-done.20, bf16[8,2048]{1,0:T(8,128)(2,1)S(1)} %copy-done.22, bf16[32,2048]{1,0:T(8,128)(2,1)S(1)} %add_convert_fusion.1), kind=kOutput, calls=%fused_computation | convolution fusion | flops 344260608 | bytes 25853952 | tf_op jit(solution)/shard_map/dot_general | solution.py:847
  359.1 10.7 %convolution_convert_fusion = bf16[2048,2048]{1,0:T(8,128)(2,1)} fusion(bf16[512,2048]{1,0:T(8,128)(2,1)} %all-gather.6.cloned.1.call-done, f32[2048,512]{1,0:T(8,128)} %get-tuple-element.49, f32[2048]{0:T(1024)S(1)} %bitcast.233, f32[512]{0:T(512)S(1)} %bitcast.249), kind=kOutput, calls=%fused_computation.1 | convolution fusion | flops 4302307328 | bytes 14690304 | tf_op jit(solution)/shard_map/dot_general | solution.py:807
  369.8 31.0 %reduce-scatter.12.cloned.1.call-done = bf16[512,1064]{0,1:T(8,128)(2,1)} async-done(((bf16[2048,1064]{0,1:T(8,128)(2,1)}), bf16[512,1064]{0,1:T(8,128)(2,1)}) %reduce-scatter.12.cloned.1.call-update) | async-done | bytes 1089552 | tf_op jit(solution)/shard_map/reduce_scatter | solution.py:841
  400.8 2.4 copy.128
  403.2 4.8 all-to-all-start
  410.3 37.5 %reduce-scatter.14.cloned.1.call-done = bf16[128,2048]{1,0:T(8,128)(2,1)} async-done(((bf16[512,2048]{1,0:T(8,128)(2,1)}), bf16[128,2048]{1,0:T(8,128)(2,1)}) %reduce-scatter.14.cloned.1.call-update) | async-done | bytes 524304 | tf_op jit(solution)/shard_map/reduce_scatter | solution.py:815
  447.7 2.1 convert_element_type.123
  455.8 1.6 fusion.28
  460.2 1.8 reshape.255
  464.9 57.4 %reduce-scatter.10.cloned.1.call-done = bf16[256,2048]{1,0:T(8,128)(2,1)} async-done(((bf16[2048,2048]{1,0:T(8,128)(2,1)}), bf16[256,2048]{1,0:T(8,128)(2,1)}) %reduce-scatter.10.cloned.1.call-update) | async-done | bytes 1048592 | tf_op jit(solution)/shard_map/reduce_scatter | solution.py:848
  522.3 2.0 fusion.15
  526.8 70.3 %reduce-scatter.6.cloned.1.call-done = bf16[256,2048]{1,0:T(8,128)(2,1)} async-done(((bf16[2048,2048]{1,0:T(8,128)(2,1)}), bf16[256,2048]{1,0:T(8,128)(2,1)}) %reduce-scatter.6.cloned.1.call-update) | async-done | bytes 1048592 | tf_op jit(solution)/shard_map/reduce_scatter | solution.py:806
  597.1 3.8 fusion.7
  600.9 130.4 %all-reduce.13.cloned.1.call-done = f32[169728]{0:T(1024)} async-done(((f32[169728]{0:T(1024)}), f32[169728]{0:T(1024)}) %all-reduce.13.cloned.1.call-update) | async-done | bytes 678928
  731.3 1.6 reshape.268
  (222 shorter events, 46.8 us)
Async XLA Ops:
  7.2 176.9 %copy-start = (f32[4096]{0:T(1024)S(1)}, f32[4096]{0:T(1024)}, u32[]{:S(2)}) copy-start(f32[4096]{0:T(1024)} %param.22) | copy-start | bytes 49156
  7.2 177.5 %all-gather.6.cloned.1.call-start = ((), (), s32[]{:S(2)}) async-start(), calls=%async_computation.7 | async-start | bytes 2621440 | tf_op jit(solution)/shard_map/all_gather | solution.py:765
  9.4 175.3 %all-gather.4.cloned.1.call-start = ((), (), s32[]{:S(2)}) async-start(), calls=%async_computation.6 | async-start | bytes 9437184 | tf_op jit(solution)/shard_map/all_gather | solution.py:794
  11.9 298.4 %reduce-scatter.8.cloned.1.call-start = ((), (), s32[]{:S(2)}) async-start(), calls=%async_computation.9 | async-start | bytes 2359296 | tf_op jit(solution)/shard_map/reduce_scatter | solution.py:823
  22.9 138.5 %copy-start.9 = (f32[1,512]{1,0:T(1,128)}, f32[1,512]{1,0:T(1,128)S(1)}, u32[]{:S(2)}) copy-start(f32[1,512]{1,0:T(1,128)S(1)} %broadcast_in_dim.7.skip_ref) | copy-start | bytes 6148
  24.0 121.4 %copy-start.33 = (f32[256]{0:T(256)}, f32[256]{0:T(256)S(1)}, u32[]{:S(2)}) copy-start(f32[256]{0:T(256)S(1)} %fusion.8) | copy-start | bytes 3076
  24.0 121.3 %copy-start.27 = (f32[256]{0:T(256)}, f32[256]{0:T(256)S(1)}, u32[]{:S(2)}) copy-start(f32[256]{0:T(256)S(1)} %add_rsqrt_fusion) | copy-start | bytes 3076
  160.6 22.1 %copy-start.2 = (bf16[256,2048]{1,0:T(8,128)(2,1)}, bf16[256,2048]{1,0:T(8,128)(2,1)S(1)}, u32[]{:S(2)}) copy-start(bf16[256,2048]{1,0:T(8,128)(2,1)S(1)} %get-tuple-element.50.bct_ref) | copy-start | bytes 3145732
  161.2 21.6 %copy-start.3 = (bf16[2048,256]{1,0:T(8,128)(2,1)}, bf16[2048,256]{1,0:T(8,128)(2,1)S(1)}, u32[]{:S(2)}) copy-start(bf16[2048,256]{1,0:T(8,128)(2,1)S(1)} %copy.120.bc_ref) | copy-start | bytes 3145732
  161.3 21.5 %copy-start.10 = (f32[1,512]{1,0:T(1,128)}, f32[1,512]{1,0:T(1,128)S(1)}, u32[]{:S(2)}) copy-start(f32[1,512]{1,0:T(1,128)S(1)} %fusion.22.bx_ref) | copy-start | bytes 6148
  161.3 21.5 %copy-start.6 = (f32[4,512]{1,0:T(4,128)}, f32[4,512]{1,0:T(4,128)S(1)}, u32[]{:S(2)}) copy-start(f32[4,512]{1,0:T(4,128)S(1)} %dynamic-slice_bitcast_fusion.wx_ref) | copy-start | bytes 24580
  161.4 21.4 %copy-start.8 = (f32[8,1]{1,0:T(8,128)}, f32[8,1]{1,0:T(8,128)S(1)}, u32[]{:S(2)}) copy-start(f32[8,1]{1,0:T(8,128)S(1)} %get-tuple-element.84.bias_ref) | copy-start | bytes 100
  268.9 131.9 %reduce-scatter.12.cloned.1.call-start = ((), (), s32[]{:S(2)}) async-start(), calls=%async_computation.11 | async-start | bytes 5447680 | tf_op jit(solution)/shard_map/reduce_scatter | solution.py:841
  321.2 126.5 %reduce-scatter.14.cloned.1.call-start = ((), (), s32[]{:S(2)}) async-start(), calls=%async_computation.12 | async-start | bytes 2621440 | tf_op jit(solution)/shard_map/reduce_scatter | solution.py:815
  332.0 190.2 %reduce-scatter.10.cloned.1.call-start = ((), (), s32[]{:S(2)}) async-start(), calls=%async_computation.10 | async-start | bytes 9437184 | tf_op jit(solution)/shard_map/reduce_scatter | solution.py:848
  359.0 238.0 %reduce-scatter.6.cloned.1.call-start = ((), (), s32[]{:S(2)}) async-start(), calls=%async_computation.8 | async-start | bytes 9437184 | tf_op jit(solution)/shard_map/reduce_scatter | solution.py:806
  369.8 38.4 %copy-start.26 = (f32[8,512]{1,0:T(8,128)S(1)}, f32[8,512]{1,0:T(8,128)}, u32[]{:S(2)}) copy-start(f32[8,512]{1,0:T(8,128)} %get-tuple-element.34) | copy-start | bytes 49156
  369.8 39.1 %copy-start.29 = (f32[8,128]{1,0:T(8,128)S(1)}, f32[8,128]{1,0:T(8,128)}, u32[]{:S(2)}) copy-start(f32[8,128]{1,0:T(8,128)} %get-tuple-element.35) | copy-start | bytes 12292
  403.2 46.7 %all-to-all-start = ((bf16[8,64,1064]{2,1,0:T(8,128)(2,1)}), bf16[8,64,1064]{2,1,0:T(8,128)(2,1)}, u32[]{:S(2)}, u32[]{:S(2)}) async-start(bf16[8,64,1064]{2,1,0:T(8,128)(2,1)} %bitcast.53), calls=%async_computation.4 | async-start | bytes 2359296 | tf_op jit(solution)/shard_map/all_to_all | solution.py:842
  407.9 323.4 %all-reduce.13.cloned.1.call-start = ((), (), s32[]{:S(2)}) async-start(), calls=%async_computation.13 | async-start | bytes 1359872
  463.3 59.0 %copy-start.25 = (f32[2048]{0:T(1024)S(1)}, f32[2048]{0:T(1024)}, u32[]{:S(2)}) copy-start(f32[2048]{0:T(1024)} %param.15) | copy-start | bytes 24580
  463.3 59.0 %copy-start.28 = (f32[256]{0:T(256)S(1)}, f32[256]{0:T(256)}, u32[]{:S(2)}) copy-start(f32[256]{0:T(256)} %copy-done.27) | copy-start | bytes 3076
  463.3 60.9 %copy-start.35 = (f32[8]{0:T(128)S(1)}, f32[8]{0:T(128)}, u32[]{:S(2)}) copy-start(f32[8]{0:T(128)} %reduce_sum.121) | copy-start | bytes 100
  463.3 60.9 %copy-start.36 = (f32[8]{0:T(128)S(1)}, f32[8]{0:T(128)}, u32[]{:S(2)}) copy-start(f32[8]{0:T(128)} %get-tuple-element.46) | copy-start | bytes 100
  463.3 60.9 %copy-start.37 = (f32[8]{0:T(128)S(1)}, f32[8]{0:T(128)}, u32[]{:S(2)}) copy-start(f32[8]{0:T(128)} %get-tuple-element.47) | copy-start | bytes 100
  463.3 60.9 %copy-start.38 = (f32[128]{0:T(128)S(1)}, f32[128]{0:T(128)}, u32[]{:S(2)}) copy-start(f32[128]{0:T(128)} %reshape.252) | copy-start | bytes 1540
  463.4 60.9 %copy-start.39 = (f32[32]{0:T(128)S(1)}, f32[32]{0:T(128)}, u32[]{:S(2)}) copy-start(f32[32]{0:T(128)} %get-tuple-element.41) | copy-start | bytes 388
  464.9 61.9 %copy-start.34 = (f32[256]{0:T(256)S(1)}, f32[256]{0:T(256)}, u32[]{:S(2)}) copy-start(f32[256]{0:T(256)} %copy-done.33) | copy-start | bytes 3076
  464.9 132.2 %copy-start.17 = (bf16[1,256,2048]{2,1,0:T(8,128)(2,1)S(1)}, bf16[1,256,2048]{2,1,0:T(8,128)(2,1)}, u32[]{:S(2)}) copy-start(bf16[1,256,2048]{2,1,0:T(8,128)(2,1)} %param.13) | copy-start | bytes 3145732
  464.9 132.2 %copy-start.32 = (f32[256]{0:T(256)S(1)}, f32[256]{0:T(256)}, u32[]{:S(2)}) copy-start(f32[256]{0:T(256)} %copy-done.31) | copy-start | bytes 3076
  522.3 74.8 %copy-start.15 = (bf16[256,2048]{1,0:T(8,128)(2,1)S(1)}, bf16[256,2048]{1,0:T(8,128)(2,1)}, u32[]{:S(2)}) copy-start(bf16[256,2048]{1,0:T(8,128)(2,1)} %reduce-scatter.10.cloned.1.call-done) | copy-start | bytes 3145732
  597.1 141.4 %copy-start.1 = (f32[4096]{0:T(1024)S(1)}, f32[4096]{0:T(1024)}, u32[]{:S(2)}) copy-start(f32[4096]{0:T(1024)} %param.22) | copy-start | bytes 49156
  (23 other events, 82.5 us)
Sparse Core Ops, SparseCore 0:
  9.6 64.4 all-gather.5
  76.0 68.4 all-gather.3
  269.0 41.2 reduce-scatter.7
  321.3 79.4 reduce-scatter.11
  403.5 44.1 reduce-scatter.13
  451.4 70.7 reduce-scatter.9
  525.7 71.2 reduce-scatter.5
  603.1 128.1 all-reduce.12

commit v3 on v2

--- a/solution.py
+++ b/solution.py
@@ -125,10 +125,10 @@
 def project_kernel(
     planes, ny, ns, cut, heads,
     pm_ref, ps_ref, nm_ref,
-    proj_ref, bct_ref, dt_ref, nall_ref, wm_ref, ws_ref,
-    wmain, wsmall, normed, acc, outb, bcb,
+    proj_ref, bct_ref, dt_ref, nt_ref, wm_ref, ws_ref,
+    wmain, wsmall, normed, acc, outb, bcb, turned,
     am_send, am_recv, as_send, as_recv, n_send, n_recv, f_send, b_send, b_recv,
-    up_send, up_recv, down_send, down_recv, sup_send, sup_recv, sdown_send, sdown_recv, local_sem,
+    up_send, up_recv, down_send, down_recv, sup_send, sup_recv, sdown_send, sdown_recv, local_sem, turn_sem,
 ):
     at = Place(planes, ny, ns)
     group, rank, z = at.group, at.rank, at.z
@@ -321,8 +321,20 @@
     lax.fori_loop(0, slabs, narrow, 0)
     for i in range(1, group):
         bc_piece(at.peer(i), i, rank).start()
-    nall_copy = pltpu.make_async_copy(normed, nall_ref, local_sem.at[0])
-    nall_copy.start()
+
+    def turn_copy(m):
+        rows = pl.ds(pl.multiple_of(m * slab, slab), slab)
+        return pltpu.make_async_copy(turned.at[lax.rem(m, 2)], nt_ref.at[:, rows], turn_sem.at[lax.rem(m, 2)])
+
+    def turn(m):
+        @pl.when(m >= 2)
+        def _():
+            turn_copy(m - 2).wait()
+
+        rows = pl.ds(pl.multiple_of(m * slab, slab), slab)
+        turned[lax.rem(m, 2)] = normed[rows, :].T
+        turn_copy(m).start()
+
     ws_copy = pltpu.make_async_copy(wsmall, ws_ref, local_sem.at[1])
     ws_copy.start()
 
@@ -339,8 +351,18 @@
             return 0
 
         lax.fori_loop(0, per_step, one, 0)
+
+        def other(i, _):
+            @pl.when((k - busy) * turns + i < slabs)
+            def _():
+                turn((k - busy) * turns + i)
+
+            return 0
+
+        lax.fori_loop(0, turns, other, 0)
         return 0
 
+    turns = -(-slabs // cut)
     lax.fori_loop(busy, steps, busy_step, 0)
     wm_copy = pltpu.make_async_copy(wmain, wm_ref, local_sem.at[2])
     wm_copy.start()
@@ -399,7 +421,8 @@
         return 0
 
     lax.fori_loop(0, planes * cut, wide_sent, 0)
-    nall_copy.wait()
+    turn_copy(slabs - 2).wait()
+    turn_copy(slabs - 1).wait()
     ws_copy.wait()
     wm_copy.wait()
     bct_copy.wait()
@@ -422,7 +445,7 @@
             jax.ShapeDtypeStruct((total, width), BF16),
             jax.ShapeDtypeStruct((2 * STATE, total), BF16),
             jax.ShapeDtypeStruct((heads, total), F32),
-            jax.ShapeDtypeStruct((total, D), BF16),
+            jax.ShapeDtypeStruct((D, total), BF16),
             jax.ShapeDtypeStruct((D, width), BF16),
             jax.ShapeDtypeStruct((D, 128), BF16),
         ],
@@ -433,17 +456,507 @@
             pltpu.VMEM((total, width), F32),
             pltpu.VMEM((total, width), BF16),
             pltpu.VMEM((2 * STATE, total), BF16),
+            pltpu.VMEM((2, D, 256), BF16),
             dma((group,)), dma((group,)), dma((group,)), dma((group,)),
             dma((group,)), dma((group,)), dma((group,)), dma((group,)), dma((group,)),
             dma((planes * cut,)), dma((planes * cut,)), dma((planes * cut,)), dma((planes * cut,)),
             dma((planes,)), dma((planes,)), dma((planes,)), dma((planes,)),
-            dma((4 + total // 256,)),
+            dma((4 + total // 256,)), dma((2,)),
         ],
         compiler_params=pltpu.CompilerParams(
             collective_id=1, has_side_effects=True, vmem_limit_bytes=58 << 20
         ),
         name="gather_project",
     )(pieces, pieces_small, normed)
+
+
+def grads_kernel(
+    planes, ny, ns, cut,
+    nt_ref, dp_ref, wm_ref, ws_ref, dbc_ref, ddt_ref, raw_ref, cw_ref,
+    gw_ref, gs_ref, ng_ref, bsum_ref,
+    ntb, dp, wmain, dw, passing, dsmall, spassing, smalls, bcs, raw, sib_out, sib_in, far_in, own,
+    a_send, a_recv, as_send, as_recv, b_send, b_recv, x_send, x_recv, f_send, f_recv,
+    up_send, up_recv, down_send, down_recv, sup_send, sup_recv, sdown_send, sdown_recv, local_sem, nt_sem,
+):
+    at = Place(planes, ny, ns)
+    group, rank, z = at.group, at.rank, at.z
+    total, width = dp.shape
+    plane_rows = D // planes
+    piece, part = plane_rows // group, plane_rows // cut
+    block = total // group
+    chips = group // 2
+    chips_x = ns // 2
+    small = bcs.shape[1]
+    heads = ddt_ref.shape[0]
+    span = total // ny
+    rows_small = smalls.shape[0]
+
+    def plane_in_turn(j):
+        return lax.rem(jnp.where(2 * z < planes, z + j, z - j + planes), planes)
+
+    def nt_plane(i):
+        return plane_in_turn(lax.rem(2 * planes - 1 - i, planes))
+
+    def nt_copy(i):
+        rows = pl.ds(pl.multiple_of(nt_plane(i) * plane_rows, plane_rows), plane_rows)
+        return pltpu.make_async_copy(nt_ref.at[rows], ntb.at[lax.rem(i, 2)], nt_sem.at[lax.rem(i, 2)])
+
+    nt_copy(0).start()
+    dp_copy = pltpu.make_async_copy(dp_ref, dp, local_sem.at[0])
+    dp_copy.start()
+    nt_copy(1).start()
+    wm_copy = pltpu.make_async_copy(wm_ref, wmain, local_sem.at[1])
+    wm_copy.start()
+    own_small = pl.ds(pl.multiple_of(rank * small, small), small)
+    raw_copy = pltpu.make_async_copy(raw_ref.at[own_small], raw, local_sem.at[2])
+    raw_copy.start()
+    bcs_copy = pltpu.make_async_copy(dbc_ref.at[own_small], bcs.at[rank], local_sem.at[3])
+    bcs_copy.start()
+    at.greet()
+
+    def bc_piece(r, i, owner):
+        rows = pl.ds(pl.multiple_of(r * small, small), small)
+        return remote(dbc_ref.at[rows], bcs.at[owner], b_send.at[i], b_recv.at[owner], at.member(r))
+
+    for i in range(1, group):
+        bc_piece(at.peer(i), i, rank).start()
+    dp_copy.wait()
+
+    half = min(256, plane_rows)
+
+    def weight_plane(i):
+        p = nt_plane(i)
+        nt_copy(i).wait()
+
+        def one(h, _):
+            rows = pl.ds(pl.multiple_of(h * half, half), half)
+            there = pl.ds(pl.multiple_of(p * plane_rows + h * half, half), half)
+            dw[there, :] = jnp.dot(ntb[lax.rem(i, 2), rows, :], dp[...], preferred_element_type=F32)
+            return 0
+
+        lax.fori_loop(0, plane_rows // half, one, 0)
+        nt_copy(i + 2).start()
+
+    def narrow_plane(i):
+        nt_copy(i).wait()
+        dsmall[nt_plane(i)] = mm_last(smalls[...], ntb[lax.rem(i, 2)])
+
+        @pl.when(i + 2 < 2 * planes)
+        def _():
+            nt_copy(i + 2).start()
+
+    def rows_in(p, q):
+        return pl.ds(pl.multiple_of(p * plane_rows + q * part, part), part)
+
+    def wide_up(t, q, k):
+        ref = passing.at[rows_in(t + 1, q)]
+        return remote(ref, ref, up_send.at[k], up_recv.at[k], at.up)
+
+    def wide_down(t, q, k):
+        ref = passing.at[rows_in(t, q)]
+        return remote(ref, ref, down_send.at[k], down_recv.at[k], at.down)
+
+    def small_up(t, j):
+        return remote(spassing.at[t + 1], spassing.at[t + 1], sup_send.at[j], sup_recv.at[j], at.up)
+
+    def small_down(t, j):
+        return remote(spassing.at[t], spassing.at[t], sdown_send.at[j], sdown_recv.at[j], at.down)
+
+    def wide_step(k):
+        j, q = k // cut, lax.rem(k, cut)
+        t = planes - 1 - j
+
+        @pl.when(t > z)
+        def _():
+            here = rows_in(t + 1, q)
+
+            @pl.when(at.has_down)
+            def _():
+                wide_up(t, q, k).wait_recv()
+                passing[here, :] = (dw[rows_in(t, q), :] + passing[here, :].astype(F32)).astype(BF16)
+
+            @pl.when(jnp.logical_not(at.has_down))
+            def _():
+                passing[here, :] = dw[rows_in(t, q), :].astype(BF16)
+
+            wide_up(t, q, k).start()
+
+        @pl.when(j < z)
+        def _():
+            here = rows_in(j, q)
+
+            @pl.when(at.has_up)
+            def _():
+                wide_down(j, q, k).wait_recv()
+                passing[here, :] = (dw[here, :] + passing[here, :].astype(F32)).astype(BF16)
+
+            @pl.when(jnp.logical_not(at.has_up))
+            def _():
+                passing[here, :] = dw[here, :].astype(BF16)
+
+            wide_down(j, q, k).start()
+
+    def small_step(j, _):
+        t = planes - 1 - j
+
+        @pl.when(t > z)
+        def _():
+            @pl.when(at.has_down)
+            def _():
+                small_up(t, j).wait_recv()
+                spassing[t + 1] = (dsmall[t] + spassing[t + 1].astype(F32)).astype(BF16)
+
+            @pl.when(jnp.logical_not(at.has_down))
+            def _():
+                spassing[t + 1] = dsmall[t].astype(BF16)
+
+            small_up(t, j).start()
+
+        @pl.when(j < z)
+        def _():
+            @pl.when(at.has_up)
+            def _():
+                small_down(j, j).wait_recv()
+                spassing[j] = (dsmall[j] + spassing[j].astype(F32)).astype(BF16)
+
+            @pl.when(jnp.logical_not(at.has_up))
+            def _():
+                spassing[j] = dsmall[j].astype(BF16)
+
+            small_down(j, j).start()
+
+        return 0
+
+    def far_rank(i):
+        x, core = at.s // 2, lax.rem(at.s, 2)
+        return (
+            lax.rem(at.y + i // chips_x, ny) * ns + lax.rem(x + lax.rem(i, chips_x), chips_x) * 2 + core
+        )
+
+    sibling = at.sibling(rank)
+
+    def normed_part(r):
+        rows = pl.ds(pl.multiple_of(r * block, block), block)
+        turned = smalls[:, rows].T
+        return mm_last(dp[rows, :], wmain[...]) + mm_last(turned, ws_ref[:, :rows_small])
+
+    def to_sibling(i):
+        return remote(sib_out.at[i], sib_in.at[i], x_send.at[i], x_recv.at[i], at.member(sibling))
+
+    def to_far(i):
+        return remote(sib_in.at[i], far_in.at[i - 1], f_send.at[i], f_recv.at[i], at.member(far_rank(i)))
+
+    def first_task(n):
+        i = lax.rem(n + 1, chips)
+        sib_out[i] = normed_part(at.sibling(far_rank(i))).astype(BF16)
+        to_sibling(i).start()
+
+    def second_task(n):
+        i = lax.rem(n + 1, chips)
+        value = normed_part(far_rank(i))
+        to_sibling(i).wait_recv()
+        value = value + sib_in[i].astype(F32)
+
+        @pl.when(i > 0)
+        def _():
+            sib_in[i] = value.astype(BF16)
+            to_far(i).start()
+
+        @pl.when(i == 0)
+        def _():
+            own[...] = value
+
+    def tasks_step(k, _):
+        wide_step(k)
+
+        @pl.when(k < chips)
+        def _():
+            first_task(k)
+
+        @pl.when((k >= chips) & (k < 2 * chips))
+        def _():
+            second_task(k - chips)
+
+        return 0
+
+    def plain_step(k, _):
+        wide_step(k)
+        return 0
+
+    ahead = planes if planes > 4 else 2
+    for i in range(ahead):
+        weight_plane(i)
+
+    raw_copy.wait()
+    bcs_copy.wait()
+    for i in range(1, group):
+        r = at.peer(i)
+        bc_piece(r, i, r).wait_recv()
+    dbc = bcs[0].astype(F32)
+    for r in range(1, group):
+        dbc = dbc + bcs[r].astype(F32)
+    values = raw[...].astype(F32)
+    place = lax.rem(iota(values.shape, 1), span)
+    later = [jnp.where(place >= n, pltpu.roll(values, n, 1), 0.0) if n else values for n in range(KERNEL)]
+    conv = cw_ref[:, KERNEL : KERNEL + 1]
+    for k in range(KERNEL):
+        conv = conv + cw_ref[:, k : k + 1] * later[KERNEL - 1 - k]
+    sig = 1.0 / (1.0 + jnp.exp(-conv))
+    dconv = dbc * (sig * (1.0 + conv * (1.0 - sig)))
+    din = jnp.zeros_like(dconv)
+    bsum_ref[...] = jnp.zeros_like(bsum_ref)
+    bsum_ref[:, KERNEL : KERNEL + 1] = jnp.sum(dconv, 1, keepdims=True)
+    for k in range(KERNEL):
+        n = KERNEL - 1 - k
+        bsum_ref[:, k : k + 1] = jnp.sum(dconv * later[n], 1, keepdims=True)
+        moved = jnp.where(place < span - n, pltpu.roll(dconv, total - n, 1), 0.0) if n else dconv
+        din = din + cw_ref[:, k : k + 1] * moved
+    filler = jnp.zeros((rows_small - small - heads, total), F32)
+    smalls[...] = jnp.concatenate([din, ddt_ref[...].astype(F32), filler], 0).astype(BF16)
+    wm_copy.wait()
+
+    steps = (planes - 1) * cut
+    lax.fori_loop(0, 2 * chips, tasks_step, 0)
+    start = 2 * chips
+    for i in range(ahead, planes):
+        weight_plane(i)
+        stop = min(max((i - ahead + 2) * cut, start), steps)
+        lax.fori_loop(start, stop, plain_step, 0)
+        start = stop
+    for i in range(planes, 2 * planes):
+        narrow_plane(i)
+        if i == planes + 1 and start < steps:
+            stop = start + (steps - start) // 2
+            lax.fori_loop(start, stop, plain_step, 0)
+            start = stop
+    lax.fori_loop(0, planes - 1, small_step, 0)
+    lax.fori_loop(start, steps, plain_step, 0)
+
+    @pl.when(at.has_down)
+    def _():
+        small_up(z, planes - 1 - z).wait_recv()
+
+    @pl.when(at.has_up)
+    def _():
+        small_down(z, z).wait_recv()
+
+    nothing = jnp.zeros((rows_small, plane_rows), F32)
+    spassing[z] = (
+        dsmall[z]
+        + jnp.where(at.has_down, spassing[z + 1].astype(F32), nothing)
+        + jnp.where(at.has_up, spassing[z].astype(F32), nothing)
+    ).astype(BF16)
+
+    def small_out(r, i, owner):
+        lanes = pl.ds(pl.multiple_of(r * piece // 128 * 128, 128), 128)
+        return remote(
+            spassing.at[z, :, lanes], gs_ref.at[owner], as_send.at[i], as_recv.at[owner], at.member(r)
+        )
+
+    own_lanes = pl.ds(pl.multiple_of(rank * piece // 128 * 128, 128), 128)
+    small_kept = pltpu.make_async_copy(spassing.at[z, :, own_lanes], gs_ref.at[rank], local_sem.at[2])
+    small_kept.start()
+    for i in range(1, group):
+        small_out(at.peer(i), i, rank).start()
+
+    def piece_rows(r):
+        return pl.ds(pl.multiple_of(z * plane_rows + r * piece, piece), piece)
+
+    def wide_out(r, owner):
+        return remote(
+            passing.at[piece_rows(r)], gw_ref.at[owner], a_send.at[r], a_recv.at[owner], at.member(r)
+        )
+
+    wide_kept = pltpu.make_async_copy(passing.at[piece_rows(rank)], gw_ref.at[rank], local_sem.at[3])
+
+    def last_step(q, _):
+        here = rows_in(z, q)
+
+        @pl.when(at.has_down)
+        def _():
+            wide_up(z, q, (planes - 1 - z) * cut + q).wait_recv()
+
+        @pl.when(at.has_up)
+        def _():
+            wide_down(z, q, z * cut + q).wait_recv()
+
+        nothing = jnp.zeros((part, width), F32)
+        passing[here, :] = (
+            dw[here, :]
+            + jnp.where(at.has_down, passing[rows_in(z + 1, q), :].astype(F32), nothing)
+            + jnp.where(at.has_up, passing[here, :].astype(F32), nothing)
+        ).astype(BF16)
+        for n in range(group // cut):
+            r = q * (group // cut) + n
+
+            @pl.when(r != rank)
+            def _():
+                wide_out(r, rank).start()
+
+            @pl.when(r == rank)
+            def _():
+                wide_kept.start()
+
+        return 0
+
+    lax.fori_loop(0, cut, last_step, 0)
+
+    value = own[...]
+    for i in range(1, chips):
+        to_far(i).wait_recv()
+        value = value + far_in[i - 1].astype(F32)
+    ng_ref[...] = value
+
+    for i in range(1, group):
+        r = at.peer(i)
+        bc_piece(r, i, rank).wait_send()
+        small_out(r, i, rank).wait_send()
+        small_out(r, i, r).wait_recv()
+        wide_out(r, rank).wait_send()
+        wide_out(r, r).wait_recv()
+    small_kept.wait()
+    wide_kept.wait()
+    for i in range(chips):
+        to_sibling(i).wait_send()
+        if i:
+            to_far(i).wait_send()
+
+    def wide_sent(k, _):
+        j, q = k // cut, lax.rem(k, cut)
+
+        @pl.when(planes - 1 - j > z)
+        def _():
+            wide_up(planes - 1 - j, q, k).wait_send()
+
+        @pl.when(j < z)
+        def _():
+            wide_down(j, q, k).wait_send()
+
+        return 0
+
+    lax.fori_loop(0, steps, wide_sent, 0)
+
+    def small_sent(j, _):
+        @pl.when(planes - 1 - j > z)
+        def _():
+            small_up(planes - 1 - j, j).wait_send()
+
+        @pl.when(j < z)
+        def _():
+            small_down(j, j).wait_send()
+
+        return 0
+
+    lax.fori_loop(0, planes - 1, small_sent, 0)
+
+
+def project_grads(normed_t, proj_grad, w_main, w_small, dbc_t, ddt_t, bc_raw, conv_own, planes, ny, ns):
+    total, width = proj_grad.shape
+    group = ny * ns
+    small, heads = 2 * STATE // group, ddt_t.shape[0]
+    rows_small = -(-(small + heads) // 16) * 16
+    plane_rows = D // planes
+    block = total // group
+    chips = group // 2
+    cut = 1
+    while cut * 2 <= min(group, 32 // planes):
+        cut *= 2
+    dma = pltpu.SemaphoreType.DMA
+    anywhere = pl.BlockSpec(memory_space=pl.ANY)
+    vmem = pl.BlockSpec(memory_space=pltpu.VMEM)
+    return pl.pallas_call(
+        functools.partial(grads_kernel, planes, ny, ns, cut),
+        in_specs=[anywhere, anywhere, anywhere, vmem, anywhere, vmem, anywhere, vmem],
+        out_specs=[anywhere, anywhere, vmem, vmem],
+        out_shape=[
+            jax.ShapeDtypeStruct((group, plane_rows // group, width), BF16),
+            jax.ShapeDtypeStruct((group, rows_small, 128), BF16),
+            jax.ShapeDtypeStruct((block, D), F32),
+            jax.ShapeDtypeStruct((small, 128), F32),
+        ],
+        scratch_shapes=[
+            pltpu.VMEM((2, plane_rows, total), BF16),
+            pltpu.VMEM((total, width), BF16),
+            pltpu.VMEM((D, width), BF16),
+            pltpu.VMEM((D, width), F32),
+            pltpu.VMEM((D + plane_rows, width), BF16),
+            pltpu.VMEM((planes, rows_small, plane_rows), F32),
+            pltpu.VMEM((planes + 1, rows_small, plane_rows), BF16),
+            pltpu.VMEM((rows_small, total), BF16),
+            pltpu.VMEM((group, small, total), BF16),
+            pltpu.VMEM((small, total), BF16),
+            pltpu.VMEM((chips, block, D), BF16),
+            pltpu.VMEM((chips, block, D), BF16),
+            pltpu.VMEM((chips - 1, block, D), BF16),
+            pltpu.VMEM((block, D), F32),
+            dma((group,)), dma((group,)), dma((group,)), dma((group,)), dma((group,)), dma((group,)),
+            dma((chips,)), dma((chips,)), dma((chips,)), dma((chips,)),
+            dma((planes * cut,)), dma((planes * cut,)), dma((planes * cut,)), dma((planes * cut,)),
+            dma((planes,)), dma((planes,)), dma((planes,)), dma((planes,)),
+            dma((4,)), dma((2,)),
+        ],
+        compiler_params=pltpu.CompilerParams(
+            collective_id=2, has_side_effects=True, vmem_limit_bytes=60 << 20
+        ),
+        name="project_grads",
+    )(normed_t, proj_grad, w_main, w_small, dbc_t, ddt_t, bc_raw, conv_own)
+
+
+def exchange_kernel(planes, ny, ns, mine_ref, out_ref, along, summed, z_send, z_recv, p_send, p_recv):
+    at = Place(planes, ny, ns)
+    group, rank, z = at.group, at.rank, at.z
+    barrier = pltpu.get_barrier_semaphore()
+    for i in range(1, planes):
+        pl.semaphore_signal(
+            barrier, inc=1, device_id=(lax.rem(z + i, planes), at.y, at.s), device_id_type=MESH
+        )
+    for i in range(1, group):
+        pl.semaphore_signal(barrier, inc=1, device_id=at.member(at.peer(i)), device_id_type=MESH)
+    pl.semaphore_wait(barrier, planes + group - 2)
+
+    def over_z(p, i, owner):
+        return remote(mine_ref, along.at[owner], z_send.at[i], z_recv.at[owner], (p, at.y, at.s))
+
+    for i in range(1, planes):
+        over_z(lax.rem(z + i, planes), i, z).start()
+    total = mine_ref[...]
+    for i in range(1, planes):
+        p = lax.rem(z + i, planes)
+        over_z(p, i, p).wait_recv()
+        total = total + along[p]
+    summed[...] = total
+
+    def over_plane(r, i, owner):
+        return remote(summed, out_ref.at[owner], p_send.at[i], p_recv.at[owner], at.member(r))
+
+    for i in range(1, group):
+        over_plane(at.peer(i), i, rank).start()
+    out_ref[rank] = total
+    for i in range(1, group):
+        r = at.peer(i)
+        over_plane(r, i, r).wait_recv()
+        over_plane(r, i, rank).wait_send()
+    for i in range(1, planes):
+        over_z(lax.rem(z + i, planes), i, z).wait_send()
+
+
+def exchange(mine, planes, ny, ns):
+    group = ny * ns
+    dma = pltpu.SemaphoreType.DMA
+    vmem = pl.BlockSpec(memory_space=pltpu.VMEM)
+    return pl.pallas_call(
+        functools.partial(exchange_kernel, planes, ny, ns),
+        in_specs=[vmem],
+        out_specs=vmem,
+        out_shape=jax.ShapeDtypeStruct((group,) + mine.shape, F32),
+        scratch_shapes=[
+            pltpu.VMEM((planes,) + mine.shape, F32),
+            pltpu.VMEM(mine.shape, F32),
+            dma((planes,)), dma((planes,)), dma((group,)), dma((group,)),
+        ],
+        compiler_params=pltpu.CompilerParams(collective_id=3, has_side_effects=True),
+        name="exchange",
+    )(mine)
 
 
 def forward_kernel(
@@ -574,8 +1087,8 @@
     dproducts = jnp.where(causal, dproducts, 0.0)
     dc_t = dc_t + mm_last(b_t, dproducts)
     db_t = db_t + mm(c_t, dproducts)
-    dbc_ref[:STATE] = db_t
-    dbc_ref[STATE:] = dc_t
+    dbc_ref[:STATE] = db_t.astype(BF16)
+    dbc_ref[STATE:] = dc_t.astype(BF16)
     dxdt = jnp.concatenate(dxdt_t, 0).T + outward_grad
 
     member = (iota((heads, channels), 1) // HEADDIM == iota((heads, channels), 0)).astype(F32)
@@ -678,7 +1191,7 @@
         ],
         out_shape=[
             jax.ShapeDtypeStruct((total, 2 * channels), BF16),
-            jax.ShapeDtypeStruct((2 * STATE, total), F32),
+            jax.ShapeDtypeStruct((2 * STATE, total), BF16),
             jax.ShapeDtypeStruct((heads, total), BF16),
             jax.ShapeDtypeStruct((8, channels), F32),
             jax.ShapeDtypeStruct((heads, 128), F32),
@@ -747,6 +1260,7 @@
     row_count = tokens.shape[1]
     planes, group = lax.axis_size("z"), lax.axis_size("y") * lax.axis_size("seq")
     seqs = lax.axis_size("y")
+    ny, ns = lax.axis_size("y"), lax.axis_size("seq")
     rank = lax.axis_index("y") * lax.axis_size("seq") + lax.axis_index("seq")
     lay = Layout(planes, group, w_out.shape[0])
     channels, small = lay.channels, lay.small
@@ -778,10 +1292,9 @@
     gain_own = own(gate_gain[None], HEADDIM)
     params = (conv_wx, conv_bx, bias_own, a_own, skip_own)
 
-    projected, bc_raw, dt_t, normed_all, w_main, w_small = gather_project(
-        pieces, pieces_small, normed, planes, lax.axis_size("y"), lax.axis_size("seq"), lay.heads
+    projected, bc_raw, dt_t, normed_t, w_main, w_small = gather_project(
+        pieces, pieces_small, normed, planes, ny, ns, lay.heads
     )
-    w_small = w_small[:, : small + lay.heads]
     bc_in = bc_raw.astype(F32)
     conv_bc = conv_b[INNER:, None]
     for k in range(KERNEL):
@@ -820,34 +1333,17 @@
     proj_grad, dbc_t, ddt_t, sums_x, sums_h = scan_backward(
         projected, bc, bc_t, dt_t, params, gain_own, scanned, states, mixed_grad, norms, seqs
     )
-    dbc = lax.psum_scatter(dbc_t, GROUP, scatter_dimension=0, tiled=True)
-    own_rows = lambda v: lax.dynamic_slice_in_dim(v, rank * small, small, 0)
-    conv_own, in_own, w_bc = own_rows(conv_bc), own_rows(bc_in), own_rows(conv_w[INNER:])
-    sig = jax.nn.sigmoid(conv_own)
-    dconv = dbc * sig * (1.0 + conv_own * (1.0 - sig))
-    din = 0.0
-    grad_w_bc = []
-    for k in range(KERNEL):
-        grad_w_bc.append(jnp.sum(dconv * shift_later(in_own, KERNEL - 1 - k, seqs), 1))
-        din = din + w_bc[:, k : k + 1] * shift_earlier(dconv, KERNEL - 1 - k, seqs)
-    small_grad_t = jnp.concatenate([din.astype(BF16), ddt_t], 0)
-
-    contract_rows = (((0,), (0,)), ((), ()))
-    in_main = lax.dot_general(normed_all, proj_grad, contract_rows, preferred_element_type=F32)
-    in_small = lax.dot_general(
-        normed_all, small_grad_t, (((0,), (1,)), ((), ())), preferred_element_type=F32
+    own_bc = lambda v: lax.dynamic_slice_in_dim(v[INNER:], rank * small, small, 0)
+    conv_own = jnp.pad(
+        jnp.concatenate([own_bc(conv_w), own_bc(conv_b[:, None])], 1), ((0, 0), (0, 128 - KERNEL - 1))
     )
-    in_part = jnp.concatenate([in_main.astype(BF16), in_small.astype(BF16)], 1)
-    in_rows = lax.psum_scatter(in_part, "z", scatter_dimension=0, tiled=True)
-    in_pieces = lax.all_to_all(in_rows, GROUP, split_axis=0, concat_axis=1, tiled=True)
-    grad_w_in = lay.uncolumns(in_pieces.reshape(w_in.shape[0], group, -1).astype(F32))
-
-    normed_part = lax.dot_general(
-        proj_grad, w_main, (((1,), (1,)), ((), ())), preferred_element_type=F32
-    ) + lax.dot_general(small_grad_t, w_small, (((0,), (1,)), ((), ())), preferred_element_type=F32)
-    normed_grad = lax.psum_scatter(
-        normed_part.astype(BF16), GROUP, scatter_dimension=0, tiled=True
-    ).astype(F32)
+    in_pieces, in_small, normed_grad, bc_sums = project_grads(
+        normed_t, proj_grad, w_main, w_small, dbc_t, ddt_t, bc_raw, conv_own, planes, ny, ns
+    )
+    lanes = in_small.reshape(group, in_small.shape[1], -1, w_in.shape[0])
+    mine = lax.dynamic_index_in_dim(lanes, lax.rem(rank, lanes.shape[2]), 2, keepdims=False)
+    mine = mine[:, : small + lay.heads].transpose(2, 0, 1)
+    grad_w_in = lay.uncolumns(jnp.concatenate([in_pieces.transpose(1, 0, 2), mine], 2)).astype(F32)
     g = normed_grad * norm_gain
     input_grad = masked_cot + rms * g - inputs * (rms ** 3 * jnp.mean(g * inputs, -1, keepdims=True))
     norm_gain_grad = jnp.sum(normed_grad * inputs * rms, 0)
@@ -858,14 +1354,15 @@
             jnp.sum(sums_x[KERNEL + 2].reshape(-1, HEADDIM), 1),
             sums_h[:, 0],
             sums_h[:, 1],
-            jnp.stack(grad_w_bc).reshape(-1),
-            jnp.sum(dconv, 1),
+            bc_sums[:, :KERNEL].T.reshape(-1),
+            bc_sums[:, KERNEL],
         ]
     )
     count = own_sums.shape[0]
-    everyone = lax.all_gather(jnp.concatenate([own_sums, norm_gain_grad]), ("z",) + GROUP)
-    grad_norm_gain = jnp.sum(everyone[:, count:], 0)
-    by_rank = jnp.sum(everyone[:, :count].reshape(planes, group, count), 0)
+    flat = jnp.concatenate([norm_gain_grad, own_sums, jnp.zeros((-(count + D) % 1024,), F32)])
+    by_rank = exchange(flat.reshape(-1, 128), planes, ny, ns).reshape(group, -1)
+    grad_norm_gain = jnp.sum(by_rank[:, :D], 0)
+    by_rank = by_rank[:, D : D + count]
     at = 0
 
     def take(size):

time: 750 us -> 492 us (0.66)
  waiting for transfers between devices: 348 us -> 0.11 us
  Pallas kernels: 190 us -> 353 us
  matrix products: 82.2 us -> 34.1 us
  local copies, waits for them, and re-layouts: 55.8 us -> 45.1 us
    pallas_call x0 -> x2, Pallas kernels: none -> 164 us  [the longest x1 152 us: project_grads(): pl.pallas_call(functools.partial(grads_kernel, planes, ny, ns, cut), in_s...]
    unnamed x9 -> x4, waiting for transfers between devices: 131 us -> 0.07 us
    reduce_scatter x3 -> x0, waiting for transfers between devices: 110 us -> none  [the longest x1 57.4 us: body(): lax.psum_scatter(normed_part.astype(BF16), GROUP, scatter_dimension=0, ti...]
    reduce_scatter x1, waiting for transfers between devices: 70.3 us -> 0.01 us  [body(): lax.psum_scatter(jnp.dot(mixed, out_own, preferred_element_type=F32).asty...]
    dot_general x4 -> x0, matrix products: 46.4 us -> none  [the longest x1 15.4 us: body(): lax.dot_general(proj_grad, w_main, (((1,), (1,)), ((), ())), preferred_el...]
    reduce_scatter x1, waiting for transfers between devices: 37.5 us -> 0.01 us  [body(): lax.psum_scatter(out_part, 'z', scatter_dimension=0, tiled=True).astype(F32)]
  transfers between devices with their start and end apart: 9 -> 4, of which waited for: 6 -> 0; matrix products, arithmetic and copies ran while one was open for 17% -> 13% of each run, Pallas kernels for 19% -> 72%
where the time goes in v3:
time: 492 us; the launch traced here: 488 us
  Pallas kernels  353 us (72%)
  local copies, waits for them, and re-layouts  45.1 us (9%)
  matrix products  34.1 us (7%)
  blocking collectives  20.4 us (4%)
  other arithmetic  20.2 us (4%)
  between operations  15.4 us (3%)
    pallas_call x1, Pallas kernels, project_grads(): pl.pallas_call(functools.partial(grads_kernel, planes, ny, ns, cut), in_s...  152 us
    pallas_call x1, Pallas kernels, gather_project(): pl.pallas_call(functools.partial(project_kernel, planes, ny, ns, cut, hea...  119 us
    pallas_call x1, Pallas kernels, scan_backward(): pl.pallas_call(backward_kernel, grid=(seqs, steps), in_specs=[pl.BlockSpe...  49 us
    pallas_call x1, Pallas kernels, scan_forward(): pl.pallas_call(forward_kernel, grid=(seqs, steps), in_specs=[pl.BlockSpec...  21.4 us
    psum x1, blocking collectives, body(): lax.psum(jnp.stack([jnp.sum(product * product, 1), jnp.sum(mixed_grad * g...  20.4 us
    dot_general x1, matrix products, body(): lax.dot_general(grad_all, out_own, (((1,), (1,)), ((), ())), preferred_el...  14.4 us
    unnamed x67, local copies, waits for them, and re-layouts  13.1 us
    pallas_call x1, Pallas kernels, exchange(): pl.pallas_call(functools.partial(exchange_kernel, planes, ny, ns), in_spe...  11.3 us
  transfers between devices with their start and end apart: 4, of which 0 were waited for; matrix products, arithmetic and copies ran while one was open for 13% of the time, Pallas kernels for 72%

profile of v3, /device:TPU:1, one launch (start us, length us, event | category | flops | bytes accessed | tf_op | source)
XLA Modules:
  0.0 488.4 jit_solution(15292572247493455323)
XLA Ops:
  7.3 2.2 convert_element_type.82
  10.2 1.3 fusion.15
  11.5 3.4 copy.85
  14.9 1.3 fusion.21
  16.6 1.6 copy.86
  19.0 1.0 reshape.201
  20.3 2.6 concatenate.21
  22.9 1.1 slice.183.pm_ref
  25.0 1.3 fusion.6.nm_ref
  26.3 119.0 %gather_project.1 = (bf16[2048,1024]{1,0:T(8,128)(2,1)}, bf16[256,2048]{1,0:T(8,128)(2,1)}, f32[8,2048]{1,0:T(8,128)}, bf16[2048,2048]{1,0:T(8,128)(2,1)}, bf16[...) custom-call(bf16[8,64,1024]{2,1,0:T(8,128)(2,1)} %slice.183.pm_ref, bf16[8,64,128]{2,1,0:T(8,128)(2,1)} %pad.20.ps_ref, ...), custom_call_target="tpu_custom_call" | custom-call | tf_op jit(solution)/shard_map/gather_project/pallas_call | solution.py:440
  145.3 3.1 reshape.205
  148.4 6.6 %pad_slice_fusion.2 = (f32[256,2,1024]{2,1,0:T(2,128)S(1)}, f32[256,2,1024]{2,1,0:T(2,128)S(1)}, f32[256,2,1024]{2,1,0:T(2,128)S(1)}) fusion(f32[256,2,1024]{2,1,0:T(2,128)S(1)} %reshape.205), kind=kLoop, calls=%fused_computation.19 | loop fusion | bytes 8388608 | tf_op jit(solution)/shard_map/slice | solution.py:1209
  158.1 1.2 multiply_convert_fusion.1.bct_ref
  161.2 21.4 %scan_forward.1 = (f32[2048,512]{1,0:T(8,128)}, f32[8,128,512]{2,1,0:T(8,128)S(1)}) custom-call(bf16[2048,1024]{1,0:T(8,128)(2,1)} %get-tuple-element.28.x_ref.gate_ref.halo_ref, bf16[2048,1024]{1,0:T(8,128)(2,1)} %get-tuple-element.28.x_ref.gate_ref.halo_ref, bf16[2048,256]{1,0:T(8,128)(2,1)S(1)} %copy.95.bc_ref, ...), custom_call_target="tpu_custom_call" | custom-call | tf_op jit(solution)/shard_map/scan_forward/pallas_call | solution.py:1135
  182.6 1.3 copy-done.3
  184.0 14.4 %multiply_reduce_fusion.1 = (f32[2048]{0:T(1024)S(1)}, f32[2048]{0:T(1024)S(1)}, f32[2048,512]{1,0:T(8,128)}, f32[2048,512]{1,0:T(8,128)}) fusion(f32[512]{0:T(512)S(1)} %bitcast.225, f32[2048,512]{1,0:T(8,128)} %get-tuple-element.31.scanned_ref, bf16[2048,1024]{1,0:T(8,128)(2,1)} %get-tuple-element.28.x_ref.gate_ref.halo_ref, ...), kind=kOutput, calls=%fused_computation.15 | convolution fusion | flops 4306497536 | bytes 25184256 | tf_op jit(solution)/shard_map/dot_general | solution.py:1308
  198.5 20.4 %psum.7 = f32[2,2048]{1,0:T(2,128)S(1)} all-reduce(f32[2,2048]{1,0:T(2,128)S(1)} %pad_maximum_fusion.1), channel_id=1, replica_groups=mesh['z'=4,'y'=2,'seq'=4] {'y','seq'}, use_global_device_ids=true, to_apply=%region_3.4 | all-reduce | flops 4096 | bytes 32768 | tf_op jit(solution)/shard_map/psum | solution.py:1312
  218.9 10.7 %convolution_convert_fusion.1 = bf16[512,2048]{1,0:T(8,128)(2,1)} fusion(bf16[2048,2048]{1,0:T(8,128)(2,1)} %all-gather.3.cloned.1.call-done, f32[2048,512]{1,0:T(8,128)} %get-tuple-element.51, f32[2048]{0:T(1024)S(1)} %bitcast.210, f32[512]{0:T(512)S(1)} %bitcast.226), kind=kOutput, calls=%fused_computation.16 | convolution fusion | flops 4299161600 | bytes 14690304 | tf_op jit(solution)/shard_map/dot_general | solution.py:1324
  229.7 1.5 copy-done.25
  231.2 9.0 %convolution_convert_fusion = bf16[2048,2048]{1,0:T(8,128)(2,1)} fusion(bf16[512,2048]{1,0:T(8,128)(2,1)S(1)} %copy-done.25, f32[2048,512]{1,0:T(8,128)} %get-tuple-element.51, f32[2048]{0:T(1024)S(1)} %bitcast.211, f32[512]{0:T(512)S(1)} %bitcast.227), kind=kOutput, calls=%fused_computation | convolution fusion | flops 4302307328 | bytes 14690304 | tf_op jit(solution)/shard_map/dot_general | solution.py:1320
  243.0 49.0 %scan_backward.1 = (bf16[2048,1024]{1,0:T(8,128)(2,1)}, bf16[256,2048]{1,0:T(8,128)(2,1)}, bf16[8,2048]{1,0:T(8,128)(2,1)}, f32[8,512]{1,0:T(8,128)}, f32[8,128]{1,0:T(8,128)}) custom-call(bf16[2048,1024]{1,0:T(8,128)(2,1)} %get-tuple-element.28.x_ref.gate_ref.halo_ref, bf16[2048,1024]{1,0:T(8,128)(2,1)} %get-tuple-element.28.x_ref.gate_ref.halo_ref, ...), custom_call_target="tpu_custom_call" | custom-call | tf_op jit(solution)/shard_map/scan_backward/pallas_call | solution.py:1166
  292.0 152.2 %project_grads.1 = (bf16[8,64,1024]{2,1,0:T(8,128)(2,1)}, bf16[8,48,128]{2,1,0:T(8,128)(2,1)}, f32[256,2048]{1,0:T(8,128)}, f32[32,128]{1,0:T(8,128)}) custom-call(bf16[2048,2048]{1,0:T(8,128)(2,1)} %get-tuple-element.32.nt_ref, bf16[2048,1024]{1,0:T(8,128)(2,1)} %get-tuple-element.34.dp_ref, bf16[2048,1024]{1,0:T(8,128)(2,1)} %get-tuple-element.35.wm_ref, ...), custom_call_target="tpu_custom_call" | custom-call | tf_op jit(solution)/shard_map/project_grads/pallas_call | solution.py:867
  445.5 0.9 slice_reduce_fusion.1
  446.4 2.2 fusion.13
  449.3 11.3 %exchange.1 = f32[8,48,128]{2,1,0:T(8,128)} custom-call(f32[48,128]{1,0:T(8,128)} %bitcast.202), custom_call_target="tpu_custom_call" | custom-call | tf_op jit(solution)/shard_map/exchange/pallas_call | solution.py:947
  460.6 1.0 copy.141
  462.5 1.3 fusion.22
  464.6 1.0 copy.139
  466.3 1.0 copy.140
  472.5 2.8 maximum_convert_fusion
  475.4 2.1 convert_element_type.89
  477.5 4.1 fusion.11
  (163 shorter events, 19.8 us)
Async XLA Ops:
  7.2 176.8 %copy-start = (f32[4096]{0:T(1024)S(1)}, f32[4096]{0:T(1024)}, u32[]{:S(2)}) copy-start(f32[4096]{0:T(1024)} %param.22) | copy-start | bytes 49156
  7.2 3.0 copy-start.14
  7.2 176.8 %all-gather.5.cloned.1.call-start = ((), (), s32[]{:S(2)}) async-start(), calls=%async_computation.3 | async-start | bytes 2621440 | tf_op jit(solution)/shard_map/all_gather | solution.py:1279
  9.5 174.5 %all-gather.3.cloned.1.call-start = ((), (), s32[]{:S(2)}) async-start(), calls=%async_computation.2 | async-start | bytes 9437184 | tf_op jit(solution)/shard_map/all_gather | solution.py:1307
  11.5 463.9 %reduce-scatter.5.cloned.1.call-start = ((), (), s32[]{:S(2)}) async-start(), calls=%async_computation.5 | async-start | bytes 2621440 | tf_op jit(solution)/shard_map/reduce_scatter | solution.py:1328
  14.9 1.7 copy-start.12
  18.2 1.8 slice-start
  18.2 1.9 slice-start.1
  20.3 4.4 copy-start.10
  22.9 2.1 copy-start.18
  156.8 0.9 copy-start.21
  156.9 0.9 copy-start.17
  156.9 1.3 copy-start.11
  159.3 23.3 %copy-start.1 = (bf16[256,2048]{1,0:T(8,128)(2,1)}, bf16[256,2048]{1,0:T(8,128)(2,1)S(1)}, u32[]{:S(2)}) copy-start(bf16[256,2048]{1,0:T(8,128)(2,1)S(1)} %multiply_convert_fusion.1.bct_ref) | copy-start | bytes 3145732
  159.3 1.2 copy-start.24
  159.3 1.9 copy-start.4
  159.9 22.7 %copy-start.2 = (bf16[2048,256]{1,0:T(8,128)(2,1)}, bf16[2048,256]{1,0:T(8,128)(2,1)S(1)}, u32[]{:S(2)}) copy-start(bf16[2048,256]{1,0:T(8,128)(2,1)S(1)} %copy.95.bc_ref) | copy-start | bytes 3145732
  161.1 21.5 %copy-start.8 = (f32[1,512]{1,0:T(1,128)}, f32[1,512]{1,0:T(1,128)S(1)}, u32[]{:S(2)}) copy-start(f32[1,512]{1,0:T(1,128)S(1)} %broadcast_in_dim.9.skip_ref) | copy-start | bytes 6148
  161.1 21.5 %copy-start.9 = (f32[1,512]{1,0:T(1,128)}, f32[1,512]{1,0:T(1,128)S(1)}, u32[]{:S(2)}) copy-start(f32[1,512]{1,0:T(1,128)S(1)} %dynamic-slice_bitcast_fusion.3.bx_ref) | copy-start | bytes 6148
  161.1 21.5 %copy-start.5 = (f32[4,512]{1,0:T(4,128)}, f32[4,512]{1,0:T(4,128)S(1)}, u32[]{:S(2)}) copy-start(f32[4,512]{1,0:T(4,128)S(1)} %dynamic-slice_bitcast_fusion.wx_ref) | copy-start | bytes 24580
  161.2 21.4 %copy-start.6 = (f32[8,1]{1,0:T(8,128)}, f32[8,1]{1,0:T(8,128)S(1)}, u32[]{:S(2)}) copy-start(f32[8,1]{1,0:T(8,128)S(1)} %get-tuple-element.73.alog_ref) | copy-start | bytes 100
  161.2 21.4 %copy-start.7 = (f32[8,1]{1,0:T(8,128)}, f32[8,1]{1,0:T(8,128)S(1)}, u32[]{:S(2)}) copy-start(f32[8,1]{1,0:T(8,128)S(1)} %get-tuple-element.74.bias_ref) | copy-start | bytes 100
  182.6 1.3 copy-start.3
  229.6 1.6 copy-start.25
  229.7 247.8 %reduce-scatter.3.cloned.1.call-start = ((), (), s32[]{:S(2)}) async-start(), calls=%async_computation.4 | async-start | bytes 9437184 | tf_op jit(solution)/shard_map/reduce_scatter | solution.py:1319
  291.9 153.1 %copy-start.19 = (f32[8,512]{1,0:T(8,128)S(1)}, f32[8,512]{1,0:T(8,128)}, u32[]{:S(2)}) copy-start(f32[8,512]{1,0:T(8,128)} %get-tuple-element.40) | copy-start | bytes 49156
  292.0 153.4 %copy-start.20 = (f32[8,128]{1,0:T(8,128)S(1)}, f32[8,128]{1,0:T(8,128)}, u32[]{:S(2)}) copy-start(f32[8,128]{1,0:T(8,128)} %get-tuple-element.41) | copy-start | bytes 12292
  444.2 17.6 %copy-start.16 = (bf16[8,48,128]{2,1,0:T(8,128)(2,1)S(1)}, bf16[8,48,128]{2,1,0:T(8,128)(2,1)}, u32[]{:S(2)}) copy-start(bf16[8,48,128]{2,1,0:T(8,128)(2,1)} %get-tuple-element.44) | copy-start | bytes 294916
  462.2 2.4 copy-start.15
  464.5 2.8 slice-start.2
  464.5 2.9 slice-start.3
  472.5 5.0 %copy-start.13 = (f32[256,2048]{1,0:T(8,128)S(1)}, f32[256,2048]{1,0:T(8,128)}, u32[]{:S(2)}) copy-start(f32[256,2048]{1,0:T(8,128)} %get-tuple-element.39) | copy-start | bytes 6291460
  (3 other events, 2.2 us)
Sparse Core Ops, SparseCore 0:
  9.6 63.5 all-gather.4
  75.1 70.2 all-gather.2
  229.8 43.8 reduce-scatter.4
  277.4 95.9 reduce-scatter.2

commit v4 on v3

v4 whole, which is shorter than its diff:
```python
import functools

import jax
import jax.numpy as jnp
from jax import lax
from jax.experimental import pallas as pl
from jax.experimental.pallas import tpu as pltpu
from jax.sharding import Mesh
from jax.sharding import PartitionSpec as P

D = 2048
HEADS = 64
HEADDIM = 64
STATE = 128
KERNEL = 4
STRETCH = 256
INNER = 4096
CHANNELS = 4352
EPSILON = 1e-05
HIGH = lax.Precision.HIGHEST
BF16 = jnp.bfloat16
F32 = jnp.float32
GROUP = ("y", "seq")


def mm(a, b):
    return jnp.dot(a.astype(BF16), b.astype(BF16), preferred_element_type=F32)


def mm_last(a, b):
    return lax.dot_general(
        a.astype(BF16), b.astype(BF16), (((1,), (1,)), ((), ())), preferred_element_type=F32
    )


def iota(shape, axis):
    return lax.broadcasted_iota(jnp.int32, shape, axis)


def head_times(raw, bias, a_log):
    pre = raw + bias
    step = jnp.maximum(pre, 0.0) + jnp.log1p(jnp.exp(-jnp.abs(pre)))
    log_decay = step * -jnp.exp(a_log)
    width = raw.shape[1]
    upper = (iota((width, width), 0) <= iota((width, width), 1)).astype(F32)
    running = jnp.dot(log_decay, upper, precision=HIGH, preferred_element_type=F32)
    return pre, step, log_decay, running


def over_channels(values, pair):
    left = values[:, 2 * pair : 2 * pair + 1]
    right = values[:, 2 * pair + 1 : 2 * pair + 2]
    lane = iota((values.shape[0], 2 * HEADDIM), 1)
    return jnp.where(lane < HEADDIM, left, right)


def spread(values):
    pairs = values.shape[1] // 2
    return jnp.concatenate([over_channels(values, i) for i in range(pairs)], axis=1)


def convolved(block, halo, conv_w, conv_b):
    rows = block.shape[0]
    joined = jnp.concatenate([halo, block], axis=0)
    base = halo.shape[0] - KERNEL + 1
    shifted = [joined[base + k : base + k + rows] for k in range(KERNEL)]
    total = conv_b
    for k in range(KERNEL):
        total = total + conv_w[k : k + 1] * shifted[k]
    return total, shifted


MESH = pl.DeviceIdType.MESH


def remote(src, dst, send_sem, recv_sem, device):
    return pltpu.make_async_remote_copy(
        src_ref=src, dst_ref=dst, send_sem=send_sem, recv_sem=recv_sem,
        device_id=device, device_id_type=MESH,
    )


class Place:
    def __init__(self, planes, ny, ns):
        self.planes, self.ny, self.ns, self.group = planes, ny, ns, ny * ns
        self.z, self.y, self.s = lax.axis_index("z"), lax.axis_index("y"), lax.axis_index("seq")
        self.rank = self.y * ns + self.s
        self.up, self.down = (self.z + 1, self.y, self.s), (self.z - 1, self.y, self.s)
        self.has_up, self.has_down = self.z < planes - 1, self.z > 0

    def member(self, rank):
        return (self.z, rank // self.ns, lax.rem(rank, self.ns))

    def peer(self, i):
        return lax.rem(self.rank + i, self.group)

    def far(self):
        chips = self.ns // 2
        x, core = self.s // 2, lax.rem(self.s, 2)
        for dy in range(self.ny):
            for dx in range(chips):
                if dy or dx:
                    yield lax.rem(self.y + dy, self.ny) * self.ns + lax.rem(x + dx, chips) * 2 + core

    def sibling(self, rank):
        return rank + 1 - 2 * lax.rem(rank, 2)

    def greet(self):
        barrier = pltpu.get_barrier_semaphore()
        for i in range(1, self.group):
            pl.semaphore_signal(barrier, inc=1, device_id=self.member(self.peer(i)), device_id_type=MESH)

        @pl.when(self.has_up)
        def _():
            pl.semaphore_signal(barrier, inc=1, device_id=self.up, device_id_type=MESH)

        @pl.when(self.has_down)
        def _():
            pl.semaphore_signal(barrier, inc=1, device_id=self.down, device_id_type=MESH)

        count = self.group - 1 + self.has_up.astype(jnp.int32) + self.has_down.astype(jnp.int32)
        pl.semaphore_wait(barrier, count)


class PlaneGather:
    def __init__(self, at, rows_of, whole, sems):
        self.at, self.rows_of, self.whole = at, rows_of, whole
        self.send, self.recv = sems
        self.square = at.ny == 2 and at.ns == 4
        self.sibling = at.sibling(at.rank)
        self.far = list(at.far())
        if not self.square:
            self.units = [(r, None) for r in self.far]
        else:
            xn, yn, dg = self.far
            self.units = [(xn, 0), (yn, 1), (xn, 1), (yn, 0), (dg, 0), (dg, 1)]

    def count(self):
        return 2 * len(self.units) + 2

    def view(self, rank, half):
        rows = self.rows_of(rank)
        if half is None:
            return self.whole.at[rows]
        size = rows.size // 2
        return self.whole.at[pl.ds(pl.multiple_of(rows.start + half * size, size), size)]

    def copy(self, rank, half, to, n, slot):
        ref = self.view(rank, half)
        return remote(ref, ref, self.send.at[n], self.recv.at[slot], self.at.member(to))

    def slot(self, unit):
        return unit

    def sends(self):
        me = self.at.rank
        if not self.square:
            return [(me, None, r, i) for i, r in enumerate(self.far)]
        xn, yn, _ = self.far
        return [(me, 0, xn, 0), (me, 1, yn, 1), (me, 1, xn, 2), (me, 0, yn, 3)]

    def start(self):
        count = len(self.units)
        self.copy(self.at.rank, None, self.sibling, 0, count).start()
        for n, (rank, half, to, slot) in enumerate(self.sends()):
            self.copy(rank, half, to, 1 + n, slot).start()

    def passed(self, unit):
        count = len(self.units)
        on = [(self.sibling, count + 1 + unit)]
        if self.square and unit == 0:
            on.append((self.far[1], 4))
        if self.square and unit == 1:
            on.append((self.far[0], 5))
        return on

    def first_send(self, unit):
        n = 1 + len(self.sends())
        for before in range(unit):
            n += len(self.passed(before))
        return n

    def arrive(self, unit):
        rank, half = self.units[unit]
        self.copy(rank, half, self.sibling, 0, unit).wait_recv()
        for n, (to, slot) in reversed(list(enumerate(self.passed(unit)))):
            self.copy(rank, half, to, self.first_send(unit) + n, slot).start()

    def rest(self):
        count = len(self.units)
        self.copy(self.sibling, None, self.sibling, 0, count).wait_recv()
        for unit, (rank, half) in enumerate(self.units):
            self.copy(self.at.sibling(rank), half, self.sibling, 0, count + 1 + unit).wait_recv()

    def finish(self):
        self.copy(self.at.rank, None, self.sibling, 0, 0).wait_send()
        for n, (rank, half, to, slot) in enumerate(self.sends()):
            self.copy(rank, half, to, 1 + n, slot).wait_send()
        for unit, (rank, half) in enumerate(self.units):
            for n, (to, slot) in enumerate(self.passed(unit)):
                self.copy(rank, half, to, self.first_send(unit) + n, slot).wait_send()


class Share:
    def __init__(self, planes, group, aligned):
        self.group = group
        self.blocks = planes if aligned else 1
        self.channels = INNER // group
        self.block = self.channels // self.blocks
        self.heads = HEADS // group
        self.small = 2 * STATE // group

    def lanes(self, rank, k, base=0):
        return pl.ds(pl.multiple_of(base + (k * self.group + rank) * self.block, self.block), self.block)

    def channel_rows(self, ref, rank):
        return jnp.concatenate([ref[:, self.lanes(rank, k)] for k in range(self.blocks)], 1)

    def head_column(self, ref, rank):
        each = self.block // HEADDIM
        own = iota((self.heads, HEADS), 0)
        head = (own // each * self.group + rank) * each + lax.rem(own, each)
        return jnp.sum(jnp.where(iota((self.heads, HEADS), 1) == head, ref[...], 0.0), 1, keepdims=True)


def project_kernel(
    planes, ny, ns, cut, share,
    len_ref, tok_ref, cot_ref, w_ref, gain_ref,
    proj_ref, bct_ref, dt_ref, nt_ref, wm_ref, ws_ref, bg_ref, half_ref,
    wmain, wsmall, normed, acc, outb, bcb, turned, pm_ref, ps_ref, grads,
    am_send, am_recv, as_send, as_recv, n_send, n_recv, g_send, g_recv, b_send, b_recv,
    up_send, up_recv, down_send, down_recv, sup_send, sup_recv, sdown_send, sdown_recv, local_sem, turn_sem,
):
    at = Place(planes, ny, ns)
    group, rank, z = at.group, at.rank, at.z
    heads = share.heads
    piece = w_ref.shape[0]
    plane_rows = piece * group
    total, slab = normed.shape[0], 256
    own_rows = tok_ref.shape[0]
    small = bcb.shape[0] // group
    part = plane_rows // cut

    def rows_of(r):
        return pl.ds(pl.multiple_of(z * plane_rows + r * piece, piece), piece)

    def block_rows(p, q):
        return pl.ds(pl.multiple_of(p * plane_rows + q * part, part), part)

    def plane_block(p):
        return pl.ds(pl.multiple_of(p * plane_rows, plane_rows), plane_rows)

    def norm_rows(r):
        return pl.ds(pl.multiple_of(r * own_rows, own_rows), own_rows)

    narrow_t = w_ref[:, 2 * INNER :].T
    filler = jnp.zeros((128 - small - heads, piece), F32)
    each = share.block // HEADDIM
    for r in range(group):
        times = [
            narrow_t[2 * STATE + (k * group + r) * each : 2 * STATE + (k * group + r + 1) * each]
            for k in range(share.blocks)
        ]
        ps_ref[r] = jnp.concatenate([narrow_t[r * small : (r + 1) * small]] + times + [filler], 0).T.astype(BF16)
    for r in range(group):
        for k in range(share.blocks):
            here = pl.ds(k * share.block, share.block)
            pm_ref[r, :, here] = w_ref[:, pl.ds((k * group + r) * share.block, share.block)].astype(BF16)
            here = pl.ds(share.channels + k * share.block, share.block)
            pm_ref[r, :, here] = w_ref[:, pl.ds(INNER + (k * group + r) * share.block, share.block)].astype(BF16)
    at.greet()

    def main_piece(r, i):
        return remote(pm_ref.at[r], wmain.at[rows_of(rank)], am_send.at[i], am_recv.at[rank], at.member(r))

    def small_piece(r, i):
        return remote(ps_ref.at[r], wsmall.at[rows_of(rank)], as_send.at[i], as_recv.at[rank], at.member(r))

    for i in range(1, group):
        small_piece(at.peer(i), i).start()
    for i in range(1, group):
        main_piece(at.peer(i), i).start()
    own_copies = [
        pltpu.make_async_copy(pm_ref.at[rank], wmain.at[rows_of(rank)], local_sem.at[0]),
        pltpu.make_async_copy(ps_ref.at[rank], wsmall.at[rows_of(rank)], local_sem.at[1]),
    ]
    for copy in own_copies:
        copy.start()
    inputs = tok_ref[...].astype(F32)
    rms = lax.rsqrt(jnp.mean(inputs * inputs, 1, keepdims=True) + EPSILON)
    normed[norm_rows(rank), :] = (inputs * rms * gain_ref[...]).astype(BF16)
    norms = PlaneGather(at, norm_rows, normed, (n_send, n_recv))
    norms.start()
    position = at.s * own_rows + iota((own_rows, 1), 0)
    valid = jnp.where(position < len_ref[0], 1.0, 0.0)
    masked = (cot_ref[...].astype(F32) * valid).astype(BF16)
    bg_ref[...] = masked
    grads[norm_rows(rank), :] = masked[:, : D // 2]
    gather_grads = PlaneGather(at, norm_rows, grads, (g_send, g_recv))
    acc[...] = jnp.zeros_like(acc)
    for copy in own_copies:
        copy.wait()

    for i in range(1, group):
        r = at.peer(i)
        remote(ps_ref.at[r], wsmall.at[rows_of(r)], as_send.at[i], as_recv.at[r], at.member(r)).wait_recv()

    def small_up(p, j):
        return remote(wsmall.at[plane_block(p)], wsmall.at[plane_block(p)], sup_send.at[j], sup_recv.at[j], at.up)

    def small_down(p, j):
        return remote(wsmall.at[plane_block(p)], wsmall.at[plane_block(p)], sdown_send.at[j], sdown_recv.at[j], at.down)

    def wide_up(p, q, k):
        return remote(wmain.at[block_rows(p, q)], wmain.at[block_rows(p, q)], up_send.at[k], up_recv.at[k], at.up)

    def wide_down(p, q, k):
        return remote(wmain.at[block_rows(p, q)], wmain.at[block_rows(p, q)], down_send.at[k], down_recv.at[k], at.down)

    def each_way(p, above, fn_up, fn_down):
        @pl.when(at.has_up & jnp.logical_not(above))
        def _():
            fn_up()

        @pl.when(at.has_down & above)
        def _():
            fn_down()

    @pl.when(at.has_up)
    def _():
        small_up(z, 0).start()

    @pl.when(at.has_down)
    def _():
        small_down(z, 0).start()

    ranks_in = group // cut
    for q in range(cut):
        for r in range(q * ranks_in, (q + 1) * ranks_in):
            @pl.when(rank != r)
            def _():
                remote(pm_ref.at[r], wmain.at[rows_of(r)], am_send.at[0], am_recv.at[r], at.member(r)).wait_recv()

        @pl.when(at.has_up)
        def _():
            wide_up(z, q, q).start()

        @pl.when(at.has_down)
        def _():
            wide_down(z, q, q).start()

    def small_step(j, _):
        @pl.when(z + j < planes)
        def _():
            small_down(z + j, j - 1).wait_recv()

            @pl.when(at.has_down)
            def _():
                small_down(z + j, j).start()

        @pl.when(z - j >= 0)
        def _():
            small_up(z - j, j - 1).wait_recv()

            @pl.when(at.has_up)
            def _():
                small_up(z - j, j).start()

        return 0

    lax.fori_loop(1, planes, small_step, 0)

    def plane_in_turn(j):
        return lax.rem(jnp.where(2 * z < planes, z + j, z - j + planes), planes)

    slabs = total // slab

    def product(index):
        j, m = index // slabs, lax.rem(index, slabs)
        p = plane_in_turn(j)
        rows = pl.ds(pl.multiple_of(m * slab, slab), slab)
        lanes = pl.ds(pl.multiple_of(p * plane_rows, 128), plane_rows)
        return rows, acc[rows, :] + jnp.dot(
            normed[rows, lanes], wmain[plane_block(p), :], preferred_element_type=F32
        )

    def narrow(m, _):
        rows = pl.ds(pl.multiple_of(m * slab, slab), slab)
        value = jnp.dot(normed[rows, :], wsmall[...], preferred_element_type=F32).T
        bcb[pl.ds(pl.multiple_of(rank * small, small), small), rows] = value[:small].astype(BF16)
        dt_ref[:, rows] = value[small : small + heads].astype(BF16).astype(F32)
        return 0

    def bc_piece(r, i, owner):
        rows = pl.ds(pl.multiple_of(owner * small, small), small)
        return remote(bcb.at[rows], bcb.at[rows], b_send.at[i], b_recv.at[owner], at.member(r))

    steps = (planes - 1) * cut
    busy = (planes - 2) * cut
    per_step = -(-(planes - 1) * slabs // cut)

    def wide_step(k, _):
        j, q = k // cut + 1, lax.rem(k, cut)

        @pl.when(z + j < planes)
        def _():
            wide_down(z + j, q, k).wait_recv()

            @pl.when(at.has_down)
            def _():
                wide_down(z + j, q, k + cut).start()

        @pl.when(z - j >= 0)
        def _():
            wide_up(z - j, q, k).wait_recv()

            @pl.when(at.has_up)
            def _():
                wide_up(z - j, q, k + cut).start()

        return 0

    units = len(norms.units)
    last = 0
    for i in range(units):
        mark = busy * (5 + 4 * (i // 2)) // 16 if norms.square else cut + i * max(busy - cut, 0) // units
        lax.fori_loop(last, mark, wide_step, 0)
        last = mark
        norms.arrive(i)
        if i == units - 1:
            gather_grads.start()
    lax.fori_loop(last, busy, wide_step, 0)
    norms.rest()
    lax.fori_loop(0, slabs, narrow, 0)
    for i in range(1, group):
        bc_piece(at.peer(i), i, rank).start()

    def turn_copy(m):
        rows = pl.ds(pl.multiple_of(m * slab, slab), slab)
        return pltpu.make_async_copy(turned.at[lax.rem(m, 2)], nt_ref.at[:, rows], turn_sem.at[lax.rem(m, 2)])

    def turn(m):
        @pl.when(m >= 2)
        def _():
            turn_copy(m - 2).wait()

        rows = pl.ds(pl.multiple_of(m * slab, slab), slab)
        turned[lax.rem(m, 2)] = normed[rows, :].T
        turn_copy(m).start()

    ws_copy = pltpu.make_async_copy(wsmall, ws_ref, local_sem.at[1])
    ws_copy.start()

    def busy_step(k, _):
        wide_step(k, 0)

        def one(i, _):
            rows, value = product(jnp.minimum((k - busy) * per_step + i, (planes - 1) * slabs))

            @pl.when((k - busy) * per_step + i < (planes - 1) * slabs)
            def _():
                acc[rows, :] = value

            return 0

        lax.fori_loop(0, per_step, one, 0)

        def other(i, _):
            @pl.when((k - busy) * turns + i < slabs)
            def _():
                turn((k - busy) * turns + i)

            return 0

        lax.fori_loop(0, turns, other, 0)
        return 0

    turns = -(-slabs // cut)
    last = busy
    for i in range(units):
        mark = busy + (steps - busy) * (4 + 2 * (i // 2)) // 8 if norms.square else steps
        lax.fori_loop(last, mark, busy_step, 0)
        last = mark
        gather_grads.arrive(i)
    lax.fori_loop(last, steps, busy_step, 0)
    wm_copy = pltpu.make_async_copy(wmain, wm_ref, local_sem.at[2])
    wm_copy.start()

    def out_copy(m):
        rows = pl.ds(pl.multiple_of(m * slab, slab), slab)
        return pltpu.make_async_copy(outb.at[rows], proj_ref.at[rows], local_sem.at[4 + m])

    def final(m, _):
        rows, value = product((planes - 1) * slabs + m)
        outb[rows, :] = value.astype(BF16)
        out_copy(m).start()
        return 0

    lax.fori_loop(0, slabs, final, 0)

    gather_grads.rest()
    half_copy = pltpu.make_async_copy(grads, half_ref, local_sem.at[0])
    half_copy.start()

    for i in range(1, group):
        r = at.peer(i)
        bc_piece(r, i, r).wait_recv()
    bct_copy = pltpu.make_async_copy(bcb, bct_ref, local_sem.at[3])
    bct_copy.start()
    for i in range(1, group):
        r = at.peer(i)
        main_piece(r, i).wait_send()
        small_piece(r, i).wait_send()
        bc_piece(r, i, rank).wait_send()
    norms.finish()
    gather_grads.finish()
    half_copy.wait()

    def small_sent(j, _):
        @pl.when((z + j < planes) & at.has_down)
        def _():
            small_down(z + j, j).wait_send()

        @pl.when((z - j >= 0) & at.has_up)
        def _():
            small_up(z - j, j).wait_send()

        return 0

    lax.fori_loop(0, planes, small_sent, 0)

    def wide_sent(k, _):
        j, q = k // cut, lax.rem(k, cut)

        @pl.when((z + j < planes) & at.has_down)
        def _():
            wide_down(z + j, q, k).wait_send()

        @pl.when((z - j >= 0) & at.has_up)
        def _():
            wide_up(z - j, q, k).wait_send()

        return 0

    lax.fori_loop(0, planes * cut, wide_sent, 0)
    turn_copy(slabs - 2).wait()
    turn_copy(slabs - 1).wait()
    ws_copy.wait()
    wm_copy.wait()
    bct_copy.wait()
    lax.fori_loop(0, slabs, lambda m, _: (out_copy(m).wait(), 0)[1], 0)


def gather_project(lengths, tokens, cotangent, w_in, norm_gain, planes, ny, ns, share):
    group, width = ny * ns, 2 * share.channels
    rows = w_in.shape[0]
    total = tokens.shape[0] * group
    cut = pieces_per_plane(planes, group)
    units = 6 if (ny, ns) == (2, 4) else group // 2 - 1
    gather = 2 * units + 2
    dma = pltpu.SemaphoreType.DMA
    anywhere = pl.BlockSpec(memory_space=pl.ANY)
    vmem = pl.BlockSpec(memory_space=pltpu.VMEM)
    return pl.pallas_call(
        functools.partial(project_kernel, planes, ny, ns, cut, share),
        in_specs=[pl.BlockSpec(memory_space=pltpu.SMEM)] + [vmem] * 4,
        out_specs=[anywhere, anywhere, vmem, anywhere, anywhere, anywhere, vmem, anywhere],
        out_shape=[
            jax.ShapeDtypeStruct((total, width), BF16),
            jax.ShapeDtypeStruct((2 * STATE, total), BF16),
            jax.ShapeDtypeStruct((share.heads, total), F32),
            jax.ShapeDtypeStruct((D, total), BF16),
            jax.ShapeDtypeStruct((D, width), BF16),
            jax.ShapeDtypeStruct((D, 128), BF16),
            jax.ShapeDtypeStruct(tokens.shape, BF16),
            jax.ShapeDtypeStruct((total, D // 2), BF16),
        ],
        scratch_shapes=[
            pltpu.VMEM((D, width), BF16),
            pltpu.VMEM((D, 128), BF16),
            pltpu.VMEM((total, D), BF16),
            pltpu.VMEM((total, width), F32),
            pltpu.VMEM((total, width), BF16),
            pltpu.VMEM((2 * STATE, total), BF16),
            pltpu.VMEM((2, D, 256), BF16),
            pltpu.VMEM((group, rows, width), BF16),
            pltpu.VMEM((group, rows, 128), BF16),
            pltpu.VMEM((total, D // 2), BF16),
            dma((group,)), dma((group,)), dma((group,)), dma((group,)),
            dma((gather,)), dma((gather,)), dma((gather,)), dma((gather,)), dma((group,)), dma((group,)),
            dma((planes * cut,)), dma((planes * cut,)), dma((planes * cut,)), dma((planes * cut,)),
            dma((planes,)), dma((planes,)), dma((planes,)), dma((planes,)),
            dma((4 + total // 256,)), dma((2,)),
        ],
        compiler_params=pltpu.CompilerParams(
            collective_id=1, has_side_effects=True, vmem_limit_bytes=60 << 20
        ),
        name="gather_project",
    )(lengths, tokens, cotangent, w_in, norm_gain)


def grads_kernel(
    planes, ny, ns, cut,
    nt_ref, dp_ref, dg_ref, wm_ref, ws_ref, dbc_ref, ddt_ref, raw_ref, cw_ref,
    gw_ref, gs_ref, ng_ref, bsum_ref,
    ntb, dp, dg, wmain, dw, passing, dsmall, spassing, smalls, bcs, raw, sib_out, sib_in, far_in, own,
    a_send, a_recv, as_send, as_recv, b_send, b_recv, x_send, x_recv, f_send, f_recv,
    up_send, up_recv, down_send, down_recv, sup_send, sup_recv, sdown_send, sdown_recv, local_sem, nt_sem,
):
    at = Place(planes, ny, ns)
    group, rank, z = at.group, at.rank, at.z
    total, width = dp.shape
    plane_rows = D // planes
    piece, part = plane_rows // group, plane_rows // cut
    block = total // group
    chips = group // 2
    chips_x = ns // 2
    small = bcs.shape[1]
    heads = ddt_ref.shape[0]
    span = total // ny
    rows_small = smalls.shape[0]

    def plane_in_turn(j):
        return lax.rem(jnp.where(2 * z < planes, z + j, z - j + planes), planes)

    def nt_plane(i):
        return plane_in_turn(lax.rem(2 * planes - 1 - i, planes))

    def nt_copy(i):
        rows = pl.ds(pl.multiple_of(nt_plane(i) * plane_rows, plane_rows), plane_rows)
        return pltpu.make_async_copy(nt_ref.at[rows], ntb.at[lax.rem(i, 2)], nt_sem.at[lax.rem(i, 2)])

    nt_copy(0).start()
    dp_copy = pltpu.make_async_copy(dp_ref, dp, local_sem.at[0])
    dp_copy.start()
    nt_copy(1).start()
    wm_copy = pltpu.make_async_copy(wm_ref, wmain, local_sem.at[1])
    wm_copy.start()
    dg_copy = pltpu.make_async_copy(dg_ref, dg, local_sem.at[4])
    dg_copy.start()
    own_small = pl.ds(pl.multiple_of(rank * small, small), small)
    raw_copy = pltpu.make_async_copy(raw_ref.at[own_small], raw, local_sem.at[2])
    raw_copy.start()
    bcs_copy = pltpu.make_async_copy(dbc_ref.at[own_small], bcs.at[rank], local_sem.at[3])
    bcs_copy.start()
    at.greet()

    def bc_piece(r, i, owner):
        rows = pl.ds(pl.multiple_of(r * small, small), small)
        return remote(dbc_ref.at[rows], bcs.at[owner], b_send.at[i], b_recv.at[owner], at.member(r))

    for i in range(1, group):
        bc_piece(at.peer(i), i, rank).start()
    dp_copy.wait()

    half = min(256, plane_rows)

    def weight_plane(i):
        p = nt_plane(i)
        nt_copy(i).wait()

        def one(h, _):
            rows = pl.ds(pl.multiple_of(h * half, half), half)
            there = pl.ds(pl.multiple_of(p * plane_rows + h * half, half), half)
            dw[there, :] = jnp.dot(ntb[lax.rem(i, 2), rows, :], dp[...], preferred_element_type=F32)
            return 0

        lax.fori_loop(0, plane_rows // half, one, 0)
        nt_copy(i + 2).start()

    def narrow_plane(i):
        nt_copy(i).wait()
        dsmall[nt_plane(i)] = mm_last(smalls[...], ntb[lax.rem(i, 2)])

        @pl.when(i + 2 < 2 * planes)
        def _():
            nt_copy(i + 2).start()

    def view(ref, t, q):
        return ref.at[pl.ds(pl.multiple_of(t * plane_rows + q * part, part), part)]

    line = LineSum(at, cut, view, dw, passing, (up_send, up_recv, down_send, down_recv))

    def small_up(t, j):
        return remote(spassing.at[t + 1], spassing.at[t + 1], sup_send.at[j], sup_recv.at[j], at.up)

    def small_down(t, j):
        return remote(spassing.at[t], spassing.at[t], sdown_send.at[j], sdown_recv.at[j], at.down)

    def small_step(j, _):
        t = planes - 1 - j

        @pl.when(t > z)
        def _():
            @pl.when(at.has_down)
            def _():
                small_up(t, j).wait_recv()
                spassing[t + 1] = (dsmall[t] + spassing[t + 1].astype(F32)).astype(BF16)

            @pl.when(jnp.logical_not(at.has_down))
            def _():
                spassing[t + 1] = dsmall[t].astype(BF16)

            small_up(t, j).start()

        @pl.when(j < z)
        def _():
            @pl.when(at.has_up)
            def _():
                small_down(j, j).wait_recv()
                spassing[j] = (dsmall[j] + spassing[j].astype(F32)).astype(BF16)

            @pl.when(jnp.logical_not(at.has_up))
            def _():
                spassing[j] = dsmall[j].astype(BF16)

            small_down(j, j).start()

        return 0

    def normed_part(r):
        rows = pl.ds(pl.multiple_of(r * block, block), block)
        turned = smalls[:, rows].T
        return (
            mm_last(dg[rows, :], wmain[:, :width])
            + mm_last(dp[rows, :], wmain[:, width:])
            + mm_last(turned, ws_ref[:, :rows_small])
        )

    plane = PlaneSum(
        at, normed_part, sib_out, sib_in, far_in, own, (x_send, x_recv, f_send, f_recv)
    )

    def steps(start, stop):
        lax.fori_loop(start, min(stop, line.slots), lambda n, _: (line.step(n), 0)[1], 0)

    def task(n, _):
        line.step(n)
        plane.task(n - early)
        return 0

    early = 0
    for i in range(planes):
        weight_plane(i)
        if planes == 4 and i == 1:
            early = line.skew
            steps(0, early)

    raw_copy.wait()
    bcs_copy.wait()
    for i in range(1, group):
        r = at.peer(i)
        bc_piece(r, i, r).wait_recv()
    dbc = bcs[0].astype(F32)
    for r in range(1, group):
        dbc = dbc + bcs[r].astype(F32)
    values = raw[...].astype(F32)
    place = lax.rem(iota(values.shape, 1), span)
    later = [jnp.where(place >= n, pltpu.roll(values, n, 1), 0.0) if n else values for n in range(KERNEL)]
    conv = cw_ref[:, KERNEL : KERNEL + 1]
    for k in range(KERNEL):
        conv = conv + cw_ref[:, k : k + 1] * later[KERNEL - 1 - k]
    sig = 1.0 / (1.0 + jnp.exp(-conv))
    dconv = dbc * (sig * (1.0 + conv * (1.0 - sig)))
    din = jnp.zeros_like(dconv)
    bsum_ref[...] = jnp.zeros_like(bsum_ref)
    bsum_ref[:, KERNEL : KERNEL + 1] = jnp.sum(dconv, 1, keepdims=True)
    for k in range(KERNEL):
        n = KERNEL - 1 - k
        bsum_ref[:, k : k + 1] = jnp.sum(dconv * later[n], 1, keepdims=True)
        moved = jnp.where(place < span - n, pltpu.roll(dconv, total - n, 1), 0.0) if n else dconv
        din = din + cw_ref[:, k : k + 1] * moved
    filler = jnp.zeros((rows_small - small - heads, total), F32)
    smalls[...] = jnp.concatenate([din, ddt_ref[...].astype(F32), filler], 0).astype(BF16)
    wm_copy.wait()
    dg_copy.wait()

    done = early + 2 * chips
    lax.fori_loop(early, done, task, 0)
    beside = -(-(line.slots - done) // (planes + 1))
    for i in range(planes, 2 * planes):
        narrow_plane(i)
        steps(done, done + beside)
        done = min(done + beside, line.slots)
    lax.fori_loop(0, planes - 1, small_step, 0)
    steps(done, line.slots)

    @pl.when(at.has_down)
    def _():
        small_up(z, planes - 1 - z).wait_recv()

    @pl.when(at.has_up)
    def _():
        small_down(z, z).wait_recv()

    nothing = jnp.zeros((rows_small, plane_rows), F32)
    spassing[z] = (
        dsmall[z]
        + jnp.where(at.has_down, spassing[z + 1].astype(F32), nothing)
        + jnp.where(at.has_up, spassing[z].astype(F32), nothing)
    ).astype(BF16)

    def small_out(r, i, owner):
        lanes = pl.ds(pl.multiple_of(r * piece // 128 * 128, 128), 128)
        return remote(
            spassing.at[z, :, lanes], gs_ref.at[owner], as_send.at[i], as_recv.at[owner], at.member(r)
        )

    own_lanes = pl.ds(pl.multiple_of(rank * piece // 128 * 128, 128), 128)
    small_kept = pltpu.make_async_copy(spassing.at[z, :, own_lanes], gs_ref.at[rank], local_sem.at[2])
    small_kept.start()
    for i in range(1, group):
        small_out(at.peer(i), i, rank).start()

    def piece_rows(r):
        return pl.ds(pl.multiple_of(z * plane_rows + r * piece, piece), piece)

    def wide_out(r, owner):
        return remote(
            passing.at[piece_rows(r)], gw_ref.at[owner], a_send.at[r], a_recv.at[owner], at.member(r)
        )

    wide_kept = pltpu.make_async_copy(passing.at[piece_rows(rank)], gw_ref.at[rank], local_sem.at[3])

    def last_step(q, _):
        view(passing, z, q)[...] = line.total(q).astype(BF16)
        for n in range(group // cut):
            r = q * (group // cut) + n

            @pl.when(r != rank)
            def _():
                wide_out(r, rank).start()

            @pl.when(r == rank)
            def _():
                wide_kept.start()

        return 0

    lax.fori_loop(0, cut, last_step, 0)

    ng_ref[...] = plane.total()

    for i in range(1, group):
        r = at.peer(i)
        bc_piece(r, i, rank).wait_send()
        small_out(r, i, rank).wait_send()
        small_out(r, i, r).wait_recv()
        wide_out(r, rank).wait_send()
        wide_out(r, r).wait_recv()
    small_kept.wait()
    wide_kept.wait()
    plane.finish()
    line.finish()

    def small_sent(j, _):
        @pl.when(planes - 1 - j > z)
        def _():
            small_up(planes - 1 - j, j).wait_send()

        @pl.when(j < z)
        def _():
            small_down(j, j).wait_send()

        return 0

    lax.fori_loop(0, planes - 1, small_sent, 0)


def project_grads(normed_t, proj_grad, gate_grad, w_main, w_small, dbc_t, ddt_t, bc_raw, conv_own, planes, ny, ns):
    total, width = proj_grad.shape
    group = ny * ns
    small, heads = 2 * STATE // group, ddt_t.shape[0]
    rows_small = -(-(small + heads) // 16) * 16
    plane_rows = D // planes
    block = total // group
    chips = group // 2
    cut = 1
    while cut * 2 <= min(group, 32 // planes):
        cut *= 2
    dma = pltpu.SemaphoreType.DMA
    anywhere = pl.BlockSpec(memory_space=pl.ANY)
    vmem = pl.BlockSpec(memory_space=pltpu.VMEM)
    return pl.pallas_call(
        functools.partial(grads_kernel, planes, ny, ns, cut),
        in_specs=[anywhere, anywhere, anywhere, anywhere, vmem, anywhere, vmem, anywhere, vmem],
        out_specs=[anywhere, anywhere, vmem, vmem],
        out_shape=[
            jax.ShapeDtypeStruct((group, plane_rows // group, width), BF16),
            jax.ShapeDtypeStruct((group, rows_small, 128), BF16),
            jax.ShapeDtypeStruct((block, D), F32),
            jax.ShapeDtypeStruct((small, 128), F32),
        ],
        scratch_shapes=[
            pltpu.VMEM((2, plane_rows, total), BF16),
            pltpu.VMEM((total, width), BF16),
            pltpu.VMEM((total, width), BF16),
            pltpu.VMEM((D, 2 * width), BF16),
            pltpu.VMEM((D, width), F32),
            pltpu.VMEM((D + plane_rows, width), BF16),
            pltpu.VMEM((planes, rows_small, plane_rows), F32),
            pltpu.VMEM((planes + 1, rows_small, plane_rows), BF16),
            pltpu.VMEM((rows_small, total), BF16),
            pltpu.VMEM((group, small, total), BF16),
            pltpu.VMEM((small, total), BF16),
            pltpu.VMEM((chips, block, D), BF16),
            pltpu.VMEM((chips, block, D), BF16),
            pltpu.VMEM((chips - 1, block, D), BF16),
            pltpu.VMEM((block, D), F32),
            dma((group,)), dma((group,)), dma((group,)), dma((group,)), dma((group,)), dma((group,)),
            dma((chips,)), dma((chips,)), dma((chips,)), dma((chips,)),
            dma((planes * cut,)), dma((planes * cut,)), dma((planes * cut,)), dma((planes * cut,)),
            dma((planes,)), dma((planes,)), dma((planes,)), dma((planes,)),
            dma((5,)), dma((2,)),
        ],
        compiler_params=pltpu.CompilerParams(
            collective_id=2, has_side_effects=True, vmem_limit_bytes=60 << 20
        ),
        name="project_grads",
    )(normed_t, proj_grad, gate_grad, w_main, w_small, dbc_t, ddt_t, bc_raw, conv_own)


def exchange_kernel(planes, ny, ns, mine_ref, out_ref, along, summed, z_send, z_recv, p_send, p_recv):
    at = Place(planes, ny, ns)
    group, rank, z = at.group, at.rank, at.z
    barrier = pltpu.get_barrier_semaphore()
    for i in range(1, planes):
        pl.semaphore_signal(
            barrier, inc=1, device_id=(lax.rem(z + i, planes), at.y, at.s), device_id_type=MESH
        )
    for i in range(1, group):
        pl.semaphore_signal(barrier, inc=1, device_id=at.member(at.peer(i)), device_id_type=MESH)
    pl.semaphore_wait(barrier, planes + group - 2)

    def over_z(p, i, owner):
        return remote(mine_ref, along.at[owner], z_send.at[i], z_recv.at[owner], (p, at.y, at.s))

    for i in range(1, planes):
        over_z(lax.rem(z + i, planes), i, z).start()
    total = mine_ref[...]
    for i in range(1, planes):
        p = lax.rem(z + i, planes)
        over_z(p, i, p).wait_recv()
        total = total + along[p]
    summed[...] = total

    def over_plane(r, i, owner):
        return remote(summed, out_ref.at[owner], p_send.at[i], p_recv.at[owner], at.member(r))

    for i in range(1, group):
        over_plane(at.peer(i), i, rank).start()
    out_ref[rank] = total
    for i in range(1, group):
        r = at.peer(i)
        over_plane(r, i, r).wait_recv()
        over_plane(r, i, rank).wait_send()
    for i in range(1, planes):
        over_z(lax.rem(z + i, planes), i, z).wait_send()


def exchange(mine, planes, ny, ns):
    group = ny * ns
    dma = pltpu.SemaphoreType.DMA
    vmem = pl.BlockSpec(memory_space=pltpu.VMEM)
    return pl.pallas_call(
        functools.partial(exchange_kernel, planes, ny, ns),
        in_specs=[vmem],
        out_specs=vmem,
        out_shape=jax.ShapeDtypeStruct((group,) + mine.shape, F32),
        scratch_shapes=[
            pltpu.VMEM((planes,) + mine.shape, F32),
            pltpu.VMEM(mine.shape, F32),
            dma((planes,)), dma((planes,)), dma((group,)), dma((group,)),
        ],
        compiler_params=pltpu.CompilerParams(collective_id=3, has_side_effects=True),
        name="exchange",
    )(mine)


class LineSum:
    def __init__(self, at, cut, view, part, passing, sems, base=0, skew=4):
        self.skew = skew
        self.at, self.cut, self.view, self.part, self.passing = at, cut, view, part, passing
        self.up_send, self.up_recv, self.down_send, self.down_recv = sems
        self.steps = (at.planes - 1) * cut
        self.slots = self.steps + (at.planes - 1) * skew
        self.base = base

    def up(self, t, q, k):
        ref = self.view(self.passing, t + 1, q)
        return remote(ref, ref, self.up_send.at[self.base + k], self.up_recv.at[self.base + k], self.at.up)

    def down(self, t, q, k):
        ref = self.view(self.passing, t, q)
        return remote(ref, ref, self.down_send.at[self.base + k], self.down_recv.at[self.base + k], self.at.down)

    def step(self, n):
        at, planes = self.at, self.at.planes
        k = n - at.z * self.skew
        q = lax.rem(k, self.cut)
        t = planes - 1 - k // self.cut

        @pl.when((k >= 0) & (t > at.z))
        def _():
            here, mine = self.view(self.passing, t + 1, q), self.view(self.part, t, q)

            @pl.when(at.has_down)
            def _():
                self.up(t, q, k).wait_recv()
                here[...] = (mine[...].astype(F32) + here[...].astype(F32)).astype(BF16)

            @pl.when(jnp.logical_not(at.has_down))
            def _():
                here[...] = mine[...].astype(BF16)

            self.up(t, q, k).start()

        m = n - (planes - 1 - at.z) * self.skew
        p = lax.rem(m, self.cut)
        j = m // self.cut

        @pl.when((m >= 0) & (j < at.z))
        def _():
            here, mine = self.view(self.passing, j, p), self.view(self.part, j, p)

            @pl.when(at.has_up)
            def _():
                self.down(j, p, m).wait_recv()
                here[...] = (mine[...].astype(F32) + here[...].astype(F32)).astype(BF16)

            @pl.when(jnp.logical_not(at.has_up))
            def _():
                here[...] = mine[...].astype(BF16)

            self.down(j, p, m).start()

    def total(self, q):
        at, planes = self.at, self.at.planes

        @pl.when(at.has_down)
        def _():
            self.up(at.z, q, (planes - 1 - at.z) * self.cut + q).wait_recv()

        @pl.when(at.has_up)
        def _():
            self.down(at.z, q, at.z * self.cut + q).wait_recv()

        value = self.view(self.part, at.z, q)[...].astype(F32)
        nothing = jnp.zeros_like(value)
        below = self.view(self.passing, at.z + 1, q)[...].astype(F32)
        above = self.view(self.passing, at.z, q)[...].astype(F32)
        return value + jnp.where(at.has_down, below, nothing) + jnp.where(at.has_up, above, nothing)

    def finish(self):
        def sent(k, _):
            j, q = k // self.cut, lax.rem(k, self.cut)

            @pl.when(self.at.planes - 1 - j > self.at.z)
            def _():
                self.up(self.at.planes - 1 - j, q, k).wait_send()

            @pl.when(j < self.at.z)
            def _():
                self.down(j, q, k).wait_send()

            return 0

        lax.fori_loop(0, self.steps, sent, 0)


class PlaneSum:
    def __init__(self, at, part, sib_out, sib_in, far_in, own, sems):
        self.at, self.part = at, part
        self.sib_out, self.sib_in, self.far_in, self.own = sib_out, sib_in, far_in, own
        self.x_send, self.x_recv, self.f_send, self.f_recv = sems
        self.chips = at.group // 2
        self.sibling = at.sibling(at.rank)

    def far_rank(self, i):
        at = self.at
        chips_x = at.ns // 2
        x, core = at.s // 2, lax.rem(at.s, 2)
        y = lax.rem(at.y + i // chips_x, at.ny)
        return y * at.ns + lax.rem(x + lax.rem(i, chips_x), chips_x) * 2 + core

    def to_sibling(self, i):
        return remote(
            self.sib_out.at[i], self.sib_in.at[i], self.x_send.at[i], self.x_recv.at[i],
            self.at.member(self.sibling),
        )

    def to_far(self, i):
        return remote(
            self.sib_in.at[i], self.far_in.at[i - 1], self.f_send.at[i], self.f_recv.at[i],
            self.at.member(self.far_rank(i)),
        )

    def first(self, n):
        i = lax.rem(n + 1, self.chips)
        self.sib_out[i] = self.part(self.at.sibling(self.far_rank(i))).astype(BF16)
        self.to_sibling(i).start()

    def second(self, n):
        i = lax.rem(n + 1, self.chips)
        value = self.part(self.far_rank(i))
        self.to_sibling(i).wait_recv()
        value = value + self.sib_in[i].astype(F32)

        @pl.when(i > 0)
        def _():
            self.sib_in[i] = value.astype(BF16)
            self.to_far(i).start()

        @pl.when(i == 0)
        def _():
            self.own[...] = value

    def task(self, n):
        @pl.when(n < self.chips)
        def _():
            self.first(n)

        @pl.when((n >= self.chips) & (n < 2 * self.chips))
        def _():
            self.second(n - self.chips)

    def total(self):
        value = self.own[...]
        for i in range(1, self.chips):
            self.to_far(i).wait_recv()
            value = value + self.far_in[i - 1].astype(F32)
        return value

    def finish(self):
        for i in range(self.chips):
            self.to_sibling(i).wait_send()
            if i:
                self.to_far(i).wait_send()


def blocked(start, size):
    return pl.ds(pl.multiple_of(start * size, size), size)


def mix_forward_kernel(
    planes, ny, ns, cut, relayed, share,
    proj_ref, raw_ref, dt_ref, wout_ref, bg_ref, half_ref,
    convw_ref, convb_ref, gate_gain_ref, dtb_ref, al_ref, sk_ref,
    states_ref, bc_ref, bct_ref, own_ref, dy_ref, mixed_ref, gate_ref, gsum_ref, grad_ref,
    proj, wout, grad, other, scanned, mixed_grad, state, halo, halo_bc, states, dy, mixed, gate_grad, sums,
    up_send, up_recv, down_send, down_recv, s_send, s_recv, g_send, g_recv, load_sem, state_sem, out_sem, own_sem,
):
    at = Place(planes, ny, ns)
    group, rank, z = at.group, at.rank, at.z
    total = proj.shape[0]
    channels = proj.shape[1] // 2
    rows = STRETCH
    count = total // rows
    steps = count // ny

    proj_copy = pltpu.make_async_copy(proj_ref, proj, load_sem.at[0])
    proj_copy.start()
    half_copy = pltpu.make_async_copy(half_ref, grad, load_sem.at[1])
    half_copy.start()
    own_rows = bg_ref.shape[0]

    def norm_rows(r):
        return blocked(r, own_rows)

    block = wout.shape[0] // planes if relayed else wout.shape[0]
    if relayed:
        wout[blocked(z, block), :] = wout_ref[...].astype(BF16)
    else:
        wout[...] = wout_ref[...].astype(BF16)
    other[norm_rows(rank), :] = bg_ref[:, D // 2 :]
    at.greet()
    gather = PlaneGather(at, norm_rows, other, (g_send, g_recv))
    part = block // cut

    def view(p, q):
        return wout.at[pl.ds(pl.multiple_of(p * block + q * part, part), part)]

    def up(p, q, k):
        return remote(view(p, q), view(p, q), up_send.at[k], up_recv.at[k], at.up)

    def down(p, q, k):
        return remote(view(p, q), view(p, q), down_send.at[k], down_recv.at[k], at.down)

    if relayed:

        def first(q, _):
            @pl.when(at.has_up)
            def _():
                up(z, q, q).start()

            @pl.when(at.has_down)
            def _():
                down(z, q, q).start()

            return 0

        lax.fori_loop(0, cut, first, 0)
    gather.start()

    def relay(k, _):
        j, q = k // cut + 1, lax.rem(k, cut)

        @pl.when(z + j < planes)
        def _():
            down(z + j, q, k).wait_recv()

            @pl.when(at.has_down)
            def _():
                down(z + j, q, k + cut).start()

        @pl.when(z - j >= 0)
        def _():
            up(z - j, q, k).wait_recv()

            @pl.when(at.has_up)
            def _():
                up(z - j, q, k + cut).start()

        return 0

    gain = share.channel_rows(gate_gain_ref, rank)
    conv_wx = share.channel_rows(convw_ref, rank)
    conv_bx = share.channel_rows(convb_ref, rank)
    conv_wbc = convw_ref[:, INNER:]
    conv_bbc = convb_ref[:, INNER:]
    bias = share.head_column(dtb_ref, rank)
    a_log = share.head_column(al_ref, rank)
    skip = spread(share.head_column(sk_ref, rank).T)
    relays = (planes - 1) * cut if relayed else 0
    per_chunk = min(2, relays // count)
    proj_copy.wait()
    causal = iota((rows, rows), 0) >= iota((rows, rows), 1)
    lane = iota((rows, 2 * HEADDIM), 1)

    def state_copy(i):
        return pltpu.make_async_copy(states.at[lax.rem(i, 2)], states_ref.at[i], state_sem.at[lax.rem(i, 2)])

    def chunk(i, _):
        here = blocked(i, rows)

        @pl.when(lax.rem(i, steps) == 0)
        def _():
            state[...] = jnp.zeros_like(state)
            halo[...] = jnp.zeros_like(halo)
            halo_bc[...] = jnp.zeros_like(halo_bc)

        raw_bc = raw_ref[:, here].astype(F32).T
        conv_bc, _ = convolved(raw_bc, halo_bc[...], conv_wbc, conv_bbc)
        halo_bc[...] = raw_bc[rows - 8 :]
        active = conv_bc / (1.0 + jnp.exp(-conv_bc))
        bc = active.astype(BF16)
        bc_ref[here, :] = bc
        bct_ref[:, here] = active.T.astype(BF16)
        b_t = bct_ref[:STATE, here]
        c = bc[:, STATE:]
        raw = proj[here, channels:].astype(F32)
        conv, _ = convolved(raw, halo[...], conv_wx, conv_bx)
        halo[...] = raw[rows - 8 :]
        xs = conv / (1.0 + jnp.exp(-conv))
        _, step_t, _, run_t = head_times(dt_ref[:, here], bias, a_log)
        run = run_t.T
        xdt = xs * spread(step_t.T)
        products = jnp.where(causal, mm(c, b_t), 0.0)
        entering = state[...]

        @pl.when(i >= 2)
        def _():
            state_copy(i - 2).wait()

        states[lax.rem(i, 2)] = entering
        state_copy(i).start()
        inward = mm(c, entering) * spread(jnp.exp(run))
        skipped = skip * xs
        for pair in range(channels // 128):
            cols = slice(pair * 128, pair * 128 + 128)
            piece = xdt[:, cols]
            value = inward[:, cols] + skipped[:, cols]
            for side in range(2):
                h = 2 * pair + side
                decay = jnp.exp(jnp.minimum(run[:, h : h + 1] - run_t[h : h + 1], 0.0))
                own = (lane < HEADDIM) if side == 0 else (lane >= HEADDIM)
                value = value + mm(products * decay, jnp.where(own, piece, 0.0))
            scanned[here, cols] = value
        last = run[rows - 1 :]
        to_end = spread(jnp.exp(last - run))
        state[...] = entering * spread(jnp.exp(last)) + mm(b_t, xdt * to_end)
        lax.fori_loop(i * per_chunk, (i + 1) * per_chunk, relay, 0)
        return 0

    units = len(gather.units)
    last = 0
    for i in range(units):
        mark = min(count, 3 + 2 * (i // 2)) if gather.square else count * (i + 1) // units
        lax.fori_loop(last, mark, chunk, 0)
        last = mark
        gather.arrive(i)
    lax.fori_loop(last, count, chunk, 0)
    lax.fori_loop(count * per_chunk, relays, relay, 0)
    gather.rest()
    half_copy.wait()
    grad_copies = [
        pltpu.make_async_copy(grad, grad_ref.at[:, pl.ds(0, D // 2)], load_sem.at[1]),
        pltpu.make_async_copy(other, grad_ref.at[:, pl.ds(D // 2, D // 2)], load_sem.at[2]),
    ]
    for copy in grad_copies:
        copy.start()
    own_copy = pltpu.make_async_copy(wout, own_ref, own_sem.at[0])
    own_copy.start()

    def gated(m):
        here = blocked(m, rows)
        gate = proj[here, :channels].astype(F32)
        sig = 1.0 / (1.0 + jnp.exp(-gate))
        return here, gate, sig, scanned[here, :]

    def sum_slab(m, _):
        here, gate, sig, inner = gated(m)
        value = mm_last(grad[here, :], wout[:, : D // 2]) + mm_last(other[here, :], wout[:, D // 2 :])
        mixed_grad[here, :] = value
        product = inner * (gate * sig)
        squares = jnp.sum(product * product, 1, keepdims=True)
        along = jnp.sum(value * gain * product, 1, keepdims=True)
        sums[rank, pl.ds(m, 1), :] = squares.T
        sums[rank, pl.ds(count + m, 1), :] = along.T
        return 0

    lax.fori_loop(0, count, sum_slab, 0)

    def sums_piece(r, i, owner):
        return remote(sums.at[owner], sums.at[owner], s_send.at[i], s_recv.at[owner], at.member(r))

    for i in range(1, group):
        sums_piece(at.peer(i), i, rank).start()
    for i in range(1, group):
        r = at.peer(i)
        sums_piece(r, i, r).wait_recv()
    whole = sums[0]
    for r in range(1, group):
        whole = whole + sums[r]
    whole = whole * (1.0 / INNER)
    scale = lax.rsqrt(whole + EPSILON)
    gsum_ref[...] = jnp.zeros_like(gsum_ref)

    def out_copies(m):
        here = blocked(m, rows)
        return [
            pltpu.make_async_copy(dy.at[lax.rem(m, 2)], dy_ref.at[here], out_sem.at[0, lax.rem(m, 2)]),
            pltpu.make_async_copy(mixed.at[lax.rem(m, 2)], mixed_ref.at[here], out_sem.at[1, lax.rem(m, 2)]),
            pltpu.make_async_copy(gate_grad.at[lax.rem(m, 2)], gate_ref.at[here], out_sem.at[2, lax.rem(m, 2)]),
        ]

    ids = iota(whole.shape, 0)

    def grad_slab(m, _):
        here, gate, sig, inner = gated(m)
        r = jnp.sum(jnp.where(ids == m, scale, 0.0), 0, keepdims=True).T
        mean = jnp.sum(jnp.where(ids == count + m, whole, 0.0), 0, keepdims=True).T
        silu = gate * sig
        product = inner * silu
        value = mixed_grad[here, :]
        normal = product * r
        product_grad = r * (value * gain) - product * (r * r * r * mean)
        gsum_ref[0:1] += jnp.sum(value * normal, 0, keepdims=True)

        @pl.when(m >= 2)
        def _():
            for copy in out_copies(m - 2):
                copy.wait()

        dy[lax.rem(m, 2)] = product_grad * silu
        mixed[lax.rem(m, 2)] = (normal * gain).astype(BF16)
        gate_grad[lax.rem(m, 2)] = (product_grad * inner * (sig * (1.0 + gate * (1.0 - sig)))).astype(BF16)
        for copy in out_copies(m):
            copy.start()
        return 0

    lax.fori_loop(0, count, grad_slab, 0)

    for n in range(2):
        state_copy(count - 2 + n).wait()
        for copy in out_copies(count - 2 + n):
            copy.wait()
    own_copy.wait()
    for copy in grad_copies:
        copy.wait()
    gather.finish()
    for i in range(1, group):
        sums_piece(at.peer(i), i, rank).wait_send()
    if relayed:

        def sent(k, _):
            j, q = k // cut, lax.rem(k, cut)

            @pl.when((z + j < planes) & at.has_down)
            def _():
                down(z + j, q, k).wait_send()

            @pl.when((z - j >= 0) & at.has_up)
            def _():
                up(z - j, q, k).wait_send()

            return 0

        lax.fori_loop(0, planes * cut, sent, 0)


def pieces_per_plane(planes, group):
    cut = 1
    while cut * 2 <= min(group, 32 // planes):
        cut *= 2
    return cut


def mix_forward(projected, bc_raw, dt_t, w_out, branch_grad, grad_half, vectors, planes, ny, ns, relayed, share):
    total, channels = projected.shape[0], projected.shape[1] // 2
    group = ny * ns
    count = total // STRETCH
    cut = pieces_per_plane(planes, group)
    units = 6 if (ny, ns) == (2, 4) else group // 2 - 1
    gather = 2 * units + 2
    dma = pltpu.SemaphoreType.DMA
    anywhere = pl.BlockSpec(memory_space=pl.ANY)
    vmem = pl.BlockSpec(memory_space=pltpu.VMEM)
    line = dma((planes * cut,))
    return pl.pallas_call(
        functools.partial(mix_forward_kernel, planes, ny, ns, cut, relayed, share),
        in_specs=[anywhere] + [vmem] * 4 + [anywhere] + [vmem] * 6,
        out_specs=[anywhere, vmem, vmem, anywhere, anywhere, anywhere, anywhere, vmem, anywhere],
        out_shape=[
            jax.ShapeDtypeStruct((count, STATE, channels), F32),
            jax.ShapeDtypeStruct((total, 2 * STATE), BF16),
            jax.ShapeDtypeStruct((2 * STATE, total), BF16),
            jax.ShapeDtypeStruct((channels, D), BF16),
            jax.ShapeDtypeStruct((total, channels), F32),
            jax.ShapeDtypeStruct((total, channels), BF16),
            jax.ShapeDtypeStruct((total, channels), BF16),
            jax.ShapeDtypeStruct((8, channels), F32),
            jax.ShapeDtypeStruct((total, D), BF16),
        ],
        scratch_shapes=[
            pltpu.VMEM((total, 2 * channels), BF16),
            pltpu.VMEM((channels, D), BF16),
            pltpu.VMEM((total, D // 2), BF16),
            pltpu.VMEM((total, D // 2), BF16),
            pltpu.VMEM((total, channels), F32),
            pltpu.VMEM((total, channels), F32),
            pltpu.VMEM((STATE, channels), F32),
            pltpu.VMEM((8, channels), F32),
            pltpu.VMEM((8, 2 * STATE), F32),
            pltpu.VMEM((2, STATE, channels), F32),
            pltpu.VMEM((2, STRETCH, channels), F32),
            pltpu.VMEM((2, STRETCH, channels), BF16),
            pltpu.VMEM((2, STRETCH, channels), BF16),
            pltpu.VMEM((group, 2 * count, STRETCH), F32),
            line, line, line, line,
            dma((group,)), dma((group,)), dma((gather,)), dma((gather,)),
            dma((3,)), dma((2,)), dma((3, 2)), dma((1,)),
        ],
        compiler_params=pltpu.CompilerParams(
            collective_id=4, has_side_effects=True, vmem_limit_bytes=60 << 20
        ),
        name="mix_forward",
    )(projected, bc_raw, dt_t, w_out, branch_grad, grad_half, *vectors)


def mix_backward_kernel(
    planes, ny, ns, cut, relayed, share,
    proj_ref, bc_ref, bct_ref, dt_ref, dy_ref, states_ref, mixed_ref, gate_ref, own_ref, grad_ref, nt_ref,
    convw_ref, convb_ref, dtb_ref, al_ref, sk_ref,
    dx_ref, dbc_ref, ddt_ref, sums_ref, heads_ref, wout_ref, branch_ref, wgate_ref,
    xin, dyb, stb, mixed, mixed_t, gate_grad, own, tile, ntb, dwo, passing_o, dwg, passing_g,
    sib_out, sib_in, far_in, kept_sum, dxb, lam, rim,
    up_send, up_recv, down_send, down_recv, x_send, x_recv, f_send, f_recv, a_send, a_recv,
    load_sem, tile_sem, nt_sem, in_sem, dx_sem,
):
    at = Place(planes, ny, ns)
    group, rank, z = at.group, at.rank, at.z
    total, channels = mixed.shape
    heads = channels // HEADDIM
    rows = STRETCH
    count = total // rows
    steps = count // ny
    plane_rows = D // planes
    piece, part = plane_rows // group, plane_rows // cut
    block = total // group
    width = tile.shape[2]
    tiles = D // width
    span = channels // planes

    mixed_copy = pltpu.make_async_copy(mixed_ref, mixed, load_sem.at[0])
    mixed_copy.start()

    def tile_copy(q):
        return pltpu.make_async_copy(
            grad_ref.at[:, blocked(q, width)], tile.at[lax.rem(q, 2)], tile_sem.at[lax.rem(q, 2)]
        )

    def plane_in_turn(j):
        return lax.rem(jnp.where(2 * z < planes, z + j, z - j + planes), planes)

    def nt_plane(i):
        return plane_in_turn(planes - 1 - i)

    def nt_copy(i):
        return pltpu.make_async_copy(
            nt_ref.at[blocked(nt_plane(i), plane_rows)], ntb.at[lax.rem(i, 2)], nt_sem.at[lax.rem(i, 2)]
        )

    tile_copy(0).start()
    tile_copy(1).start()
    gate_copy = pltpu.make_async_copy(gate_ref, gate_grad, load_sem.at[1])
    gate_copy.start()
    nt_copy(0).start()
    nt_copy(1).start()
    own_copy = pltpu.make_async_copy(own_ref, own, load_sem.at[2])
    own_copy.start()
    x_copy = pltpu.make_async_copy(proj_ref.at[:, pl.ds(channels, channels)], xin, load_sem.at[3])
    x_copy.start()

    def chunk_of(n):
        return n // steps * steps + steps - 1 - lax.rem(n, steps)

    def in_copies(n):
        i, slot = chunk_of(n), lax.rem(n, 2)
        return [
            pltpu.make_async_copy(dy_ref.at[blocked(i, rows)], dyb.at[slot], in_sem.at[0, slot]),
            pltpu.make_async_copy(states_ref.at[i], stb.at[slot], in_sem.at[1, slot]),
        ]

    for n in range(2):
        for copy in in_copies(n):
            copy.start()
    at.greet()

    def view_out(ref, t, q):
        return ref.at[blocked(t, span), blocked(q, width)]

    sems = (up_send, up_recv, down_send, down_recv)
    line_out = LineSum(at, tiles, view_out, dwo, passing_o, sems)

    def view_gate(ref, t, q):
        return ref.at[pl.ds(pl.multiple_of(t * plane_rows + q * part, part), part)]

    line_gate = LineSum(at, cut, view_gate, dwg, passing_g, sems, line_out.steps if relayed else 0)
    mixed_copy.wait()

    def turn(m, _):
        here = blocked(m, rows)
        mixed_t[:, here] = mixed[here, :].T
        return 0

    lax.fori_loop(0, count, turn, 0)

    def out_tile(q, _):
        tile_copy(q).wait()
        value = jnp.dot(mixed_t[...], tile[lax.rem(q, 2)], preferred_element_type=F32)
        dwo[:, blocked(q, width)] = value.astype(BF16)

        @pl.when(q + 2 < tiles)
        def _():
            tile_copy(q + 2).start()

        if relayed:
            line_out.step(q)
        return 0

    lax.fori_loop(0, tiles, out_tile, 0)
    if not relayed:
        kept_out = pltpu.make_async_copy(dwo, wout_ref, load_sem.at[0])
        kept_out.start()

    own_copy.wait()

    def branch_part(r):
        return jnp.dot(mixed[blocked(r, block), :], own[...], preferred_element_type=F32)

    plane = PlaneSum(
        at, branch_part, sib_out, sib_in, far_in, kept_sum, (x_send, x_recv, f_send, f_recv)
    )

    gate_copy.wait()
    half = min(256, plane_rows)

    def weight_plane(i, _):
        nt_copy(i).wait()

        def one(h, _):
            there = pl.ds(pl.multiple_of(nt_plane(i) * plane_rows + h * half, half), half)
            dwg[there, :] = jnp.dot(
                ntb[lax.rem(i, 2), blocked(h, half), :], gate_grad[...], preferred_element_type=F32
            ).astype(BF16)
            return 0

        lax.fori_loop(0, plane_rows // half, one, 0)

        @pl.when(i + 2 < planes)
        def _():
            nt_copy(i + 2).start()

        out_steps(tiles + i * beside, tiles + (i + 1) * beside)
        return 0

    def out_steps(start, stop):
        if relayed:
            lax.fori_loop(start, jnp.minimum(stop, line_out.slots), lambda n, _: (line_out.step(n), 0)[1], 0)

    def gate_steps(start, stop):
        lax.fori_loop(start, jnp.minimum(stop, line_gate.slots), lambda n, _: (line_gate.step(n), 0)[1], 0)

    beside = -(-tiles // planes)
    lax.fori_loop(0, planes, weight_plane, 0)
    out_done = tiles + planes * beside

    def task(n, _):
        plane.task(n)
        out_steps(out_done + n, out_done + n + 1)
        gate_steps(n, n + 1)
        return 0

    tasks = 2 * plane.chips
    lax.fori_loop(0, tasks, task, 0)
    out_done = out_done + tasks
    per_out = -(-max(line_out.slots - out_done, 0) // count)
    per_gate = -(-(line_gate.slots - tasks) // count)

    sums_ref[...] = jnp.zeros_like(sums_ref)
    heads_ref[...] = jnp.zeros_like(heads_ref)
    x_copy.wait()
    conv_wx = share.channel_rows(convw_ref, rank)
    conv_bx = share.channel_rows(convb_ref, rank)
    bias = share.head_column(dtb_ref, rank)
    a_log = share.head_column(al_ref, rank)
    skip = spread(share.head_column(sk_ref, rank).T)
    causal = iota((rows, rows), 0) >= iota((rows, rows), 1)
    lower = causal.astype(F32)
    lane = iota((rows, 2 * HEADDIM), 1)
    wide = iota((rows, heads), 1)
    member = (iota((heads, channels), 1) // HEADDIM == iota((heads, channels), 0)).astype(F32)

    def per_head(values):
        return lax.dot_general(
            member, values, (((1,), (1,)), ((), ())), precision=HIGH, preferred_element_type=F32
        )

    def dx_copy(n):
        return pltpu.make_async_copy(
            dxb.at[lax.rem(n, 2)], dx_ref.at[blocked(chunk_of(n), rows)], dx_sem.at[lax.rem(n, 2)]
        )

    def chunk(n, _):
        i, slot = chunk_of(n), lax.rem(n, 2)
        here = blocked(i, rows)
        start = lax.rem(n, steps) == 0

        @pl.when(start)
        def _():
            lam[...] = jnp.zeros_like(lam)
            rim[...] = jnp.zeros_like(rim)

        for copy in in_copies(n):
            copy.wait()
        dy = dyb[slot]
        entering = stb[slot]
        raw = xin[here, :].astype(F32)
        ahead = pl.ds(pl.multiple_of(jnp.maximum(i * rows - 16, 0), 16), 16)
        before = jnp.where(lax.rem(i, steps) == 0, 0.0, xin[ahead, :].astype(F32))
        conv, shifted = convolved(raw, before, conv_wx, conv_bx)
        sig_c = 1.0 / (1.0 + jnp.exp(-conv))
        xs = conv * sig_c
        sums_ref[6:7] += jnp.sum(dy * xs, 0, keepdims=True)
        pre, step_t, decay_t, run_t = head_times(dt_ref[:, here], bias, a_log)
        run = run_t.T
        step = spread(step_t.T)
        xdt = xs * step
        b = bc_ref[here, :STATE]
        c = bc_ref[here, STATE:]
        b_t = bct_ref[:STATE, here]
        c_t = bct_ref[STATE:, here]
        products = jnp.where(causal, mm(c, b_t), 0.0)
        leaving = lam[...]
        last = run[rows - 1 :]
        to_end = spread(jnp.exp(last - run))
        dye = dy * spread(jnp.exp(run))
        xend = xdt * to_end
        inward = dye * mm(c, entering)
        outward_grad = mm(b, leaving) * to_end
        outward = outward_grad * xdt
        dc_t = mm_last(entering, dye)
        db_t = mm_last(leaving, xend)
        kept = leaving * spread(jnp.exp(last))
        lam[...] = kept + mm(c_t, dye)

        dy_t = dy.T.astype(BF16)
        dproducts = jnp.zeros((rows, rows), F32)
        row_sums = jnp.zeros((rows, heads), F32)
        col_sums = []
        dxdt_t = []
        for h in range(heads):
            cols = slice((h // 2) * 128, (h // 2) * 128 + 128)
            mine = (lane < HEADDIM) if h % 2 == 0 else (lane >= HEADDIM)
            decay = jnp.exp(jnp.minimum(run[:, h : h + 1] - run_t[h : h + 1], 0.0))
            weights = products * decay
            dweights = mm_last(dy[:, cols], jnp.where(mine, xdt[:, cols], 0.0))
            dproducts = dproducts + dweights * decay
            shares = dweights * weights
            row_sums = jnp.where(wide == h, jnp.sum(shares, 1, keepdims=True), row_sums)
            col_sums.append(jnp.sum(shares, 0, keepdims=True))
            dxdt_t.append(mm(dy_t[h * HEADDIM : (h + 1) * HEADDIM], weights))
        dproducts = jnp.where(causal, dproducts, 0.0)
        dbc_ref[:STATE, here] = (db_t + mm(c_t, dproducts)).astype(BF16)
        dbc_ref[STATE:, here] = (dc_t + mm_last(b_t, dproducts)).astype(BF16)
        dxdt = jnp.concatenate(dxdt_t, 0).T + outward_grad

        out_t = per_head(outward)
        run_grad = per_head(inward) - out_t + row_sums.T - jnp.concatenate(col_sums, 0)
        at_end = jnp.sum(out_t, 1, keepdims=True) + jnp.sum(per_head(kept * entering), 1, keepdims=True)
        decay_grad = at_end + jnp.dot(run_grad, lower, precision=HIGH, preferred_element_type=F32)
        step_grad = per_head(dxdt * xs) - jnp.exp(a_log) * decay_grad
        dt_grad = step_grad / (1.0 + jnp.exp(-pre))
        ddt_ref[:, here] = dt_grad.astype(BF16)
        heads_ref[:, 0:1] += jnp.sum(dt_grad, 1, keepdims=True)
        heads_ref[:, 1:2] += jnp.sum(decay_grad * decay_t, 1, keepdims=True)

        dx = dxdt * step + skip * dy
        dconv = dx * (sig_c * (1.0 + conv * (1.0 - sig_c)))
        sums_ref[4:5] += jnp.sum(dconv, 0, keepdims=True)
        for k in range(KERNEL):
            sums_ref[k : k + 1] += jnp.sum(dconv * shifted[k], 0, keepdims=True)
        joined = jnp.concatenate([dconv, rim[...]], 0)
        rim[...] = dconv[:8]
        dx_in = conv_wx[KERNEL - 1 : KERNEL] * dconv
        for k in range(KERNEL - 1):
            later = KERNEL - 1 - k
            dx_in = dx_in + conv_wx[k : k + 1] * joined[later : later + rows]

        @pl.when(n >= 2)
        def _():
            dx_copy(n - 2).wait()

        dxb[slot] = dx_in.astype(BF16)
        dx_copy(n).start()

        @pl.when(n + 2 < count)
        def _():
            for copy in in_copies(n + 2):
                copy.start()

        out_steps(out_done + n * per_out, out_done + (n + 1) * per_out)
        gate_steps(tasks + n * per_gate, tasks + (n + 1) * per_gate)
        return 0

    lax.fori_loop(0, count, chunk, 0)

    if relayed:

        def out_total(q, _):
            wout_ref[:, blocked(q, width)] = line_out.total(q)
            return 0

        lax.fori_loop(0, tiles, out_total, 0)

    def piece_rows(r):
        return pl.ds(pl.multiple_of(z * plane_rows + r * piece, piece), piece)

    def wide_out(r, owner):
        return remote(
            passing_g.at[piece_rows(r)], wgate_ref.at[owner], a_send.at[r], a_recv.at[owner], at.member(r)
        )

    wide_kept = pltpu.make_async_copy(passing_g.at[piece_rows(rank)], wgate_ref.at[rank], load_sem.at[1])

    def last_step(q, _):
        view_gate(passing_g, z, q)[...] = line_gate.total(q).astype(BF16)
        for m in range(group // cut):
            r = q * (group // cut) + m

            @pl.when(r != rank)
            def _():
                wide_out(r, rank).start()

            @pl.when(r == rank)
            def _():
                wide_kept.start()

        return 0

    lax.fori_loop(0, cut, last_step, 0)
    branch_ref[...] = plane.total()

    for n in range(2):
        dx_copy(count - 2 + n).wait()
    for i in range(1, group):
        r = at.peer(i)
        wide_out(r, rank).wait_send()
        wide_out(r, r).wait_recv()
    wide_kept.wait()
    plane.finish()
    if relayed:
        line_out.finish()
    else:
        kept_out.wait()
    line_gate.finish()


def mix_backward(
    projected, bc, bc_t, dt_t, dy, states, mixed, gate_grad, own, grad_all, normed_t, vectors, planes, ny, ns, relayed, share
):
    total, channels = projected.shape[0], projected.shape[1] // 2
    heads = channels // HEADDIM
    group = ny * ns
    cut = pieces_per_plane(planes, group)
    width = D // 8
    span = channels // planes
    plane_rows = D // planes
    block = total // group
    chips = group // 2
    dma = pltpu.SemaphoreType.DMA
    anywhere = pl.BlockSpec(memory_space=pl.ANY)
    vmem = pl.BlockSpec(memory_space=pltpu.VMEM)
    line = dma(((planes - 1) * (8 + cut),))
    slots = channels + span if relayed else 16
    return pl.pallas_call(
        functools.partial(mix_backward_kernel, planes, ny, ns, cut, relayed, share),
        in_specs=[anywhere, vmem, vmem, vmem] + [anywhere] * 7 + [vmem] * 5,
        out_specs=[anywhere, vmem, vmem, vmem, vmem, vmem if relayed else anywhere, vmem, anywhere],
        out_shape=[
            jax.ShapeDtypeStruct((total, channels), BF16),
            jax.ShapeDtypeStruct((2 * STATE, total), BF16),
            jax.ShapeDtypeStruct((heads, total), BF16),
            jax.ShapeDtypeStruct((8, channels), F32),
            jax.ShapeDtypeStruct((heads, 128), F32),
            jax.ShapeDtypeStruct((span, D), F32) if relayed else jax.ShapeDtypeStruct((channels, D), BF16),
            jax.ShapeDtypeStruct((block, D), F32),
            jax.ShapeDtypeStruct((group, plane_rows // group, channels), BF16),
        ],
        scratch_shapes=[
            pltpu.VMEM((total, channels), BF16),
            pltpu.VMEM((2, STRETCH, channels), F32),
            pltpu.VMEM((2, STATE, channels), F32),
            pltpu.VMEM((total, channels), BF16),
            pltpu.VMEM((channels, total), BF16),
            pltpu.VMEM((total, channels), BF16),
            pltpu.VMEM((channels, D), BF16),
            pltpu.VMEM((2, total, width), BF16),
            pltpu.VMEM((2, plane_rows, total), BF16),
            pltpu.VMEM((channels, D), BF16),
            pltpu.VMEM((slots, D), BF16),
            pltpu.VMEM((D, channels), BF16),
            pltpu.VMEM((D + plane_rows, channels), BF16),
            pltpu.VMEM((chips, block, D), BF16),
            pltpu.VMEM((chips, block, D), BF16),
            pltpu.VMEM((chips - 1, block, D), BF16),
            pltpu.VMEM((block, D), F32),
            pltpu.VMEM((2, STRETCH, channels), BF16),
            pltpu.VMEM((STATE, channels), F32),
            pltpu.VMEM((8, channels), F32),
            line, line, line, line,
            dma((chips,)), dma((chips,)), dma((chips,)), dma((chips,)), dma((group,)), dma((group,)),
            dma((4,)), dma((2,)), dma((2,)), dma((2, 2)), dma((2,)),
        ],
        compiler_params=pltpu.CompilerParams(
            collective_id=5, has_side_effects=True, vmem_limit_bytes=62 << 20
        ),
        name="mix_backward",
    )(projected, bc, bc_t, dt_t, dy, states, mixed, gate_grad, own, grad_all, normed_t, *vectors)


class Layout:
    def __init__(self, planes, group, rows_out):
        self.planes, self.group = planes, group
        self.aligned = rows_out % HEADDIM == 0
        self.blocks = planes if self.aligned else 1
        self.block = INNER // group // self.blocks
        self.heads = HEADS // group
        self.channels = INNER // group
        self.small = 2 * STATE // group

    def pieces(self, values, unit):
        rows = values.shape[0]
        parts = values.reshape(rows, self.blocks, self.group, self.block // HEADDIM * unit)
        return parts.transpose(0, 2, 1, 3).reshape(rows, self.group, -1)

    def joined(self, values, unit):
        rows = values.shape[0]
        parts = values.reshape(rows, self.group, self.blocks, self.block // HEADDIM * unit)
        return parts.transpose(0, 2, 1, 3).reshape(rows, -1)

    def columns(self, w):
        gate = self.pieces(w[:, :INNER], HEADDIM)
        x = self.pieces(w[:, INNER : 2 * INNER], HEADDIM)
        bc = w[:, 2 * INNER : INNER + CHANNELS].reshape(w.shape[0], self.group, self.small)
        dt = self.pieces(w[:, INNER + CHANNELS :], 1)
        return jnp.concatenate([gate, x, bc, dt], 2)

    def uncolumns(self, g):
        c, s = self.channels, self.small
        gate = self.joined(g[:, :, :c], HEADDIM)
        x = self.joined(g[:, :, c : 2 * c], HEADDIM)
        bc = g[:, :, 2 * c : 2 * c + s].reshape(g.shape[0], -1)
        dt = self.joined(g[:, :, 2 * c + s :], 1)
        return jnp.concatenate([gate, x, bc, dt], 1)


def body(
    tokens, cotangent, lengths, norm_gain, w_in, conv_w, conv_b, dt_bias, a_log, skip_scale, gate_gain, w_out,
):
    row_count = tokens.shape[1]
    planes, group = lax.axis_size("z"), lax.axis_size("y") * lax.axis_size("seq")
    seqs = lax.axis_size("y")
    ny, ns = lax.axis_size("y"), lax.axis_size("seq")
    rank = lax.axis_index("y") * lax.axis_size("seq") + lax.axis_index("seq")
    lay = Layout(planes, group, w_out.shape[0])
    channels, small = lay.channels, lay.small
    inputs = tokens.reshape(row_count, D).astype(F32)
    position = lax.axis_index("seq") * row_count + jnp.arange(row_count, dtype=jnp.int32)
    valid_mask = (position < lengths[0]).astype(F32)[:, None]
    rms = lax.rsqrt(jnp.mean(inputs * inputs, -1, keepdims=True) + EPSILON)
    masked_cot = cotangent.reshape(row_count, D).astype(F32) * valid_mask

    share = Share(planes, group, lay.aligned)
    projected, bc_raw, dt_t, normed_t, w_main, w_small, branch_grad, grad_half = gather_project(
        lengths, tokens.reshape(row_count, D), cotangent.reshape(row_count, D), w_in, norm_gain[None],
        planes, ny, ns, share,
    )
    out_rows = w_out
    if not lay.aligned:
        out_all = lax.all_gather(w_out.astype(BF16), ("z",) + GROUP, axis=0, tiled=True)
        out_rows = lax.dynamic_slice_in_dim(out_all, rank * channels, channels, 0)
    taps, offsets = conv_w.T, conv_b[None]
    head_vectors = (dt_bias[None], a_log[None], skip_scale[None])
    states, bc, bc_t, out_own, dy, mixed, gate_grad, gain_sums, grad_all = mix_forward(
        projected, bc_raw, dt_t, out_rows, branch_grad, grad_half,
        (taps, offsets, gate_gain[None]) + head_vectors, planes, ny, ns, lay.aligned, share,
    )
    x_grad, dbc_t, ddt_t, sums_x, sums_h, out_part, branch, gate_pieces = mix_backward(
        projected, bc, bc_t, dt_t, dy, states, mixed, gate_grad, out_own, grad_all, normed_t,
        (taps, offsets) + head_vectors, planes, ny, ns, lay.aligned, share,
    )
    output = (valid_mask * (inputs + branch)).astype(BF16)
    if lay.aligned:
        grad_w_out = out_part
    else:
        placed = lax.dynamic_update_slice_in_dim(jnp.zeros((INNER, D), BF16), out_part, rank * channels, 0)
        grad_w_out = lax.psum_scatter(placed, ("z",) + GROUP, scatter_dimension=0, tiled=True).astype(F32)

    own_bc = lambda v: lax.dynamic_slice_in_dim(v[INNER:], rank * small, small, 0)
    conv_own = jnp.pad(
        jnp.concatenate([own_bc(conv_w), own_bc(conv_b[:, None])], 1), ((0, 0), (0, 128 - KERNEL - 1))
    )
    in_pieces, in_small, normed_grad, bc_sums = project_grads(
        normed_t, x_grad, gate_grad, w_main, w_small, dbc_t, ddt_t, bc_raw, conv_own, planes, ny, ns
    )
    lanes = in_small.reshape(group, in_small.shape[1], -1, w_in.shape[0])
    mine = lax.dynamic_index_in_dim(lanes, lax.rem(rank, lanes.shape[2]), 2, keepdims=False)
    mine = mine[:, : small + lay.heads].transpose(2, 0, 1)
    grad_w_in = lay.uncolumns(jnp.concatenate([gate_pieces.transpose(1, 0, 2), in_pieces.transpose(1, 0, 2), mine], 2)).astype(F32)
    g = normed_grad * norm_gain
    input_grad = masked_cot + rms * g - inputs * (rms ** 3 * jnp.mean(g * inputs, -1, keepdims=True))
    norm_gain_grad = jnp.sum(normed_grad * inputs * rms, 0)

    own_sums = jnp.concatenate(
        [
            sums_x[: KERNEL + 1].reshape(-1),
            gain_sums[0],
            jnp.sum(sums_x[KERNEL + 2].reshape(-1, HEADDIM), 1),
            sums_h[:, 0],
            sums_h[:, 1],
            bc_sums[:, :KERNEL].T.reshape(-1),
            bc_sums[:, KERNEL],
        ]
    )
    count = own_sums.shape[0]
    flat = jnp.concatenate([norm_gain_grad, own_sums, jnp.zeros((-(count + D) % 1024,), F32)])
    by_rank = exchange(flat.reshape(-1, 128), planes, ny, ns).reshape(group, -1)
    grad_norm_gain = jnp.sum(by_rank[:, :D], 0)
    by_rank = by_rank[:, D : D + count]
    at = 0

    def take(size):
        nonlocal at
        at += size
        return by_rank[:, at - size : at]

    taken_x = take((KERNEL + 2) * channels).reshape(group, KERNEL + 2, channels).transpose(1, 0, 2)
    full_x = lay.joined(taken_x, HEADDIM)
    grad_skip, grad_bias, grad_a = (
        lay.joined(take(lay.heads)[None], 1)[0] for _ in range(3)
    )
    conv_w_bc = take(KERNEL * small).reshape(group, KERNEL, small).transpose(1, 0, 2).reshape(KERNEL, -1)
    conv_b_bc = take(small).reshape(-1)
    grad_conv_w = jnp.concatenate([full_x[:KERNEL], conv_w_bc], 1).T
    grad_conv_b = jnp.concatenate([full_x[KERNEL], conv_b_bc])
    return (
        output.reshape(tokens.shape),
        input_grad.reshape(1, row_count, D),
        grad_norm_gain,
        grad_w_in,
        grad_conv_w,
        grad_conv_b,
        grad_bias,
        grad_a,
        grad_skip,
        full_x[KERNEL + 1],
        grad_w_out,
    )


def solution(mesh):
    dp, seq = mesh.shape["dp"], mesh.shape["seq"]
    inner_mesh = Mesh(mesh.devices.reshape(dp // 2, 2, seq), ("z", "y", "seq"))
    placed = P(("z", "y"), "seq", None)
    rows = P(("z", "y", "seq"), None)
    in_specs = (placed, placed, P(("z", "y")), P(), rows, P(), P(), P(), P(), P(), P(), rows)
    out_specs = (placed, placed, P(), rows, P(), P(), P(), P(), P(), P(), rows)
    return jax.shard_map(body, mesh=inner_mesh, in_specs=in_specs, out_specs=out_specs, check_vma=False)
```

time: 492 us -> 398 us (0.81)
  matrix products: 34.1 us -> 0 us
  local copies, waits for them, and re-layouts: 45.1 us -> 13.8 us
  blocking collectives: 20.4 us -> 0 us
  between operations: 15.4 us -> 1.79 us
  Pallas kernels: 353 us -> 365 us
  other arithmetic: 20.2 us -> 11.8 us
    pallas_call x3, Pallas kernels: 189 us -> 251 us  [the longest x1 103 us: gather_project(): pl.pallas_call(functools.partial(project_kernel, planes, ny, ns, cut, sha...]
    pallas_call x1, Pallas kernels: 152 us -> 103 us  [project_grads(): pl.pallas_call(functools.partial(grads_kernel, planes, ny, ns, cut), in_s...]
    dot_general x3 -> x0, matrix products: 34.1 us -> none  [the longest x1 14.4 us: body(): lax.dot_general(grad_all, out_own, (((1,), (1,)), ((), ())), preferred_el...]
    psum x1 -> x0, blocking collectives: 20.4 us -> none  [body(): lax.psum(jnp.stack([jnp.sum(product * product, 1), jnp.sum(mixed_grad * g...]
    unnamed x67 -> x30, local copies, waits for them, and re-layouts: 13.1 us -> 2.28 us
    slice x11 -> x1, local copies, waits for them, and re-layouts: 10.3 us -> 0.72 us  [body(): gain_sums[0]]
    convert_element_type x6 -> x1, other arithmetic: 10.9 us -> 2.85 us  [body(): lay.uncolumns(jnp.concatenate([gate_pieces.transpose(1, 0, 2), in_pieces....]
    reshape x10 -> x1, local copies, waits for them, and re-layouts: 6.78 us -> 0.01 us  [body(): sums_x[:KERNEL + 1].reshape(-1)]
  transfers between devices with their start and end apart: 4 -> 0, of which waited for: 0 -> 0; matrix products, arithmetic and copies ran while one was open for 13% -> 0% of each run, Pallas kernels for 72% -> 0%
where the time goes in v4:
time: 398 us; the launch traced here: 393 us
  Pallas kernels  365 us (92%)
  local copies, waits for them, and re-layouts  13.8 us (3%)
  other arithmetic  11.8 us (3%)
    pallas_call x1, Pallas kernels, gather_project(): pl.pallas_call(functools.partial(project_kernel, planes, ny, ns, cut, sha...  103 us
    pallas_call x1, Pallas kernels, project_grads(): pl.pallas_call(functools.partial(grads_kernel, planes, ny, ns, cut), in_s...  103 us
    pallas_call x1, Pallas kernels, mix_backward(): pl.pallas_call(functools.partial(mix_backward_kernel, planes, ny, ns, cut...  86.5 us
    pallas_call x1, Pallas kernels, mix_forward(): pl.pallas_call(functools.partial(mix_forward_kernel, planes, ny, ns, cut,...  61.7 us
    pallas_call x1, Pallas kernels, exchange(): pl.pallas_call(functools.partial(exchange_kernel, planes, ny, ns), in_spe...  11 us

profile of v4, /device:TPU:1, one launch (start us, length us, event | category | flops | bytes accessed | tf_op | source)
XLA Modules:
  0.0 392.7 jit_solution(14474754060081298670)
XLA Ops:
  1.3 103.1 %gather_project.1 = (bf16[2048,1024]{1,0:T(8,128)(2,1)}, bf16[256,2048]{1,0:T(8,128)(2,1)}, f32[8,2048]{1,0:T(8,128)}, bf16[2048,2048]{1,0:T(8,128)(2,1)}, bf16[...) custom-call(s32[1]{0:T(128)} %copy.87.len_ref, ...), custom_call_target="tpu_custom_call" | custom-call | tf_op jit(solution)/shard_map/gather_project/pallas_call | solution.py:564
  104.4 0.6 broadcast_in_dim.27.convb_ref
  105.1 61.7 %mix_forward.1 = (f32[8,128,512]{2,1,0:T(8,128)}, bf16[2048,256]{1,0:T(8,128)(2,1)}, bf16[256,2048]{1,0:T(8,128)(2,1)}, bf16[512,2048]{1,0:T(8,128)(2,1)}, f32[2...) custom-call(bf16[2048,1024]{1,0:T(8,128)(2,1)} %get-tuple-element.40, ...), custom_call_target="tpu_custom_call" | custom-call | tf_op jit(solution)/shard_map/mix_forward/pallas_call | solution.py:1430
  166.8 86.5 %mix_backward.1 = (bf16[2048,512]{1,0:T(8,128)(2,1)}, bf16[256,2048]{1,0:T(8,128)(2,1)}, bf16[8,2048]{1,0:T(8,128)(2,1)}, f32[8,512]{1,0:T(8,128)}, f32[8,128]{1...) custom-call(bf16[2048,1024]{1,0:T(8,128)(2,1)} %get-tuple-element.40.proj_ref, ...), custom_call_target="tpu_custom_call" | custom-call | tf_op jit(solution)/shard_map/mix_backward/pallas_call | solution.py:1827
  253.3 0.7 slice.79
  254.3 0.6 pad.4.cw_ref
  254.9 102.9 %project_grads.1 = (bf16[8,64,512]{2,1,0:T(8,128)(2,1)}, bf16[8,48,128]{2,1,0:T(8,128)(2,1)}, f32[256,2048]{1,0:T(8,128)}, f32[32,128]{1,0:T(8,128)}) custom-call(bf16[2048,2048]{1,0:T(8,128)(2,1)} %get-tuple-element.53.nt_ref, bf16[2048,512]{1,0:T(8,128)(2,1)} %get-tuple-element.55.dp_ref, bf16[2048,512]{1,0:T(8,128)(2,1)} %get-tuple-element.50.gate_ref.dg_ref, ...), custom_call_target="tpu_custom_call" | custom-call | tf_op jit(solution)/shard_map/project_grads/pallas_call | solution.py:884
  357.8 0.7 slice_bitcast_fusion.4
  358.7 0.3 fusion.2
  359.0 2.2 fusion.7
  361.2 0.2 slice_reduce_fusion.1
  361.6 0.2 slice_reduce_fusion.2
  361.8 0.7 slice.82
  362.5 0.7 concatenate.16
  363.2 11.0 %exchange.1 = f32[8,48,128]{2,1,0:T(8,128)} custom-call(f32[48,128]{1,0:T(8,128)} %bitcast.115), custom_call_target="tpu_custom_call" | custom-call | tf_op jit(solution)/shard_map/exchange/pallas_call | solution.py:965
  374.2 1.0 copy.82
  375.2 0.6 slice_bitcast_fusion.2
  376.0 0.6 pad_maximum_fusion
  376.9 0.6 maximum_bitcast_fusion
  377.6 0.1 reshape.132
  377.7 0.6 copy.55
  378.3 0.1 reshape.130
  378.5 0.6 copy.54
  379.1 1.4 copy_bitcast_fusion
  380.6 0.2 constant_dynamic-slice_fusion
  381.1 2.9 maximum_convert_fusion
  384.2 0.6 squeeze_reshape.10
  385.0 0.6 squeeze_reshape.11
  385.8 0.6 squeeze_reshape.9
  386.4 0.6 slice_reduce_fusion
  387.0 4.5 %fusion.5 = (f32[1,256,2048]{2,1,0:T(8,128)}, bf16[1,256,2048]{2,1,0:T(8,128)(2,1)}) fusion(f32[256,2048]{1,0:T(8,128)S(1)} %copy-done.1, f32[256]{0:T(256)S(1)} %fusion.9, f32[2048]{0:T(1024)S(1)} %copy-done.6, f32[256]{0:T(256)S(1)} %add_rsqrt_fusion, f32[256]{0:T(256)S(1)} %compare_convert_fusion, bf16[1,256,2048]{2,1,0:T(8,128)(2,1)} %param.13, ...), kind=kLoop, calls=%fused_computation.10 | loop fusion | flops 5767168 | bytes 9448448 | tf_op jit(solution)/shard_map/reshape | solution.py:2000
  391.5 1.0 copy.88
  (63 shorter events, 2.1 us)
Async XLA Ops:
  1.3 103.1 %copy-start.8 = (f32[4352]{0:T(1024)S(1)}, f32[4352]{0:T(1024)}, u32[]{:S(2)}) copy-start(f32[4352]{0:T(1024)} %param.18) | copy-start | bytes 52228
  166.8 87.3 %slice-start = ((f32[4352]{0:T(1024)}), f32[256]{0:T(256)S(1)}, s32[]{:S(2)}) async-start(f32[4352]{0:T(1024)} %param.18), calls=%async_computation | async-start | bytes 2048 | tf_op jit(solution)/shard_map/slice | solution.py:1951
  254.9 103.8 %copy-start = (bf16[1,256,2048]{2,1,0:T(8,128)(2,1)S(1)}, bf16[1,256,2048]{2,1,0:T(8,128)(2,1)}, u32[]{:S(2)}) copy-start(bf16[1,256,2048]{2,1,0:T(8,128)(2,1)} %param.12) | copy-start | bytes 3145732
  254.9 104.1 %copy-start.6 = (f32[2048]{0:T(1024)S(1)}, f32[2048]{0:T(1024)}, u32[]{:S(2)}) copy-start(f32[2048]{0:T(1024)} %param.15) | copy-start | bytes 24580
  358.7 2.5 copy-start.7
  358.7 2.7 copy-start.9
  358.7 2.9 copy-start.10
  359.0 18.6 %copy-start.4 = (bf16[8,64,512]{2,1,0:T(8,128)(2,1)S(1)}, bf16[8,64,512]{2,1,0:T(8,128)(2,1)}, u32[]{:S(2)}) copy-start(bf16[8,64,512]{2,1,0:T(8,128)(2,1)} %get-tuple-element.66) | copy-start | bytes 1572868
  361.2 17.1 %copy-start.3 = (bf16[8,64,512]{2,1,0:T(8,128)(2,1)S(1)}, bf16[8,64,512]{2,1,0:T(8,128)(2,1)}, u32[]{:S(2)}) copy-start(bf16[8,64,512]{2,1,0:T(8,128)(2,1)} %get-tuple-element.65) | copy-start | bytes 1572868
  378.3 2.1 copy-start.5
  380.8 6.2 %copy-start.1 = (f32[256,2048]{1,0:T(8,128)S(1)}, f32[256,2048]{1,0:T(8,128)}, u32[]{:S(2)}) copy-start(f32[256,2048]{1,0:T(8,128)} %get-tuple-element.60) | copy-start | bytes 6291460
  387.0 4.5 %copy-start.2 = (f32[128,2048]{1,0:T(8,128)S(1)}, f32[128,2048]{1,0:T(8,128)}, u32[]{:S(2)}) copy-start(f32[128,2048]{1,0:T(8,128)} %get-tuple-element.103) | copy-start | bytes 3145732
